TPU v7x, 32 devices: a whole 2x2x4 slice. The times are simulated.
32 devices in a mesh: rows: 8 (over z, x), depth: 4 (over y, core).
Axes of the slice: x: 2, y: 2, z: 4, core: 2. Of those that a mesh axis runs over, the one named last changes fastest.
Arguments:
- block_input: bfloat16 [4096, 768], P(('rows', 'depth')), may hold values from -6 to 6
- history: bfloat16 [4, 4096, 768], P('depth', 'rows'), may hold values from -6 to 6
- cotangent: bfloat16 [4096, 768], P(('rows', 'depth')), may hold values from -6 to 6
- token_mask: int32 [4096], P(('rows', 'depth')), may hold values from 0 to 1, as said below
- qkv_weight: bfloat16 [768, 2304], P(('rows', 'depth')), may hold values from -0.21875 to 0.21875
- out_weight: bfloat16 [768, 768], P(('rows', 'depth')), may hold values from -1.5 to 1.5
- up_weight: bfloat16 [768, 3072], P(('rows', 'depth')), may hold values from -0.21875 to 0.21875
- down_weight: bfloat16 [3072, 768], P(('rows', 'depth')), may hold values from -0.109375 to 0.109375
- norm_params: float32 [4, 768], P(None, ('rows', 'depth')), may hold values from -1 to 1
- depth_weights: float32 [5], replicated, may hold values from 0.2 to 1
Outputs:
- output: bfloat16 [4096, 768], P(('rows', 'depth'))
- input_grad: bfloat16 [4096, 768], P(('rows', 'depth'))
- history_grad: bfloat16 [4, 4096, 768], P('depth', 'rows')
- qkv_gradient: float32 [768, 2304], P(('rows', 'depth'))
- out_gradient: float32 [768, 768], P(('rows', 'depth'))
- up_gradient: float32 [768, 3072], P(('rows', 'depth'))
- down_gradient: float32 [3072, 768], P(('rows', 'depth'))
- norm_gradient: float32 [4, 768], P(None, ('rows', 'depth'))
- depth_gradient: float32 [5], replicated
Inputs may be any that keep to these rules, and one draw needn't show every extreme that they name: `token_mask`: the first row is 1.
All inputs are finite; a program needn't handle non-finite values.
Results may differ from a plain program's by a relative error of at most 0.035.
Values may be sent and summed in bfloat16 or wider, within the bound.
A program may use at most 192 MiB of HBM per device.

v0:
```python
import jax
import jax.numpy as jnp
from jax import lax
from jax.sharding import PartitionSpec as P

HEADS = 12
HD = 64


def norm_rows(value, gain, shift):
    center = value - jnp.mean(value, axis=-1, keepdims=True)
    spread = jnp.mean(center * center, axis=-1, keepdims=True)
    return center * lax.rsqrt(spread + 1e-05) * (1.0 + gain) + shift


def rotate(value, place, sign):
    half = value.shape[-1] // 2
    freq = 10000.0 ** (-jnp.arange(half, dtype=jnp.float32) / half)
    angle = place.astype(jnp.float32)[:, None] * freq[None, :]
    cosine = jnp.cos(angle)[:, None, :]
    sine = jnp.sin(angle)[:, None, :] * sign
    first = value[..., :half]
    second = value[..., half:]
    return jnp.concatenate(
        [first * cosine - second * sine, second * cosine + first * sine], axis=-1
    )


def block_scores(query, key_block, start, query_place, scale):
    block_len = key_block.shape[0]
    scores = (
        jnp.einsum("qhd,khd->hqk", query, key_block, preferred_element_type=jnp.float32) * scale
    )
    key_place = start + jnp.arange(block_len, dtype=jnp.int32)
    allowed = query_place[:, None] >= key_place[None, :]
    return (scores, allowed)


def local(
    block_input,
    history,
    cotangent,
    token_mask,
    qkv_weight,
    out_weight,
    up_weight,
    down_weight,
    norm_params,
    depth_weights,
):
    rows_tok, width = block_input.shape
    depth_count = lax.axis_size("depth")
    device_count = lax.axis_size("rows") * depth_count
    place_depth = lax.axis_index("depth")
    heads = HEADS
    head_size = HD
    scale = head_size ** (-0.5)
    seq_len = rows_tok * depth_count
    slot_count = history.shape[0]
    hist_total = slot_count * depth_count
    wide_qkv, wide_out, wide_up, wide_down, wide_norms = (
        lax.all_gather(qkv_weight, ("rows", "depth"), axis=0, tiled=True),
        lax.all_gather(out_weight, ("rows", "depth"), axis=0, tiled=True),
        lax.all_gather(up_weight, ("rows", "depth"), axis=0, tiled=True),
        lax.all_gather(down_weight, ("rows", "depth"), axis=0, tiled=True),
        lax.all_gather(
            norm_params.astype(jnp.bfloat16), ("rows", "depth"), axis=1, tiled=True
        ).astype(norm_params.dtype),
    )
    total = lax.psum(jnp.sum(token_mask), ("rows", "depth")).astype(jnp.float32)
    loss_scale = rows_tok * device_count / total
    float_input = block_input.astype(jnp.float32)
    place = place_depth * rows_tok + jnp.arange(rows_tok, dtype=jnp.int32)
    first = norm_rows(float_input, wide_norms[0], wide_norms[1]).astype(jnp.bfloat16)
    projected = jnp.dot(first, wide_qkv, preferred_element_type=jnp.float32)
    query = rotate(projected[:, :width].reshape(rows_tok, heads, head_size), place, 1.0).astype(
        jnp.bfloat16
    )
    keys = rotate(projected[:, width : 2 * width].reshape(rows_tok, heads, head_size), place, 1.0)
    keys = keys.astype(jnp.bfloat16).reshape(rows_tok, width)
    values = projected[:, 2 * width :].astype(jnp.bfloat16)
    all_keys, all_values = (
        lax.all_gather(keys, "depth", axis=0, tiled=True),
        lax.all_gather(values, "depth", axis=0, tiled=True),
    )
    block_len = min(512, seq_len)
    block_count = seq_len // block_len
    key_blocks = all_keys.reshape(block_count, block_len, heads, head_size)
    value_blocks = all_values.reshape(block_count, block_len, heads, head_size)
    starts = jnp.arange(block_count, dtype=jnp.int32) * block_len

    def peak_step(carry, item):
        peak, weight_sum = carry
        key_block, value_block, start = item
        scores, allowed = block_scores(query, key_block, start, place, scale)
        scores = jnp.where(allowed[None], scores, -1e30)
        new_peak = jnp.maximum(peak, jnp.max(scores, axis=-1))
        weight_sum = weight_sum * jnp.exp(peak - new_peak) + jnp.sum(
            jnp.exp(scores - new_peak[..., None]), axis=-1
        )
        return ((new_peak, weight_sum), None)

    start_carry = (
        jnp.full((heads, rows_tok), -1e30, jnp.float32),
        jnp.zeros((heads, rows_tok), jnp.float32),
    )
    (peak, weight_sum), _ = lax.scan(peak_step, start_carry, (key_blocks, value_blocks, starts))
    log_total = peak + jnp.log(weight_sum)

    def value_step(running, item):
        key_block, value_block, start = item
        scores, allowed = block_scores(query, key_block, start, place, scale)
        probs = jnp.where(allowed[None], jnp.exp(scores - log_total[..., None]), 0.0)
        running = running + jnp.einsum(
            "hqk,khd->qhd",
            probs.astype(jnp.bfloat16),
            value_block,
            preferred_element_type=jnp.float32,
        )
        return (running, None)

    running, _ = lax.scan(
        value_step,
        jnp.zeros((rows_tok, heads, head_size), jnp.float32),
        (key_blocks, value_blocks, starts),
    )
    mixed = running.reshape(rows_tok, width)
    mixed_low = mixed.astype(jnp.bfloat16)
    middle = float_input + jnp.dot(mixed_low, wide_out, preferred_element_type=jnp.float32)
    second = norm_rows(middle, wide_norms[2], wide_norms[3]).astype(jnp.bfloat16)
    upper = jnp.dot(second, wide_up, preferred_element_type=jnp.float32)
    active = jax.nn.gelu(upper).astype(jnp.bfloat16)
    block_out = middle + jnp.dot(active, wide_down, preferred_element_type=jnp.float32)
    own_alpha = lax.dynamic_slice_in_dim(depth_weights, place_depth * slot_count, slot_count)
    partial_mix = jnp.sum(own_alpha[:, None, None] * history.astype(jnp.float32), axis=0)
    mixture = lax.psum_scatter(
        partial_mix.astype(jnp.bfloat16), "depth", scatter_dimension=0, tiled=True
    ).astype(jnp.float32)
    output = (mixture + depth_weights[hist_total] * block_out).astype(jnp.bfloat16)
    grad_out = token_mask.astype(jnp.float32)[:, None] * cotangent.astype(jnp.float32) * loss_scale
    last_term = jnp.sum(grad_out * block_out)
    index_all = jnp.arange(hist_total + 1, dtype=jnp.int32)
    grad_rows = lax.all_gather(grad_out.astype(jnp.bfloat16), "depth", axis=0, tiled=True).astype(
        grad_out.dtype
    )
    history_grad = (own_alpha[:, None, None] * grad_rows[None]).astype(jnp.bfloat16)
    hist_terms = jnp.sum(history.astype(jnp.float32) * grad_rows[None], axis=(1, 2))
    own_index = place_depth * slot_count + jnp.arange(slot_count, dtype=jnp.int32)
    alpha_terms = jnp.sum(
        jnp.where(index_all[None, :] == own_index[:, None], hist_terms[:, None], 0.0), axis=0
    )
    alpha_terms = alpha_terms + jnp.where(index_all == hist_total, last_term, 0.0)
    depth_gradient = lax.psum(alpha_terms, ("rows", "depth"))
    wide_qkv, wide_out, wide_up, wide_down, wide_norms = (
        lax.all_gather(qkv_weight, ("rows", "depth"), axis=0, tiled=True),
        lax.all_gather(out_weight, ("rows", "depth"), axis=0, tiled=True),
        lax.all_gather(up_weight, ("rows", "depth"), axis=0, tiled=True),
        lax.all_gather(down_weight, ("rows", "depth"), axis=0, tiled=True),
        lax.all_gather(
            norm_params.astype(jnp.bfloat16), ("rows", "depth"), axis=1, tiled=True
        ).astype(norm_params.dtype),
    )
    block_grad = depth_weights[hist_total] * grad_out
    lower_grad = block_grad.astype(jnp.bfloat16)
    down_gradient = jnp.dot(active.T, lower_grad, preferred_element_type=jnp.float32)
    active_grad = jnp.dot(lower_grad, wide_down.T, preferred_element_type=jnp.float32)
    _, gelu_pull = jax.vjp(jax.nn.gelu, upper)
    upper_grad = gelu_pull(active_grad)[0].astype(jnp.bfloat16)
    up_gradient = jnp.dot(second.T, upper_grad, preferred_element_type=jnp.float32)
    second_grad = jnp.dot(upper_grad, wide_up.T, preferred_element_type=jnp.float32)
    _, norm_pull = jax.vjp(norm_rows, middle, wide_norms[2], wide_norms[3])
    middle_part, gain_two, shift_two = norm_pull(second_grad)
    middle_grad = block_grad + middle_part
    branch_grad = middle_grad.astype(jnp.bfloat16)
    out_gradient = jnp.dot(mixed_low.T, branch_grad, preferred_element_type=jnp.float32)
    mixed_grad = jnp.dot(branch_grad, wide_out.T, preferred_element_type=jnp.float32).astype(
        jnp.bfloat16
    )
    delta = jnp.sum(
        (mixed_grad.astype(jnp.float32) * mixed).reshape(rows_tok, heads, head_size), axis=-1
    ).T
    mixed_heads = mixed_grad.reshape(rows_tok, heads, head_size)

    def score_grads(
        query_rows, grad_rows, lse_rows, delta_rows, key_block, value_block, query_place, start
    ):
        scores, allowed = block_scores(query_rows, key_block, start, query_place, scale)
        probs = jnp.where(allowed[None], jnp.exp(scores - lse_rows[..., None]), 0.0)
        prob_grad = jnp.einsum(
            "qhd,khd->hqk", grad_rows, value_block, preferred_element_type=jnp.float32
        )
        score_grad = (probs * (prob_grad - delta_rows[..., None])).astype(jnp.bfloat16)
        return (probs, score_grad)

    def grad_step(query_total, item):
        key_block, value_block, start = item
        probs, score_grad = score_grads(
            query, mixed_heads, log_total, delta, key_block, value_block, place, start
        )
        query_total = (
            query_total
            + jnp.einsum("hqk,khd->qhd", score_grad, key_block, preferred_element_type=jnp.float32)
            * scale
        )
        key_part = (
            jnp.einsum("hqk,qhd->khd", score_grad, query, preferred_element_type=jnp.float32)
            * scale
        )
        value_part = jnp.einsum(
            "hqk,qhd->khd",
            probs.astype(jnp.bfloat16),
            mixed_heads,
            preferred_element_type=jnp.float32,
        )
        return (query_total, (key_part, value_part))

    query_total, (key_parts, value_parts) = lax.scan(
        grad_step,
        jnp.zeros((rows_tok, heads, head_size), jnp.float32),
        (key_blocks, value_blocks, starts),
    )
    key_sum, value_sum = (
        lax.psum_scatter(
            key_parts.reshape(seq_len, width).astype(jnp.bfloat16),
            "depth",
            scatter_dimension=0,
            tiled=True,
        ).astype(jnp.float32),
        lax.psum_scatter(
            value_parts.reshape(seq_len, width).astype(jnp.bfloat16),
            "depth",
            scatter_dimension=0,
            tiled=True,
        ).astype(jnp.float32),
    )
    query_grad = rotate(query_total, place, -1.0).reshape(rows_tok, width)
    key_grad = rotate(key_sum.reshape(rows_tok, heads, head_size), place, -1.0).reshape(
        rows_tok, width
    )
    projected_grad = jnp.concatenate([query_grad, key_grad, value_sum], axis=1).astype(jnp.bfloat16)
    qkv_gradient = jnp.dot(first.T, projected_grad, preferred_element_type=jnp.float32)
    first_grad = jnp.dot(projected_grad, wide_qkv.T, preferred_element_type=jnp.float32)
    _, first_pull = jax.vjp(norm_rows, float_input, wide_norms[0], wide_norms[1])
    input_part, gain_one, shift_one = first_pull(first_grad)
    input_grad = (middle_grad + input_part).astype(jnp.bfloat16)
    norms_full = jnp.stack([gain_one, shift_one, gain_two, shift_two])
    qkv_gradient, out_gradient, up_gradient, down_gradient, norm_gradient = (
        lax.psum_scatter(qkv_gradient, ("rows", "depth"), scatter_dimension=0, tiled=True),
        lax.psum_scatter(out_gradient, ("rows", "depth"), scatter_dimension=0, tiled=True),
        lax.psum_scatter(up_gradient, ("rows", "depth"), scatter_dimension=0, tiled=True),
        lax.psum_scatter(down_gradient, ("rows", "depth"), scatter_dimension=0, tiled=True),
        lax.psum_scatter(norms_full, ("rows", "depth"), scatter_dimension=1, tiled=True),
    )
    return (
        output,
        input_grad,
        history_grad,
        qkv_gradient,
        out_gradient,
        up_gradient,
        down_gradient,
        norm_gradient,
        depth_gradient,
    )


def solution(mesh):
    return jax.shard_map(
        local,
        mesh=mesh,
        in_specs=(
            P(("rows", "depth"), None),
            P("depth", "rows", None),
            P(("rows", "depth"), None),
            P(("rows", "depth")),
            P(("rows", "depth"), None),
            P(("rows", "depth"), None),
            P(("rows", "depth"), None),
            P(("rows", "depth"), None),
            P(None, ("rows", "depth")),
            P(),
        ),
        out_specs=(
            P(("rows", "depth"), None),
            P(("rows", "depth"), None),
            P("depth", "rows", None),
            P(("rows", "depth"), None),
            P(("rows", "depth"), None),
            P(("rows", "depth"), None),
            P(("rows", "depth"), None),
            P(None, ("rows", "depth")),
            P(),
        ),
        check_vma=False,
    )
```

profile of v0, /device:TPU:0, one launch (start us, length us, event | category | flops | bytes accessed | tf_op | source)
XLA Modules:
  0.0 878.0 jit_solution(8360385755623764965)
XLA Ops:
  11.4 42.3 %psum.14 = s32[]{:T(128)} all-reduce(s32[]{:T(128)} %get-tuple-element.118), channel_id=1, replica_groups=mesh['rows'=8,'depth'=4] {'rows','depth'}, use_global_device_ids=true, to_apply=%region_8.9 | all-reduce | flops 1 | bytes 8 | tf_op jit(solution)/shard_map/psum | solution.py:70
  54.3 40.6 %all-gather = bf16[32,24,4]{1,2,0:T(4,128)(2,1)S(1)} all-gather(bf16[1,24,4]{1,2,0:T(4,128)(2,1)S(1)} %convert_bitcast_fusion.1), channel_id=1, replica_groups=mesh['rows'=8,'depth'=4] {'rows','depth'}, dimensions={0}, use_global_device_ids=true | all-gather | bytes 6336 | tf_op jit(solution)/shard_map/all_gather | solution.py:66
  100.5 2.8 fusion.60
  103.8 8.7 all_gather.31
  112.9 11.0 %all_gather.32 = bf16[512,768]{0,1:T(8,128)(2,1)S(1)} all-gather(bf16[128,768]{0,1:T(8,128)(2,1)S(1)} %bitcast.77), channel_id=1, replica_groups=mesh['rows'=8,'depth'=4] {'depth'}, dimensions={0}, use_global_device_ids=true | all-gather | bytes 983040 | tf_op jit(solution)/shard_map/all_gather | solution.py:83
  132.0 63.2 %all-gather.10.cloned.1.call-done = bf16[768,3072]{1,0:T(8,128)(2,1)} async-done(((bf16[24,3072]{1,0:T(8,128)(2,1)}), bf16[768,3072]{1,0:T(8,128)(2,1)}) %all-gather.10.cloned.1.call-update) | async-done | bytes 4718608 | tf_op jit(solution)/shard_map/all_gather | solution.py:64
  195.3 3.3 fusion.64
  198.6 61.9 %all-gather.12.cloned.1.call-done = bf16[3072,768]{1,0:T(8,128)(2,1)} async-done(((bf16[96,768]{1,0:T(8,128)(2,1)}), bf16[3072,768]{1,0:T(8,128)(2,1)}) %all-gather.12.cloned.1.call-update) | async-done | bytes 4718608 | tf_op jit(solution)/shard_map/all_gather | solution.py:65
  260.5 5.2 fusion.10
  284.2 2.7 convolution_convert_fusion
  289.5 8.6 all_gather.36
  298.1 2.6 fusion.2
  300.9 2.6 fusion.31
  307.8 24.4 %reduce-scatter.25.cloned.1.call-done = bf16[128,768]{1,0:T(8,128)(2,1)} async-done(((bf16[512,768]{1,0:T(8,128)(2,1)}), bf16[128,768]{1,0:T(8,128)(2,1)}) %reduce-scatter.25.cloned.1.call-update) | async-done | bytes 196624
  334.2 4.1 fusion.28
  339.5 5.2 fusion.63
  346.1 5.9 fusion.36
  355.0 3.5 fusion.24
  358.9 5.6 multiply_reduce_fusion
  365.9 39.6 %all-reduce.1 = (f32[4,768]{1,0:T(4,128)S(1)}, f32[5]{0:T(128)}) all-reduce(f32[4,768]{1,0:T(4,128)S(1)} %pad_maximum_fusion.9, f32[5]{0:T(128)S(1)} %fusion.47), channel_id=9, replica_groups=mesh['rows'=8,'depth'=4] {'rows','depth'}, use_global_device_ids=true, to_apply=%region_24.25.clone | all-reduce | flops 3077 | bytes 24616
  406.1 57.8 %reduce-scatter.17.cloned.1.call-done = f32[24,768]{1,0:T(8,128)} async-done(((f32[768,768]{1,0:T(8,128)}), f32[24,768]{1,0:T(8,128)}) %reduce-scatter.17.cloned.1.call-update) | async-done | bytes 73744 | tf_op jit(solution)/shard_map/reduce_scatter | solution.py:249
  463.8 124.4 %reduce-scatter.15.cloned.1.call-done = f32[24,2304]{1,0:T(8,128)} async-done(((f32[768,2304]{1,0:T(8,128)}), f32[24,2304]{1,0:T(8,128)}) %reduce-scatter.15.cloned.1.call-update) | async-done | bytes 221200 | tf_op jit(solution)/shard_map/reduce_scatter | solution.py:248
  588.3 142.0 %reduce-scatter.19.cloned.1.call-done = f32[24,3072]{1,0:T(8,128)} async-done(((f32[768,3072]{1,0:T(8,128)}), f32[24,3072]{1,0:T(8,128)}) %reduce-scatter.19.cloned.1.call-update) | async-done | bytes 294928 | tf_op jit(solution)/shard_map/reduce_scatter | solution.py:250
  730.3 141.1 %reduce-scatter.21.cloned.1.call-done = f32[96,768]{1,0:T(8,128)} async-done(((f32[3072,768]{1,0:T(8,128)}), f32[96,768]{1,0:T(8,128)}) %reduce-scatter.21.cloned.1.call-update) | async-done | bytes 294928 | tf_op jit(solution)/shard_map/reduce_scatter | solution.py:251
  (210 shorter events, 53.3 us)
Async XLA Ops:
  7.2 93.3 %all-gather.6.cloned.1.call-start = ((), (), s32[]{:S(2)}) async-start(), calls=%async_computation.8 | async-start | bytes 3649536 | tf_op jit(solution)/shard_map/all_gather | solution.py:62
  7.9 122.2 %all-gather.8.cloned.1.call-start = ((), (), s32[]{:S(2)}) async-start(), calls=%async_computation.9 | async-start | bytes 1216512 | tf_op jit(solution)/shard_map/all_gather | solution.py:63
  8.7 186.6 %all-gather.10.cloned.1.call-start = ((), (), s32[]{:S(2)}) async-start(), calls=%async_computation.10 | async-start | bytes 4866048 | tf_op jit(solution)/shard_map/all_gather | solution.py:64
  9.4 251.1 %all-gather.12.cloned.1.call-start = ((), (), s32[]{:S(2)}) async-start(), calls=%async_computation.11 | async-start | bytes 4866048 | tf_op jit(solution)/shard_map/all_gather | solution.py:65
  10.0 296.6 %reduce-scatter.23.cloned.1.call-start = ((), (), s32[]{:S(2)}) async-start(), calls=%async_computation.16 | async-start | bytes 983040
  11.4 249.1 %copy-start.45 = (f32[128]{0:T(128)}, f32[128]{0:T(128)S(1)}, u32[]{:S(2)}) copy-start(f32[128]{0:T(128)S(1)} %get-tuple-element.117) | copy-start | bytes 1540
  100.4 12.4 %copy-start.33 = (f32[128,32]{0,1:T(8,128)}, f32[128,32]{0,1:T(8,128)S(1)}, u32[]{:S(2)}) copy-start(f32[128,32]{0,1:T(8,128)S(1)} %get-tuple-element.116) | copy-start | bytes 49156
  100.5 25.3 %copy-start.32 = (pred[128,512]{1,0:T(8,128)(4,1)}, pred[128,512]{1,0:T(8,128)(4,1)S(1)}, u32[]{:S(2)}) copy-start(pred[128,512]{1,0:T(8,128)(4,1)S(1)} %iota_compare_fusion) | copy-start | bytes 196612
  112.8 13.0 %copy-start.28 = (bf16[512,768]{0,1:T(8,128)(2,1)}, bf16[512,768]{0,1:T(8,128)(2,1)S(1)}, u32[]{:S(2)}) copy-start(bf16[512,768]{0,1:T(8,128)(2,1)S(1)} %copy.44) | copy-start | bytes 2359300
  131.8 136.3 %copy-start.34 = (f32[128]{0:T(128)}, f32[128]{0:T(128)S(1)}, u32[]{:S(2)}) copy-start(f32[128]{0:T(128)S(1)} %broadcast_multiply_fusion.1) | copy-start | bytes 1540
  132.0 136.1 %copy-start.38 = (f32[128]{0:T(128)}, f32[128]{0:T(128)S(1)}, u32[]{:S(2)}) copy-start(f32[128]{0:T(128)S(1)} %fusion.49) | copy-start | bytes 1540
  195.3 65.2 %copy-start.16 = (bf16[128,768]{1,0:T(8,128)(2,1)S(1)}, bf16[128,768]{1,0:T(8,128)(2,1)}, u32[]{:S(2)}) copy-start(bf16[128,768]{1,0:T(8,128)(2,1)} %param.12) | copy-start | bytes 589828
  195.3 70.4 %slice-start = ((s8[4718592]{0:T(1024)(128)(4,1)}), s8[524288]{0:T(1024)(128)(4,1)S(1)}, s32[]{:S(2)}) async-start(s8[4718592]{0:T(1024)(128)(4,1)} %bitcast.62), calls=%async_computation.18 | async-start | bytes 1048576
  198.5 67.1 %copy-start.2 = (f32[128,3072]{1,0:T(8,128)}, f32[128,3072]{1,0:T(8,128)S(1)}, u32[]{:S(2)}) copy-start(f32[128,3072]{1,0:T(8,128)S(1)} %fusion.64) | copy-start | bytes 4718596
  284.1 48.1 %reduce-scatter.25.cloned.1.call-start = ((), (), s32[]{:S(2)}) async-start(), calls=%async_computation.17 | async-start | bytes 983040
  289.3 69.6 %reduce-scatter.13.cloned.1.call-start = ((), (), s32[]{:S(2)}) async-start(), calls=%async_computation.7 | async-start | bytes 983040 | tf_op jit(solution)/shard_map/reduce_scatter | solution.py:136
  300.8 163.0 %reduce-scatter.17.cloned.1.call-start = ((), (), s32[]{:S(2)}) async-start(), calls=%async_computation.13 | async-start | bytes 2433024 | tf_op jit(solution)/shard_map/reduce_scatter | solution.py:249
  303.5 284.8 %reduce-scatter.15.cloned.1.call-start = ((), (), s32[]{:S(2)}) async-start(), calls=%async_computation.12 | async-start | bytes 7299072 | tf_op jit(solution)/shard_map/reduce_scatter | solution.py:248
  306.6 26.7 %copy-start.23 = (f32[128,12,64]{0,2,1:T(8,128)S(1)}, f32[128,12,64]{0,2,1:T(8,128)}, u32[]{:S(2)}) copy-start(f32[128,12,64]{0,2,1:T(8,128)} %fusion.11) | copy-start | bytes 1179652
  307.7 26.5 %copy-start.5 = (bf16[128,768]{1,0:T(8,128)(2,1)S(1)}, bf16[128,768]{1,0:T(8,128)(2,1)}, u32[]{:S(2)}) copy-start(bf16[128,768]{1,0:T(8,128)(2,1)} %param.10) | copy-start | bytes 589828
  307.7 26.5 %copy-start.41 = (f32[128]{0:T(128)S(1)}, f32[128]{0:T(128)}, u32[]{:S(2)}) copy-start(f32[128]{0:T(128)} %copy-done.40) | copy-start | bytes 1540
  307.7 26.5 %copy-start.52 = (f32[128]{0:T(128)S(1)}, f32[128]{0:T(128)}, u32[]{:S(2)}) copy-start(f32[128]{0:T(128)} %copy-done.51) | copy-start | bytes 1540
  338.4 391.9 %reduce-scatter.19.cloned.1.call-start = ((), (), s32[]{:S(2)}) async-start(), calls=%async_computation.14 | async-start | bytes 9732096 | tf_op jit(solution)/shard_map/reduce_scatter | solution.py:250
  344.7 526.7 %reduce-scatter.21.cloned.1.call-start = ((), (), s32[]{:S(2)}) async-start(), calls=%async_computation.15 | async-start | bytes 9732096 | tf_op jit(solution)/shard_map/reduce_scatter | solution.py:251
  (47 other events, 165.5 us)
Sparse Core Ops, SparseCore 0:
  10.9 62.9 all-gather.5
  76.9 53.1 all-gather.7
  133.0 62.2 all-gather.9
  198.0 62.3 all-gather.11
  284.2 22.0 reduce-scatter.22
  308.9 23.2 reduce-scatter.24
  334.7 23.2 reduce-scatter.12
  364.8 99.0 reduce-scatter.16
  470.1 118.1 reduce-scatter.14
  595.6 134.6 reduce-scatter.18
  736.8 134.5 reduce-scatter.20
where the time goes:
time: 879 us; the launch traced here: 878 us
  waiting for transfers between devices  619 us (70%)
  blocking collectives  151 us (17%)
  matrix products  53.7 us (6%)
  local copies, waits for them, and re-layouts  22.7 us (3%)
  between operations  15.4 us (2%)
  other arithmetic  15.2 us (2%)
    reduce_scatter x1, waiting for transfers between devices, local(): lax.psum_scatter(up_gradient, ('rows', 'depth'), scatter_dimension=0, til...  142 us
    reduce_scatter x1, waiting for transfers between devices, local(): lax.psum_scatter(down_gradient, ('rows', 'depth'), scatter_dimension=0, t...  141 us
    reduce_scatter x1, waiting for transfers between devices, local(): lax.psum_scatter(qkv_gradient, ('rows', 'depth'), scatter_dimension=0, ti...  124 us
    all_gather x1, waiting for transfers between devices, local(): lax.all_gather(up_weight, ('rows', 'depth'), axis=0, tiled=True)  63.2 us
    all_gather x1, waiting for transfers between devices, local(): lax.all_gather(down_weight, ('rows', 'depth'), axis=0, tiled=True)  61.9 us
    reduce_scatter x1, waiting for transfers between devices, local(): lax.psum_scatter(out_gradient, ('rows', 'depth'), scatter_dimension=0, ti...  57.8 us
    psum x1, blocking collectives, local(): total = lax.psum(jnp.sum(token_mask), ('rows', 'depth')).astype(jnp.float32)  42.3 us
    all_gather x1, blocking collectives, local(): lax.all_gather(norm_params.astype(jnp.bfloat16), ('rows', 'depth'), axis=...  40.6 us
  transfers between devices with their start and end apart: 11, of which 8 were waited for; matrix products, arithmetic and copies ran while one was open for 7% of the time, Pallas kernels for 0%

commit v1 on v0

--- a/solution.py
+++ b/solution.py
@@ -1,6 +1,11 @@
+import functools
+
 import jax
 import jax.numpy as jnp
+import numpy as np
 from jax import lax
+from jax.experimental import pallas as pl
+from jax.experimental.pallas import tpu as pltpu
 from jax.sharding import PartitionSpec as P
 
 HEADS = 12
@@ -263,33 +268,959 @@
         depth_gradient,
     )
 
+SEQ = 512
+OWN = 128
+WIDTH = 768
+ROWS = 8
+GROUP = 4
+PACK = 640
+BLOCK = WIDTH // ROWS
+CHUNK = BLOCK // GROUP
+QBLOCK = 256
+BF = jnp.bfloat16
+F32 = jnp.float32
+MESH = pl.DeviceIdType.MESH
+
+
+def dot(a, b, ca=1, cb=0):
+    return lax.dot_general(a, b, (((ca,), (cb,)), ((), ())), preferred_element_type=F32)
+
+
+def lane_id(shape):
+    return lax.broadcasted_iota(jnp.int32, shape, len(shape) - 1)
+
+
+def row_id(shape):
+    return lax.broadcasted_iota(jnp.int32, shape, len(shape) - 2)
+
+
+def tiles_of(value):
+    return [value[:, 128 * i : 128 * (i + 1)] for i in range(value.shape[1] // 128)]
+
+
+def permute_chunks(tiles, picks):
+    group = lax.div(lane_id(tiles[0].shape), jnp.int32(32))
+    out = []
+    for t in range(len(picks) // 4):
+        total, rolled = jnp.zeros_like(tiles[0]), {}
+        for j in range(4):
+            pick = picks[4 * t + j]
+            if pick is None:
+                continue
+            source, place = divmod(pick, 4)
+            shift = (j - place) * 32 % 128
+            if (source, shift) not in rolled:
+                value = tiles[source]
+                rolled[source, shift] = pltpu.roll(value, shift, 1) if shift else value
+            total = jnp.where(group == j, rolled[source, shift], total)
+        out.append(total)
+    return out
+
+
+def fold(tiles):
+    half = (len(tiles) + 1) // 2
+    low = [t[16:] for t in tiles]
+    if len(low) % 2:
+        low.append(jnp.zeros_like(low[0]))
+    return [t[:16] for t in tiles] + [
+        jnp.concatenate([low[i], low[half + i]], axis=0) for i in range(half)
+    ]
+
+
+def unfold(tiles, count):
+    half = (count + 1) // 2
+    rest = tiles[count:]
+    low = [rest[i][:8] for i in range(half)] + [rest[i][8:] for i in range(half)]
+    return [jnp.concatenate([tiles[i], low[i]], axis=0) for i in range(count)]
+
+
+def qkv_chunk(block, head, half):
+    return 24 * block + 2 * head + half
+
+
+def qkv_picks(d):
+    heads = [3 * d + i for i in range(3)]
+    picks = []
+    for block in range(2):
+        for half in range(2):
+            picks += [qkv_chunk(block, h, half) for h in heads]
+            picks.append(qkv_chunk(2, heads[2], half) if block == 0 else None)
+    return picks + [qkv_chunk(2, h, half) for h in heads[:2] for half in range(2)]
+
+
+def up_picks(d):
+    return [3 * (GROUP * r + d) + j for r in range(ROWS) for j in range(3)]
+
+
+def inverse_picks(per_device, count, tiles_each):
+    back = [None] * count
+    for d, picks in enumerate(per_device):
+        for place, pick in enumerate(picks):
+            if pick is not None:
+                back[pick] = 4 * tiles_each * d + place
+    return back
+
+
+QKV_BACK = inverse_picks([qkv_picks(d) for d in range(GROUP)], 72, 5)
+UP_BACK = inverse_picks([up_picks(d) for d in range(GROUP)], 96, 6)
+
+
+def tables():
+    half = HD // 2
+    freq = np.float32(10000.0) ** (-np.arange(half, dtype=np.float32) / np.float32(half))
+    angle = (np.arange(SEQ, dtype=np.float32)[:, None] * freq[None, :]).astype(np.float32)
+    angle = angle.astype(np.float64)
+    cosine, sine = np.ones((SEQ, 128), np.float32), np.zeros((SEQ, 128), np.float32)
+    cosine[:, :96] = np.tile(np.cos(angle), (1, 3))
+    sine[:, :96] = np.tile(np.sin(angle), (1, 3))
+    return cosine, sine
+
+
+def standardize(value):
+    center = value - jnp.mean(value, axis=-1, keepdims=True)
+    spread = jnp.mean(center * center, axis=-1, keepdims=True)
+    scale = lax.rsqrt(spread + 1e-05)
+    return center * scale, scale
+
+
+def norm_back(grad, gain, normal, scale):
+    part = grad * (1.0 + gain)
+    inner = jnp.mean(part, axis=-1, keepdims=True)
+    along = jnp.mean(part * normal, axis=-1, keepdims=True)
+    return scale * (part - inner - normal * along)
+
+
+def sublane_sum(value):
+    return jnp.sum(value.reshape(value.shape[0] // 8, 8, value.shape[1]), axis=0)
+
+
+SCRATCH = dict(
+    x_all=((GROUP, OWN, WIDTH), BF),
+    c_all=((GROUP, OWN, WIDTH), BF),
+    qp_s=((GROUP, 16, 1024), BF),
+    qp_l=((GROUP, 16, 1024), BF),
+    up_s=((GROUP, 16, 1152), BF),
+    up_l=((GROUP, 16, 1152), BF),
+    tmp=((BLOCK, WIDTH), F32),
+    w_qkv=((WIDTH, PACK), BF),
+    w_up=((WIDTH, WIDTH), BF),
+    w_down=((WIDTH, WIDTH), BF),
+    wo_l=((GROUP, ROWS, 16, 1152), BF),
+    w_out=((WIDTH, WIDTH), BF),
+    w_own=((384, WIDTH), BF),
+    norms=((8, WIDTH), F32),
+    normal=((SEQ, WIDTH), F32),
+    h1=((SEQ, WIDTH), BF),
+    qv=((SEQ, 256), BF),
+    kk=((SEQ, 256), BF),
+    v01=((SEQ, 128), BF),
+    probs=((3, SEQ, SEQ), F32),
+    o_l=((GROUP, 2, 384, 128), BF),
+    ob=((SEQ, WIDTH), BF),
+    y=((SEQ, WIDTH), F32),
+    h2=((SEQ, WIDTH), BF),
+    slope=((SEQ, WIDTH), F32),
+    act=((SEQ, WIDTH), BF),
+    dm=((SEQ, WIDTH), BF),
+    g_down=((WIDTH, WIDTH), F32),
+    g_up=((WIDTH, WIDTH), F32),
+    g_out=((WIDTH, WIDTH), F32),
+    g_qkv=((WIDTH, PACK), F32),
+    du=((SEQ, WIDTH), BF),
+    part=((SEQ, WIDTH), F32),
+    dy=((OWN, WIDTH), F32),
+    dyb=((GROUP, OWN, WIDTH), BF),
+    dob=((SEQ, 384), BF),
+    dq=((SEQ, 256), F32),
+    dk=((SEQ, 256), F32),
+    dv=((SEQ, 384), F32),
+    dqkv=((SEQ, PACK), BF),
+    terms=((8, WIDTH), F32),
+    terms2=((8, WIDTH), F32),
+    t0=((8, WIDTH), F32),
+    t1=((8, WIDTH), F32),
+    tz=((4, 8, WIDTH), F32),
+    td=((4, 8, WIDTH), F32),
+    a_qkv=((GROUP, CHUNK, PACK), F32),
+    a_up=((GROUP, CHUNK, WIDTH), F32),
+)
+for _name, _rows, _cols in (
+    ("down", BLOCK, WIDTH),
+    ("up", BLOCK, WIDTH),
+    ("out", 16, 1152),
+    ("qkv", BLOCK, PACK),
+):
+    SCRATCH["xs_" + _name] = ((4, _rows, _cols), BF)
+    SCRATCH["xl_" + _name] = ((4, _rows, _cols), BF)
+    SCRATCH["zs_" + _name] = ((3, _rows, _cols), BF)
+    SCRATCH["zl_" + _name] = ((3, _rows, _cols), BF)
+    SCRATCH["f_" + _name] = ((_rows, _cols), F32)
+for _name in ("mix", "mid", "in"):
+    SCRATCH["s1_" + _name] = ((2, OWN, WIDTH), BF)
+    SCRATCH["l1_" + _name] = ((2, OWN, WIDTH), BF)
+    SCRATCH["s2_" + _name] = ((OWN, WIDTH), BF)
+    SCRATCH["l2_" + _name] = ((OWN, WIDTH), BF)
+N_SEMS = 160
+N_IN = 12
+N_OUT = 9
+
+
+class Names:
+    pass
+
+
+def fused_kernel(*refs):
+    (x_in, hist, cot, mask, wq, wo, wu, wd, nrm, dw, cosine, sine) = refs[:N_IN]
+    (out_o, ig_o, hg_o, gq_o, go_o, gu_o, gd_o, ng_o, dg_o) = refs[N_IN : N_IN + N_OUT]
+    s = Names()
+    for name, ref in zip(SCRATCH, refs[N_IN + N_OUT :]):
+        setattr(s, name, ref)
+    send_sems, recv_sems = refs[-2:]
+
+    r, d = lax.axis_index("rows"), lax.axis_index("depth")
+    z, x = lax.div(r, 2), lax.rem(r, 2)
+    yy, c = lax.div(d, 2), lax.rem(d, 2)
+    other_x, other_c, other_y = 1 - x, 1 - c, 1 - yy
+    x_dev = (2 * z + other_x, d)
+    z_of = [lax.rem(z + k, 4) for k in range(4)]
+    z_dev = [(2 * zk + x, d) for zk in z_of]
+    core_d, y_d, far_d = 2 * yy + other_c, 2 * other_y + c, 2 * other_y + other_c
+    core_dev, y_dev, far_dev = (r, core_d), (r, y_d), (r, far_d)
+    mates = ((core_d, core_dev), (y_d, y_dev), (far_d, far_dev))
+    counter = [0]
+    sent = []
+
+    def copy_to(src, dst, device):
+        index = counter[0]
+        counter[0] += 1
+        copy = pltpu.make_async_remote_copy(
+            src_ref=src,
+            dst_ref=dst,
+            send_sem=send_sems.at[index],
+            recv_sem=recv_sems.at[index],
+            device_id=device,
+            device_id_type=MESH,
+        )
+        copy.start()
+        sent.append(copy)
+        return copy
+
+    def rows_at(ref, index, size):
+        return ref.at[pl.ds(pl.multiple_of(index * size, size), size)]
+
+    def by_rows(count, step, body):
+        def one(i, carry):
+            body(pl.ds(pl.multiple_of(i * step, step), step))
+            return carry
+
+        lax.fori_loop(0, count // step, one, 0)
+
+    barrier = pltpu.get_barrier_semaphore()
+    for device in (x_dev, *z_dev[1:], core_dev, y_dev, far_dev):
+        pl.semaphore_signal(barrier, inc=1, device_id=device, device_id_type=MESH)
+    pl.semaphore_wait(barrier, 7)
+
+    class Gather:
+        def __init__(self, piece):
+            self.piece = piece
+
+        def send(self):
+            mine = self.piece(r)
+            self.along_z = [copy_to(mine, mine, z_dev[k]) for k in (1, 2, 3)]
+            self.along_x = [copy_to(mine, mine, x_dev)]
+
+        def forward(self):
+            for k in (1, 2, 3):
+                self.along_z[k - 1].wait_recv()
+                piece = self.piece(2 * z_of[4 - k] + x)
+                self.along_x.append(copy_to(piece, piece, x_dev))
+
+        def finish(self):
+            for copy in self.along_x:
+                copy.wait_recv()
+
+    class GroupGather:
+        def __init__(self, slab):
+            self.slab = slab
+
+        def send(self):
+            mine = self.slab(d)
+            self.to_core = copy_to(mine, mine, core_dev)
+            self.to_y = copy_to(mine, mine, y_dev)
+
+        def relay(self):
+            self.to_y.wait_recv()
+            slab = self.slab(y_d)
+            self.on = copy_to(slab, slab, core_dev)
+
+        def finish(self):
+            self.to_core.wait_recv()
+            self.on.wait_recv()
+
+    class RowSum:
+        def __init__(self, name, block, step):
+            self.xs, self.xl, self.zs, self.zl, self.total = (
+                getattr(s, p + name) for p in ("xs_", "xl_", "zs_", "zl_", "f_")
+            )
+            self.block, self.step = block, step
+            self.count = self.total.shape[0]
+
+        def send(self):
+            self.along_x = []
+            for k in (2, 1, 3, 0):
+                zk = z_of[k]
+
+                def stage(at):
+                    self.xs[zk, at, :] = self.block(2 * zk + other_x, at).astype(BF)
+
+                by_rows(self.count, self.step, stage)
+                self.along_x.append(copy_to(self.xs.at[zk], self.xl.at[zk], x_dev))
+
+        def middle(self):
+            self.along_z = {}
+            for place, k in enumerate((2, 1, 3)):
+                self.along_x[place].wait_recv()
+                zk = z_of[k]
+
+                def stage(at):
+                    value = self.block(2 * zk + x, at) + self.xl[zk, at, :].astype(F32)
+                    self.zs[k - 1, at, :] = value.astype(BF)
+
+                by_rows(self.count, self.step, stage)
+                self.along_z[k] = copy_to(self.zs.at[k - 1], self.zl.at[k - 1], z_dev[k])
+
+        def finish(self):
+            self.along_x[3].wait_recv()
+            for k in (1, 2, 3):
+                self.along_z[k].wait_recv()
+
+            def stage(at):
+                value = self.block(r, at) + self.xl[z, at, :].astype(F32)
+                for k in range(3):
+                    value = value + self.zl[k, at, :].astype(F32)
+                self.total[at, :] = value
+
+            by_rows(self.count, self.step, stage)
+
+    class GroupSum:
+        def __init__(self, name, source):
+            self.s1, self.l1, self.s2, self.l2 = (
+                getattr(s, p + name) for p in ("s1_", "l1_", "s2_", "l2_")
+            )
+            self.source = source
+
+        def block(self, index, at):
+            return self.source[pl.ds(pl.multiple_of(index * OWN + at.start, at.size), at.size), :]
+
+        def send(self):
+            self.first = []
+            for j, yj in enumerate((other_y, yy)):
+
+                def stage(at):
+                    self.s1[j, at, :] = self.block(2 * yj + other_c, at).astype(BF)
+
+                by_rows(OWN, 32, stage)
+                self.first.append(copy_to(self.s1.at[j], self.l1.at[j], core_dev))
+
+        def middle(self):
+            self.first[0].wait_recv()
+
+            def stage(at):
+                value = self.block(2 * other_y + c, at) + self.l1[0, at, :].astype(F32)
+                self.s2[at, :] = value.astype(BF)
+
+            by_rows(OWN, 32, stage)
+            self.second = copy_to(self.s2, self.l2, y_dev)
+
+        def wait(self):
+            self.first[1].wait_recv()
+            self.second.wait_recv()
+
+        def value(self, at):
+            return (
+                self.block(d, at)
+                + self.l1[1, at, :].astype(F32)
+                + self.l2[at, :].astype(F32)
+            )
+
+    out_gather = Gather(lambda i: s.wo_l.at[d, i])
+    for t, tile in enumerate(fold(tiles_of(wo[...].astype(F32)))):
+        s.wo_l[d, r, :, 128 * t : 128 * (t + 1)] = tile.astype(BF)
+    out_gather.send()
+
+    lane = lane_id((CHUNK, 128))
+    eye = row_id((CHUNK, CHUNK)) == lane_id((CHUNK, CHUNK))
+    extra = jnp.zeros((CHUNK, 128), F32)
+    for k in range(4):
+        column = jnp.sum(jnp.where(eye, nrm[k : k + 1, :], 0.0), axis=1, keepdims=True)
+        high = column.astype(BF).astype(F32)
+        extra = jnp.where(lane == 96 + k, high, extra)
+        extra = jnp.where(lane == 100 + k, column - high, extra)
+    mask_row = mask[...].astype(F32)
+    ones = jnp.sum(mask_row, axis=1, keepdims=True)
+    extra = jnp.where((lane == 104) & (row_id((CHUNK, 128)) == 0), ones, extra)
+
+    wq_tiles = tiles_of(wq[...].astype(F32))
+    for k in range(GROUP):
+        tiles = permute_chunks(wq_tiles, qkv_picks(k))
+        tiles[2] = tiles[2] + extra
+        for t, tile in enumerate(fold(tiles)):
+            s.qp_s[k, :, 128 * t : 128 * (t + 1)] = tile.astype(BF)
+    qp_copies = [copy_to(s.qp_s.at[m], s.qp_l.at[d], device) for m, device in mates]
+    s.qp_l[d] = s.qp_s[d]
+
+    s.x_all[d] = x_in[...]
+    x_gather = GroupGather(lambda i: s.x_all.at[i])
+    x_gather.send()
+
+    wu_tiles = tiles_of(wu[...].astype(F32))
+    for k in range(GROUP):
+        for t, tile in enumerate(fold(permute_chunks(wu_tiles, up_picks(k)))):
+            s.up_s[k, :, 128 * t : 128 * (t + 1)] = tile.astype(BF)
+    up_copies = [copy_to(s.up_s.at[m], s.up_l.at[d], device) for m, device in mates]
+    s.up_l[d] = s.up_s[d]
+
+    diagonal = jnp.where(
+        row_id((OWN, OWN)) == lane_id((OWN, OWN)), jnp.broadcast_to(mask_row, (OWN, OWN)), 0.0
+    )
+    s.c_all[d] = dot(diagonal.astype(BF), cot[...]).astype(BF)
+    c_gather = GroupGather(lambda i: s.c_all.at[i])
+    c_gather.send()
+
+    rows_at(s.w_down, r, BLOCK)[...] = wd[...]
+
+    def assemble(landing, count, target):
+        for k in range(GROUP):
+            tiles = [t.astype(F32) for t in tiles_of(landing[k])]
+            for t, tile in enumerate(unfold(tiles, count)):
+                s.tmp[CHUNK * k : CHUNK * (k + 1), 128 * t : 128 * (t + 1)] = tile
+        rows_at(target, r, BLOCK)[...] = s.tmp[:, : 128 * count].astype(BF)
+
+    for copy in qp_copies:
+        copy.wait_recv()
+    assemble(s.qp_l, 5, s.w_qkv)
+    qkv_gather = Gather(lambda i: rows_at(s.w_qkv, i, BLOCK))
+    qkv_gather.send()
+    for copy in up_copies:
+        copy.wait_recv()
+    assemble(s.up_l, 6, s.w_up)
+    up_gather = Gather(lambda i: rows_at(s.w_up, i, BLOCK))
+    up_gather.send()
+    down_gather = Gather(lambda i: rows_at(s.w_down, i, BLOCK))
+    down_gather.send()
+
+    x_gather.relay()
+    c_gather.relay()
+    out_gather.forward()
+    x_gather.finish()
+
+    for i in range(GROUP):
+
+        def normalize(at, i=i):
+            normal, _ = standardize(s.x_all[i, at, :].astype(F32))
+            s.normal[pl.ds(pl.multiple_of(OWN * i + at.start, at.size), at.size), :] = normal
+
+        by_rows(OWN, 64, normalize)
+    qkv_gather.forward()
+    out_gather.finish()
+    slab_gather = GroupGather(lambda i: s.wo_l.at[i])
+    slab_gather.send()
+    qkv_gather.finish()
+
+    lane = lane_id((8, 128))
+    row = row_id((8, 128))
+    pick = jnp.where((lane == 96 + row) | (lane == 100 + row), 1.0, 0.0)
+    pick = jnp.where(row < 4, pick, jnp.where((row == 4) & (lane == 104), 1.0, 0.0))
+    s.norms[...] = dot(pick.astype(BF), s.w_qkv[:, 256:384], 1, 1)
+    total = jnp.sum(s.norms[4:5, :], axis=1, keepdims=True)
+    loss_scale = (SEQ * ROWS) / total
+    own_weight = dw[d]
+    last_weight = dw[GROUP]
+
+    def first_norm(at):
+        value = s.normal[at, :] * (1.0 + s.norms[0:1, :]) + s.norms[1:2, :]
+        s.h1[at, :] = value.astype(BF)
+
+    by_rows(SEQ, 64, first_norm)
+
+    def project(at):
+        value = dot(s.h1[at, :], s.w_qkv[...])
+        co, si = cosine[at, :], sine[at, :]
+        for left, target in ((0, s.qv), (256, s.kk)):
+            a, b = value[:, left : left + 128], value[:, left + 128 : left + 256]
+            target[at, :128] = (a * co - b * si).astype(BF)
+            target[at, 128:] = (b * co + a * si).astype(BF)
+        s.v01[at, :] = value[:, 512:].astype(BF)
+
+    by_rows(SEQ, 256, project)
+    slab_gather.relay()
+    c_gather.finish()
+
+    s.terms[...] = jnp.zeros((8, WIDTH), F32)
+    for i in range(GROUP):
+
+        def loss_rows(at, i=i):
+            here = pl.ds(pl.multiple_of(OWN * i + at.start, at.size), at.size)
+            grad = s.c_all[i, at, :].astype(F32) * loss_scale
+            s.dm[here, :] = (last_weight * grad).astype(BF)
+            hg_o[here, :] = (own_weight * grad).astype(BF)
+            s.terms[...] += sublane_sum(grad * hist[here, :].astype(F32))
+
+        by_rows(OWN, 32, loss_rows)
+    up_gather.forward()
+
+    lane2 = lax.div(lax.rem(lane_id((1, 256)), 128), jnp.int32(32))
+    head_mask = [jnp.where(lane2 == h, 1.0, 0.0).astype(BF) for h in range(3)]
+    tail_mask = jnp.where(lane2 == 3, 1.0, 0.0).astype(BF)
+    half_id = lax.div(lane_id((1, 128)), jnp.int32(64))
+    half_mask = [jnp.where(half_id == h, 1.0, 0.0).astype(BF) for h in range(2)]
+    root = HD**-0.5
+    o_gathers = []
+    for b in range(2):
+        rows = slice(QBLOCK * b, QBLOCK * (b + 1))
+        keys = QBLOCK * (b + 1)
+        query = s.qv[rows, :]
+        allowed = row_id((QBLOCK, keys)) + QBLOCK * b >= lane_id((QBLOCK, keys))
+        first = jnp.zeros((QBLOCK, 128), F32)
+        third = None
+        for h in range(3):
+            scores = dot(query * head_mask[h], s.kk[:keys, :], 1, 1) * root
+            scores = jnp.where(allowed, scores, -1e30)
+            raised = jnp.exp(scores - jnp.max(scores, axis=1, keepdims=True))
+            probs = raised * (1.0 / jnp.sum(raised, axis=1, keepdims=True))
+            s.probs[h, rows, :keys] = probs
+            if h < 2:
+                first = first + dot(probs.astype(BF), s.v01[:keys, :] * half_mask[h])
+            else:
+                third = dot(probs.astype(BF), s.qv[:keys, :])
+        s.o_l[d, b, :QBLOCK, :] = first.astype(BF)
+        lane = lane_id((QBLOCK, 128))
+        third = jnp.where(
+            lane < 32, pltpu.roll(third[:, :128], 32, 1), pltpu.roll(third[:, 128:], 64, 1)
+        )
+        lane = lane_id((OWN, 128))
+        third = jnp.where(lane < 64, third[:OWN], pltpu.roll(third[OWN:], 64, 1))
+        s.o_l[d, b, QBLOCK:, :] = third.astype(BF)
+        o_gathers.append(GroupGather(lambda i, b=b: s.o_l.at[i, b]))
+        o_gathers[b].send()
+        if b == 0:
+            slab_gather.finish()
+            for k in range(GROUP):
+                for i in range(ROWS):
+                    tiles = [t.astype(F32) for t in tiles_of(s.wo_l[k, i])]
+                    at = CHUNK * (GROUP * i + k)
+                    for t, tile in enumerate(unfold(tiles, 6)):
+                        s.g_out[at : at + CHUNK, 128 * t : 128 * (t + 1)] = tile
+    down_gather.forward()
+
+    def out_place(head):
+        k, h = divmod(head, 3)
+        return 128 * k + 64 * h if h < 2 else 512 + 64 * k
+
+    for head in range(HEADS):
+        at = out_place(head)
+        s.w_out[at : at + 64, :] = s.g_out[64 * head : 64 * head + 64, :].astype(BF)
+    s.w_own[...] = jnp.zeros((384, WIDTH), BF)
+    third_rows = rows_at(s.w_out.at[pl.ds(512, 256)], d, 64)
+    s.w_own[96:128, :] = third_rows[:32, :]
+    s.w_own[224:256, :] = third_rows[32:, :]
+    s.w_own[256:, :] = rows_at(s.w_out.at[pl.ds(0, 512)], d, 128)[...]
+
+    for b in range(2):
+        o_gathers[b].relay()
+        o_gathers[b].finish()
+        rows = slice(QBLOCK * b, QBLOCK * (b + 1))
+        thirds = []
+        for k in range(GROUP):
+            s.ob[rows, 128 * k : 128 * (k + 1)] = s.o_l[k, b, :QBLOCK, :]
+            thirds.append(s.o_l[k, b, QBLOCK:, :].astype(F32))
+        lane = lane_id((OWN, 128))
+        for p in range(2):
+            even, odd = thirds[2 * p], thirds[2 * p + 1]
+            top = jnp.where(lane < 64, even, pltpu.roll(odd, 64, 1))
+            low = jnp.where(lane < 64, pltpu.roll(even, 64, 1), odd)
+            cols = slice(512 + 128 * p, 640 + 128 * p)
+            s.ob[QBLOCK * b : QBLOCK * b + OWN, cols] = top.astype(BF)
+            s.ob[QBLOCK * b + OWN : QBLOCK * (b + 1), cols] = low.astype(BF)
+        s.y[rows, :] = dot(s.ob[rows, :], s.w_out[...])
+        for i in (2 * b, 2 * b + 1):
+
+            def second_norm(at, i=i):
+                here = pl.ds(pl.multiple_of(OWN * i + at.start, at.size), at.size)
+                value = s.y[here, :] + s.x_all[i, at, :].astype(F32)
+                s.y[here, :] = value
+                normal, _ = standardize(value)
+                value = normal * (1.0 + s.norms[2:3, :]) + s.norms[3:4, :]
+                s.h2[here, :] = value.astype(BF)
+
+            by_rows(OWN, 64, second_norm)
+
+    up_gather.finish()
+
+    def widen(at):
+        s.part[at, :] = dot(s.h2[at, :], s.w_up[...])
+
+    by_rows(SEQ, 256, widen)
+
+    def gate(at):
+        u = s.part[at, :]
+        rate = 0.7978845608028654
+        bend = jnp.tanh(rate * (u + 0.044715 * u * u * u))
+        s.act[at, :] = (0.5 * u * (1.0 + bend)).astype(BF)
+        inner = rate * (1.0 + 3 * 0.044715 * u * u)
+        s.slope[at, :] = 0.5 * (1.0 + bend) + 0.5 * u * (1.0 - bend * bend) * inner
+
+    by_rows(SEQ, 32, gate)
+
+    def block_of(ref):
+        def block(index, at):
+            return ref[pl.ds(pl.multiple_of(index * BLOCK + at.start, at.size), at.size), :]
+
+        return block
+
+    for i in range(3):
+        cols = slice(QBLOCK * i, QBLOCK * (i + 1))
+        s.g_down[cols, :] = dot(s.act[:, cols], s.dm[...], 0, 0)
+    down_sum = RowSum("down", block_of(s.g_down), 16)
+    down_sum.send()
+
+    down_gather.finish()
+
+    def narrow(at):
+        value = dot(s.dm[at, :], s.w_down[...], 1, 1)
+        s.du[at, :] = (value * s.slope[at, :]).astype(BF)
+
+    by_rows(SEQ, 256, narrow)
+
+    def second_back(at):
+        s.part[at, :] = dot(s.du[at, :], s.w_up[...], 1, 1)
+
+    by_rows(SEQ, 256, second_back)
+    mid_sum = GroupSum("mid", s.part)
+    mid_sum.send()
+    down_sum.middle()
+
+    for i in range(3):
+        cols = slice(QBLOCK * i, QBLOCK * (i + 1))
+        s.g_up[cols, :] = dot(s.h2[:, cols], s.du[...], 0, 0)
+    up_sum = RowSum("up", block_of(s.g_up), 16)
+    up_sum.send()
+    mid_sum.middle()
+    mid_sum.wait()
+
+    s.terms2[...] = jnp.zeros((8, WIDTH), F32)
+    s.t0[...] = jnp.zeros((8, WIDTH), F32)
+
+    def second_norm_back(at):
+        here = pl.ds(pl.multiple_of(OWN * d + at.start, at.size), at.size)
+        grad = mid_sum.value(at)
+        value = s.y[here, :]
+        normal, scale = standardize(value)
+        loss = s.c_all[d, at, :].astype(F32) * loss_scale
+        back = last_weight * loss + norm_back(grad, s.norms[2:3, :], normal, scale)
+        s.dy[at, :] = back
+        s.dyb[d, at, :] = back.astype(BF)
+        s.t0[2:3, :] += jnp.sum(grad * normal, axis=0, keepdims=True)
+        s.t0[3:4, :] += jnp.sum(grad, axis=0, keepdims=True)
+        s.terms2[...] += sublane_sum(loss * value)
+
+    by_rows(OWN, 32, second_norm_back)
+    dy_gather = GroupGather(lambda i: s.dyb.at[i])
+    dy_gather.send()
+
+    def block_out(at):
+        value = dot(s.act[at, :], s.w_down[...])
+        s.part[at, :] = value
+
+    by_rows(SEQ, 256, block_out)
+    for i in range(GROUP):
+
+        def mix(at, i=i):
+            here = pl.ds(pl.multiple_of(OWN * i + at.start, at.size), at.size)
+            value = s.part[here, :]
+            loss = s.c_all[i, at, :].astype(F32) * loss_scale
+            s.terms2[...] += sublane_sum(loss * value)
+            s.part[here, :] = own_weight * hist[here, :].astype(F32) + last_weight * value
+
+        by_rows(OWN, 32, mix)
+    mix_sum = GroupSum("mix", s.part)
+    mix_sum.send()
+    up_sum.middle()
+    dy_gather.relay()
+    mix_sum.middle()
+    dy_gather.finish()
+
+    by_group = s.dyb[...].reshape(SEQ, WIDTH)
+
+    s.dob[...] = dot(by_group, s.w_own[...], 1, 1).astype(BF)
+    for p in range(3):
+        cols = slice(QBLOCK * p, QBLOCK * (p + 1))
+        value = dot(s.ob[:, cols], by_group, 0, 0)
+        for i in range(4):
+            place = QBLOCK * p + 64 * i
+            for head in range(HEADS):
+                if out_place(head) == place:
+                    s.g_out[64 * head : 64 * head + 64, :] = value[64 * i : 64 * i + 64]
+
+    def out_block(index, at):
+        start = pl.multiple_of((GROUP * index + d) * CHUNK, 8)
+        tiles = tiles_of(s.g_out[pl.ds(start, CHUNK), :])
+        return jnp.concatenate(fold(tiles), axis=1)
+
+    out_sum = RowSum("out", out_block, 16)
+    out_sum.send()
+    mix_sum.wait()
+
+    def write_out(at):
+        here = pl.ds(pl.multiple_of(OWN * d + at.start, at.size), at.size)
+        out_o[at, :] = (mix_sum.value(at) + last_weight * s.y[here, :]).astype(BF)
+
+    by_rows(OWN, 32, write_out)
+
+    for b in range(2):
+        rows = slice(QBLOCK * b, QBLOCK * (b + 1))
+        keys = QBLOCK * (b + 1)
+        query = s.qv[rows, :]
+        dq = jnp.zeros((QBLOCK, 256), F32)
+        for h in range(3):
+            probs = s.probs[h, rows, :keys]
+            if h < 2:
+                grad = s.dob[rows, 256:] * half_mask[h]
+                dp = dot(grad, s.v01[:keys, :], 1, 1)
+            else:
+                grad = s.dob[rows, :256]
+                dp = dot(grad, s.qv[:keys, :], 1, 1)
+            delta = jnp.sum(dp * probs, axis=1, keepdims=True)
+            ds = (probs * (dp - delta)).astype(BF)
+            dq = dq + dot(ds, s.kk[:keys, :] * head_mask[h])
+            dk = dot(ds, query * head_mask[h], 0, 0) * root
+            dv = dot(probs.astype(BF), grad, 0, 0)
+            cols = slice(256, 384) if h < 2 else slice(0, 256)
+            if b == 0:
+                old, new = slice(0, QBLOCK), None
+            else:
+                old, new = slice(0, QBLOCK), slice(QBLOCK, SEQ)
+            if h == 0 and b == 0:
+                s.dk[old, :] = dk[:QBLOCK]
+            else:
+                s.dk[old, :] += dk[:QBLOCK]
+            if b == 0 and h != 1:
+                s.dv[old, cols] = dv[:QBLOCK]
+            else:
+                s.dv[old, cols] += dv[:QBLOCK]
+            if new is not None:
+                if h == 0:
+                    s.dk[new, :] = dk[QBLOCK:]
+                else:
+                    s.dk[new, :] += dk[QBLOCK:]
+                if h != 1:
+                    s.dv[new, cols] = dv[QBLOCK:]
+                else:
+                    s.dv[new, cols] += dv[QBLOCK:]
+        s.dq[rows, :] = dq * root
+
+    def turn_back(at):
+        co, si = cosine[at, :], sine[at, :]
+        for left, source in ((0, s.dq), (256, s.dk)):
+            a, b = source[at, :128], source[at, 128:]
+            first, second = a * co + b * si, b * co - a * si
+            if left == 0:
+                first, second = first + s.dv[at, :128], second + s.dv[at, 128:256]
+            s.dqkv[at, left : left + 128] = first.astype(BF)
+            s.dqkv[at, left + 128 : left + 256] = second.astype(BF)
+        s.dqkv[at, 512:] = s.dv[at, 256:].astype(BF)
+
+    by_rows(SEQ, 64, turn_back)
+    for i in range(3):
+        cols = slice(QBLOCK * i, QBLOCK * (i + 1))
+        s.g_qkv[cols, :] = dot(s.h1[:, cols], s.dqkv[...], 0, 0)
+    qkv_sum = RowSum("qkv", block_of(s.g_qkv), 16)
+    qkv_sum.send()
+
+    def first_back(at):
+        s.part[at, :] = dot(s.dqkv[at, :], s.w_qkv[...], 1, 1)
+
+    by_rows(SEQ, 256, first_back)
+    in_sum = GroupSum("in", s.part)
+    in_sum.send()
+    out_sum.middle()
+    in_sum.middle()
+
+    def spread(total, landing):
+        copies = [
+            copy_to(total.at[pl.ds(pl.multiple_of(CHUNK * m, CHUNK), CHUNK)], landing.at[d], device)
+            for m, device in mates
+        ]
+        landing[d] = total[pl.ds(pl.multiple_of(CHUNK * d, CHUNK), CHUNK), :]
+        return copies
+
+    down_sum.finish()
+    gd_o[...] = s.f_down[...]
+    up_sum.finish()
+    up_spread = spread(s.f_up, s.a_up)
+    qkv_sum.middle()
+    in_sum.wait()
+
+    def first_norm_back(at):
+        grad = in_sum.value(at)
+        normal, scale = standardize(x_in[at, :].astype(F32))
+        back = norm_back(grad, s.norms[0:1, :], normal, scale)
+        ig_o[at, :] = (s.dy[at, :] + back).astype(BF)
+        s.t0[0:1, :] += jnp.sum(grad * normal, axis=0, keepdims=True)
+        s.t0[1:2, :] += jnp.sum(grad, axis=0, keepdims=True)
+
+    by_rows(OWN, 32, first_norm_back)
+
+    lane = lane_id((1, WIDTH))
+    own_term = jnp.sum(jnp.sum(s.terms[...], axis=0, keepdims=True), axis=1, keepdims=True)
+    last_term = jnp.sum(jnp.sum(s.terms2[...], axis=0, keepdims=True), axis=1, keepdims=True)
+    s.t0[4:5, :] = jnp.where(lane == d, own_term, jnp.where(lane == GROUP, last_term, 0.0))
+    small = copy_to(s.t0, s.t1, x_dev)
+    out_sum.finish()
+    for t, tile in enumerate(unfold(tiles_of(s.f_out[...]), 6)):
+        go_o[:, 128 * t : 128 * (t + 1)] = tile
+    small.wait_recv()
+    s.tz[z] = s.t0[...] + s.t1[...]
+    small_z = [copy_to(s.tz.at[z], s.tz.at[z], z_dev[k]) for k in (1, 2, 3)]
+    for copy in up_spread:
+        copy.wait_recv()
+    tiles = [t for k in range(GROUP) for t in tiles_of(s.a_up[k])]
+    for t, tile in enumerate(permute_chunks(tiles, UP_BACK)):
+        gu_o[:, 128 * t : 128 * (t + 1)] = tile
+    for copy in small_z:
+        copy.wait_recv()
+    s.td[d] = (s.tz[0] + s.tz[1]) + (s.tz[2] + s.tz[3])
+    small_d = [copy_to(s.td.at[d], s.td.at[d], device) for m, device in mates]
+
+    qkv_sum.finish()
+    qkv_spread = spread(s.f_qkv, s.a_qkv)
+    for copy in small_d:
+        copy.wait_recv()
+    value = (s.td[0] + s.td[1]) + (s.td[2] + s.td[3])
+    dg_o[...] = value[:, :128]
+    choose = row_id((WIDTH, 128)) == lane_id((WIDTH, 128)) + CHUNK * (GROUP * r + d)
+    ng_o[...] = lax.dot_general(
+        value,
+        jnp.where(choose, 1.0, 0.0),
+        (((1,), (0,)), ((), ())),
+        preferred_element_type=F32,
+        precision=lax.Precision.HIGHEST,
+    )
+    for copy in qkv_spread:
+        copy.wait_recv()
+    tiles = [t for k in range(GROUP) for t in tiles_of(s.a_qkv[k])]
+    for t, tile in enumerate(permute_chunks(tiles, QKV_BACK)):
+        gq_o[:, 128 * t : 128 * (t + 1)] = tile
+    for copy in sent:
+        copy.wait_send()
+
+
+def fused(
+    block_input,
+    history,
+    cotangent,
+    token_mask,
+    qkv_weight,
+    out_weight,
+    up_weight,
+    down_weight,
+    norm_params,
+    depth_weights,
+):
+    cosine, sine = tables()
+    vmem = pl.BlockSpec(memory_space=pltpu.VMEM)
+    smem = pl.BlockSpec(memory_space=pltpu.SMEM)
+    shape = jax.ShapeDtypeStruct
+    outs = pl.pallas_call(
+        fused_kernel,
+        out_shape=(
+            shape((OWN, WIDTH), BF),
+            shape((OWN, WIDTH), BF),
+            shape((SEQ, WIDTH), BF),
+            shape((CHUNK, 3 * WIDTH), F32),
+            shape((CHUNK, WIDTH), F32),
+            shape((CHUNK, 4 * WIDTH), F32),
+            shape((BLOCK, WIDTH), F32),
+            shape((8, 128), F32),
+            shape((8, 128), F32),
+        ),
+        in_specs=[vmem] * 9 + [smem] + [vmem] * 2,
+        out_specs=[vmem] * 9,
+        scratch_shapes=[pltpu.VMEM(dims, kind) for dims, kind in SCRATCH.values()]
+        + [pltpu.SemaphoreType.DMA((N_SEMS,))] * 2,
+        compiler_params=pltpu.CompilerParams(
+            collective_id=0, has_side_effects=True, vmem_limit_bytes=62 * 2**20
+        ),
+        cost_estimate=pl.CostEstimate(flops=12 * 10**9, bytes_accessed=4 * 10**6, transcendentals=10**6),
+    )(
+        block_input,
+        history.reshape(SEQ, WIDTH),
+        cotangent,
+        token_mask.reshape(1, OWN),
+        qkv_weight,
+        out_weight,
+        up_weight,
+        down_weight,
+        norm_params,
+        depth_weights,
+        jnp.asarray(cosine),
+        jnp.asarray(sine),
+    )
+    out, input_grad, history_grad, g_qkv, g_out, g_up, g_down, g_norm, g_depth = outs
+    return (
+        out,
+        input_grad,
+        history_grad.reshape(1, SEQ, WIDTH),
+        g_qkv,
+        g_out,
+        g_up,
+        g_down,
+        g_norm[:4, :CHUNK],
+        g_depth[4, : GROUP + 1],
+    )
+
+
+def fits(mesh, block_input, history, up_weight):
+    devices = ROWS * GROUP
+    return (
+        mesh.shape["rows"] == ROWS
+        and mesh.shape["depth"] == GROUP
+        and block_input.shape == (OWN * devices, WIDTH)
+        and history.shape[0] == GROUP
+        and up_weight.shape == (WIDTH, 4 * WIDTH)
+    )
+
 
 def solution(mesh):
-    return jax.shard_map(
-        local,
-        mesh=mesh,
-        in_specs=(
-            P(("rows", "depth"), None),
-            P("depth", "rows", None),
-            P(("rows", "depth"), None),
-            P(("rows", "depth")),
-            P(("rows", "depth"), None),
-            P(("rows", "depth"), None),
-            P(("rows", "depth"), None),
-            P(("rows", "depth"), None),
-            P(None, ("rows", "depth")),
-            P(),
-        ),
-        out_specs=(
-            P(("rows", "depth"), None),
-            P(("rows", "depth"), None),
-            P("depth", "rows", None),
-            P(("rows", "depth"), None),
-            P(("rows", "depth"), None),
-            P(("rows", "depth"), None),
-            P(("rows", "depth"), None),
-            P(None, ("rows", "depth")),
-            P(),
-        ),
-        check_vma=False,
-    )
+    weights = P(("rows", "depth"), None)
+    in_specs = (
+        weights,
+        P("depth", "rows", None),
+        weights,
+        P(("rows", "depth")),
+        weights,
+        weights,
+        weights,
+        weights,
+        P(None, ("rows", "depth")),
+        P(),
+    )
+    out_specs = (
+        weights,
+        weights,
+        P("depth", "rows", None),
+        weights,
+        weights,
+        weights,
+        weights,
+        P(None, ("rows", "depth")),
+        P(),
+    )
+
+    def run(*args):
+        body = fused if fits(mesh, args[0], args[1], args[6]) else local
+        return jax.shard_map(
+            body, mesh=mesh, in_specs=in_specs, out_specs=out_specs, check_vma=False
+        )(*args)
+
+    return run

time: 879 us -> 130 us (0.15)
  waiting for transfers between devices: 619 us -> 0 us
  blocking collectives: 151 us -> 0 us
  Pallas kernels: 0 us -> 119 us
  matrix products: 53.7 us -> 0 us
  other arithmetic: 15.2 us -> 0 us
  between operations: 15.4 us -> 0.67 us
  local copies, waits for them, and re-layouts: 22.7 us -> 10.2 us
    reduce_scatter x5 -> x0, waiting for transfers between devices: 465 us -> none  [the longest x1 142 us: local(): lax.psum_scatter(up_gradient, ('rows', 'depth'), scatter_dimension=0, til...]
    all_gather x4 -> x0, waiting for transfers between devices: 127 us -> none  [the longest x1 63.2 us: local(): lax.all_gather(up_weight, ('rows', 'depth'), axis=0, tiled=True)]
    pallas_call x0 -> x1, Pallas kernels: none -> 119 us  [fused(): pl.pallas_call(fused_kernel, out_shape=(shape((OWN, WIDTH), BF), shape((O...]
    all_gather x4 -> x0, blocking collectives: 69 us -> none  [the longest x1 40.6 us: local(): lax.all_gather(norm_params.astype(jnp.bfloat16), ('rows', 'depth'), axis=...]
    dot_general x18 -> x0, matrix products: 53.7 us -> none  [the longest x1 5.94 us: local(): jnp.dot(active.T, lower_grad, preferred_element_type=jnp.float32)]
    psum x1 -> x0, blocking collectives: 42.3 us -> none  [local(): total = lax.psum(jnp.sum(token_mask), ('rows', 'depth')).astype(jnp.float32)]
    unnamed x1 -> x0, blocking collectives: 39.6 us -> none
    unnamed x13 -> x0, waiting for transfers between devices: 27.1 us -> none
  transfers between devices with their start and end apart: 11 -> 0, of which waited for: 8 -> 0; matrix products, arithmetic and copies ran while one was open for 7% -> 0% of each run, Pallas kernels for 0% -> 0%
where the time goes in v1:
time: 130 us
  Pallas kernels  119 us (92%)
  local copies, waits for them, and re-layouts  10.2 us (8%)
    pallas_call x1, Pallas kernels, fused(): pl.pallas_call(fused_kernel, out_shape=(shape((OWN, WIDTH), BF), shape((O...  119 us
    unnamed x17, local copies, waits for them, and re-layouts  7.71 us

profile of v1, /device:TPU:0, one launch (start us, length us, event | category | flops | bytes accessed | tf_op | source)
XLA Modules:
  0.0 129.5 jit_solution(16249540090925459470)
XLA Ops:
  0.6 118.6 %shard_map.187 = (bf16[128,768]{1,0:T(8,128)(2,1)}, bf16[128,768]{1,0:T(8,128)(2,1)}, bf16[512,768]{1,0:T(8,128)(2,1)}, f32[24,2304]{1,0:T(8,128)}, f32[24,768]{...) custom-call(bf16[128,768]{1,0:T(8,128)(2,1)} %refs_0_.1, ...), custom_call_target="tpu_custom_call" | custom-call | flops 12000000000 | bytes 4000000 | tf_op jit(solution)/shard_map/pallas_call | solution.py:1134
  119.3 0.0 copy-start
  119.3 1.3 slice_bitcast_fusion
  120.6 1.2 slice.6
  121.8 1.6 %copy.28 = bf16[128,768]{1,0:T(8,128)(2,1)} copy(bf16[128,768]{1,0:T(8,128)(2,1)} %get-tuple-element.36) | data formatting | bytes 393216
  123.4 1.6 %copy.29 = bf16[128,768]{1,0:T(8,128)(2,1)} copy(bf16[128,768]{1,0:T(8,128)(2,1)} %get-tuple-element.37) | data formatting | bytes 393216
  125.1 0.0 copy-done
  125.1 0.0 copy-start.3
  125.1 0.9 copy.30
  125.9 0.3 copy-done.3
  126.2 0.0 copy-start.4
  126.2 0.0 copy-start.2
  126.2 0.7 copy.31
  126.9 0.2 copy-done.4
  127.1 0.6 copy.32
  127.8 0.0 copy-done.2
  127.8 0.0 copy-start.1
  127.8 0.7 copy.33
  128.5 0.4 copy-done.1
  128.8 0.7 copy.34
Async XLA Ops:
  119.3 5.8 %copy-start = (bf16[512,768]{1,0:T(8,128)(2,1)S(1)}, bf16[512,768]{1,0:T(8,128)(2,1)}, u32[]{:S(2)}) copy-start(bf16[512,768]{1,0:T(8,128)(2,1)} %get-tuple-element.20) | copy-start | bytes 2359300
  125.1 1.1 copy-start.3
  126.2 0.9 copy-start.4
  126.2 1.5 %copy-start.2 = (f32[24,3072]{1,0:T(8,128)S(1)}, f32[24,3072]{1,0:T(8,128)}, u32[]{:S(2)}) copy-start(f32[24,3072]{1,0:T(8,128)} %get-tuple-element.41) | copy-start | bytes 884740
  127.8 1.1 copy-start.1

commit v2 on v1

--- a/solution.py
+++ b/solution.py
@@ -428,6 +428,7 @@
     g_qkv=((WIDTH, PACK), F32),
     du=((SEQ, WIDTH), BF),
     part=((SEQ, WIDTH), F32),
+    part2=((SEQ, WIDTH), F32),
     dy=((OWN, WIDTH), F32),
     dyb=((GROUP, OWN, WIDTH), BF),
     dob=((SEQ, 384), BF),
@@ -441,8 +442,12 @@
     t1=((8, WIDTH), F32),
     tz=((4, 8, WIDTH), F32),
     td=((4, 8, WIDTH), F32),
-    a_qkv=((GROUP, CHUNK, PACK), F32),
-    a_up=((GROUP, CHUNK, WIDTH), F32),
+    a_qkv=((GROUP, 16, 1024), BF),
+    a_up=((GROUP, 16, 1152), BF),
+    b_qkv=((GROUP, 16, 1024), BF),
+    b_up=((GROUP, 16, 1152), BF),
+    gain_sum=((8, WIDTH), F32),
+    shift_sum=((8, WIDTH), F32),
 )
 for _name, _rows, _cols in (
     ("down", BLOCK, WIDTH),
@@ -452,8 +457,10 @@
 ):
     SCRATCH["xs_" + _name] = ((4, _rows, _cols), BF)
     SCRATCH["xl_" + _name] = ((4, _rows, _cols), BF)
-    SCRATCH["zs_" + _name] = ((3, _rows, _cols), BF)
+    SCRATCH["zs_" + _name] = ((2, _rows, _cols), BF)
     SCRATCH["zl_" + _name] = ((3, _rows, _cols), BF)
+    SCRATCH["ns_" + _name] = ((2, _rows, _cols), BF)
+    SCRATCH["nl_" + _name] = ((2, _rows, _cols), BF)
     SCRATCH["f_" + _name] = ((_rows, _cols), F32)
 for _name in ("mix", "mid", "in"):
     SCRATCH["s1_" + _name] = ((2, OWN, WIDTH), BF)
@@ -463,6 +470,7 @@
 N_SEMS = 160
 N_IN = 12
 N_OUT = 9
+VMEM_MIB = 60
 
 
 class Names:
@@ -482,25 +490,32 @@
     yy, c = lax.div(d, 2), lax.rem(d, 2)
     other_x, other_c, other_y = 1 - x, 1 - c, 1 - yy
     x_dev = (2 * z + other_x, d)
-    z_of = [lax.rem(z + k, 4) for k in range(4)]
-    z_dev = [(2 * zk + x, d) for zk in z_of]
+    z_two, z_mirror, z_near = lax.rem(z + 2, 4), 3 - z, z + 1 - 2 * lax.rem(z, 2)
+    two_dev, mirror_dev, near_dev = ((2 * zk + x, d) for zk in (z_two, z_mirror, z_near))
+    inside = lax.rem(z + 1, 4) >= 2
     core_d, y_d, far_d = 2 * yy + other_c, 2 * other_y + c, 2 * other_y + other_c
     core_dev, y_dev, far_dev = (r, core_d), (r, y_d), (r, far_d)
     mates = ((core_d, core_dev), (y_d, y_dev), (far_d, far_dev))
     counter = [0]
     sent = []
-
-    def copy_to(src, dst, device):
+    sent_inside = []
+    sent_outside = []
+
+    def prepare(src, dst, device, arrival=None):
         index = counter[0]
         counter[0] += 1
         copy = pltpu.make_async_remote_copy(
             src_ref=src,
             dst_ref=dst,
             send_sem=send_sems.at[index],
-            recv_sem=recv_sems.at[index],
+            recv_sem=recv_sems.at[index if arrival is None else arrival],
             device_id=device,
             device_id_type=MESH,
         )
+        return copy, index
+
+    def copy_to(src, dst, device):
+        copy, _ = prepare(src, dst, device)
         copy.start()
         sent.append(copy)
         return copy
@@ -516,24 +531,58 @@
         lax.fori_loop(0, count // step, one, 0)
 
     barrier = pltpu.get_barrier_semaphore()
-    for device in (x_dev, *z_dev[1:], core_dev, y_dev, far_dev):
+    for device in (x_dev, two_dev, mirror_dev, near_dev, core_dev, y_dev, far_dev):
         pl.semaphore_signal(barrier, inc=1, device_id=device, device_id_type=MESH)
     pl.semaphore_wait(barrier, 7)
 
     class Gather:
-        def __init__(self, piece):
-            self.piece = piece
-
-        def send(self):
+        def __init__(self, piece, cross=False):
+            self.piece, self.cross = piece, cross
+            self.along_x = []
+
+        def send_two(self):
             mine = self.piece(r)
-            self.along_z = [copy_to(mine, mine, z_dev[k]) for k in (1, 2, 3)]
-            self.along_x = [copy_to(mine, mine, x_dev)]
-
-        def forward(self):
-            for k in (1, 2, 3):
-                self.along_z[k - 1].wait_recv()
-                piece = self.piece(2 * z_of[4 - k] + x)
-                self.along_x.append(copy_to(piece, piece, x_dev))
+            self.two = copy_to(mine, mine, two_dev)
+
+        def send_mirror(self):
+            mine, passed = self.piece(r), self.piece(2 * z_two + x)
+            self.mirror, index = prepare(mine, mine, mirror_dev)
+            self.passing, _ = prepare(passed, passed, near_dev, index)
+            sent_inside.extend([self.mirror, self.passing])
+            pl.when(inside)(self.mirror.start)
+
+        def send_near(self, where=None):
+            if where is not False:
+                mine = self.piece(r)
+                self.near, _ = prepare(mine, mine, near_dev)
+                sent.append(self.near)
+            if where is None:
+                self.near.start()
+            else:
+                pl.when(jnp.logical_not(inside) if where else inside)(self.near.start)
+
+        def send_x(self, index=r):
+            piece = self.piece(index)
+            self.along_x.append(copy_to(piece, piece, x_dev))
+
+        def forward_near(self):
+            self.near.wait_recv()
+            if not self.cross:
+                self.send_x(2 * z_near + x)
+
+        def forward_cross(self):
+            self.along_x[0].wait_recv()
+            piece = self.piece(2 * z + other_x)
+            self.along_x[0] = copy_to(piece, piece, near_dev)
+
+        def forward_two(self):
+            self.two.wait_recv()
+            pl.when(inside)(self.passing.start)
+            self.send_x(2 * z_two + x)
+
+        def forward_mirror(self):
+            self.mirror.wait_recv()
+            self.send_x(2 * z_mirror + x)
 
         def finish(self):
             for copy in self.along_x:
@@ -558,49 +607,96 @@
             self.on.wait_recv()
 
     class RowSum:
-        def __init__(self, name, block, step):
-            self.xs, self.xl, self.zs, self.zl, self.total = (
-                getattr(s, p + name) for p in ("xs_", "xl_", "zs_", "zl_", "f_")
+        def __init__(self, name, block, step, cross):
+            self.xs, self.xl, self.zs, self.zl, self.ns, self.nl, self.total = (
+                getattr(s, p + name) for p in ("xs_", "xl_", "zs_", "zl_", "ns_", "nl_", "f_")
             )
-            self.block, self.step = block, step
+            self.block, self.step, self.cross = block, step, cross
             self.count = self.total.shape[0]
+            self.along_x = {}
+
+        def stage(self, target, index, *extras):
+            def one(at):
+                value = self.block(index, at)
+                for ref in extras:
+                    value = value + ref[at, :].astype(F32)
+                target[at, :] = value.astype(BF)
+
+            by_rows(self.count, self.step, one)
+
+        def send_x(self, name, zk, *extras):
+            self.stage(self.xs.at[zk], 2 * zk + other_x, *extras)
+            self.along_x[name] = copy_to(self.xs.at[zk], self.xl.at[zk], x_dev)
 
         def send(self):
-            self.along_x = []
-            for k in (2, 1, 3, 0):
-                zk = z_of[k]
-
-                def stage(at):
-                    self.xs[zk, at, :] = self.block(2 * zk + other_x, at).astype(BF)
-
-                by_rows(self.count, self.step, stage)
-                self.along_x.append(copy_to(self.xs.at[zk], self.xl.at[zk], x_dev))
-
-        def middle(self):
-            self.along_z = {}
-            for place, k in enumerate((2, 1, 3)):
-                self.along_x[place].wait_recv()
-                zk = z_of[k]
-
-                def stage(at):
-                    value = self.block(2 * zk + x, at) + self.xl[zk, at, :].astype(F32)
-                    self.zs[k - 1, at, :] = value.astype(BF)
-
-                by_rows(self.count, self.step, stage)
-                self.along_z[k] = copy_to(self.zs.at[k - 1], self.zl.at[k - 1], z_dev[k])
+            self.send_x("mirror", z_mirror)
+            if self.cross:
+                self.stage(self.ns.at[0], 2 * z_near + other_x)
+                self.crossing = copy_to(self.ns.at[0], self.nl.at[0], near_dev)
+            self.send_x("two", z_two)
+            if self.cross:
+                self.stage(self.ns.at[1], 2 * z_near + x)
+                self.near = copy_to(self.ns.at[1], self.nl.at[1], near_dev)
+            else:
+                self.send_x("near", z_near)
+                self.send_x("own", z)
+
+        def send_own(self):
+            self.crossing.wait_recv()
+            self.send_x("own", z, self.nl.at[0])
+
+        def send_mirror(self):
+            self.along_x["mirror"].wait_recv()
+            self.stage(self.zs.at[0], 2 * z_mirror + x, self.xl.at[z_mirror])
+            self.mirror, _ = prepare(self.zs.at[0], self.zl.at[0], mirror_dev)
+            self.passing, _ = prepare(self.zs.at[0], self.zl.at[2], near_dev)
+            sent_inside.append(self.mirror)
+            sent_outside.append(self.passing)
+            pl.when(inside)(self.mirror.start)
+            pl.when(jnp.logical_not(inside))(self.passing.start)
+
+        def send_two(self):
+            self.along_x["two"].wait_recv()
+
+            @pl.when(inside)
+            def _():
+                self.passing.wait_recv()
+                self.stage(self.zs.at[1], 2 * z_two + x, self.xl.at[z_two], self.zl.at[2])
+
+            @pl.when(jnp.logical_not(inside))
+            def _():
+                self.stage(self.zs.at[1], 2 * z_two + x, self.xl.at[z_two])
+
+            self.two = copy_to(self.zs.at[1], self.zl.at[1], two_dev)
+
+        def send_near(self):
+            self.along_x["near"].wait_recv()
+            self.stage(self.ns.at[1], 2 * z_near + x, self.xl.at[z_near])
+            self.near = copy_to(self.ns.at[1], self.nl.at[1], near_dev)
 
         def finish(self):
-            self.along_x[3].wait_recv()
-            for k in (1, 2, 3):
-                self.along_z[k].wait_recv()
-
-            def stage(at):
-                value = self.block(r, at) + self.xl[z, at, :].astype(F32)
-                for k in range(3):
-                    value = value + self.zl[k, at, :].astype(F32)
-                self.total[at, :] = value
-
-            by_rows(self.count, self.step, stage)
+            self.along_x["own"].wait_recv()
+            self.two.wait_recv()
+            self.near.wait_recv()
+
+            def add(at):
+                self.total[at, :] = (
+                    self.block(r, at)
+                    + self.xl[z, at, :].astype(F32)
+                    + self.zl[1, at, :].astype(F32)
+                    + self.nl[1, at, :].astype(F32)
+                )
+
+            by_rows(self.count, self.step, add)
+
+            @pl.when(inside)
+            def _():
+                self.mirror.wait_recv()
+
+                def add_mirror(at):
+                    self.total[at, :] += self.zl[0, at, :].astype(F32)
+
+                by_rows(self.count, self.step, add_mirror)
 
     class GroupSum:
         def __init__(self, name, source):
@@ -646,7 +742,10 @@
     out_gather = Gather(lambda i: s.wo_l.at[d, i])
     for t, tile in enumerate(fold(tiles_of(wo[...].astype(F32)))):
         s.wo_l[d, r, :, 128 * t : 128 * (t + 1)] = tile.astype(BF)
-    out_gather.send()
+    out_gather.send_two()
+    out_gather.send_mirror()
+    out_gather.send_near()
+    out_gather.send_x()
 
     lane = lane_id((CHUNK, 128))
     eye = row_id((CHUNK, CHUNK)) == lane_id((CHUNK, CHUNK))
@@ -669,10 +768,6 @@
     qp_copies = [copy_to(s.qp_s.at[m], s.qp_l.at[d], device) for m, device in mates]
     s.qp_l[d] = s.qp_s[d]
 
-    s.x_all[d] = x_in[...]
-    x_gather = GroupGather(lambda i: s.x_all.at[i])
-    x_gather.send()
-
     wu_tiles = tiles_of(wu[...].astype(F32))
     for k in range(GROUP):
         for t, tile in enumerate(fold(permute_chunks(wu_tiles, up_picks(k)))):
@@ -680,14 +775,25 @@
     up_copies = [copy_to(s.up_s.at[m], s.up_l.at[d], device) for m, device in mates]
     s.up_l[d] = s.up_s[d]
 
+    rows_at(s.w_down, r, BLOCK)[...] = wd[...]
+    downs = [
+        Gather(lambda i, h=h: rows_at(s.w_down, 2 * i + h, BLOCK // 2), cross=True) for h in range(2)
+    ]
+    downs[0].send_two()
+    downs[0].send_near(True)
+    for half in downs:
+        half.send_x()
+
+    s.x_all[d] = x_in[...]
+    x_gather = GroupGather(lambda i: s.x_all.at[i])
+    x_gather.send()
+
     diagonal = jnp.where(
         row_id((OWN, OWN)) == lane_id((OWN, OWN)), jnp.broadcast_to(mask_row, (OWN, OWN)), 0.0
     )
     s.c_all[d] = dot(diagonal.astype(BF), cot[...]).astype(BF)
     c_gather = GroupGather(lambda i: s.c_all.at[i])
     c_gather.send()
-
-    rows_at(s.w_down, r, BLOCK)[...] = wd[...]
 
     def assemble(landing, count, target):
         for k in range(GROUP):
@@ -699,33 +805,54 @@
     for copy in qp_copies:
         copy.wait_recv()
     assemble(s.qp_l, 5, s.w_qkv)
-    qkv_gather = Gather(lambda i: rows_at(s.w_qkv, i, BLOCK))
-    qkv_gather.send()
+    halves = [Gather(lambda i, h=h: rows_at(s.w_qkv, 2 * i + h, BLOCK // 2)) for h in range(2)]
+    for half in halves:
+        half.send_two()
+    for half in halves:
+        half.send_near()
+        half.send_x()
+    for half in halves:
+        half.send_mirror()
+    out_gather.forward_two()
+    out_gather.forward_near()
     for copy in up_copies:
         copy.wait_recv()
     assemble(s.up_l, 6, s.w_up)
     up_gather = Gather(lambda i: rows_at(s.w_up, i, BLOCK))
-    up_gather.send()
-    down_gather = Gather(lambda i: rows_at(s.w_down, i, BLOCK))
-    down_gather.send()
-
+    up_gather.send_two()
+    up_gather.send_near(True)
+    up_gather.send_x()
     x_gather.relay()
-    c_gather.relay()
-    out_gather.forward()
+    halves[0].forward_near()
+    halves[0].forward_two()
+    out_gather.forward_mirror()
+    halves[1].forward_near()
     x_gather.finish()
 
-    for i in range(GROUP):
-
-        def normalize(at, i=i):
+    def normalize(i):
+        def one(at):
             normal, _ = standardize(s.x_all[i, at, :].astype(F32))
             s.normal[pl.ds(pl.multiple_of(OWN * i + at.start, at.size), at.size), :] = normal
 
-        by_rows(OWN, 64, normalize)
-    qkv_gather.forward()
+        by_rows(OWN, 64, one)
+
+    normalize(0)
+    halves[1].forward_two()
+    up_gather.send_near(False)
+    up_gather.send_mirror()
+    downs[1].send_two()
+    downs[1].send_near(True)
+    normalize(1)
+    halves[0].forward_mirror()
+    normalize(2)
+    normalize(3)
     out_gather.finish()
     slab_gather = GroupGather(lambda i: s.wo_l.at[i])
     slab_gather.send()
-    qkv_gather.finish()
+    halves[1].forward_mirror()
+    c_gather.relay()
+    for half in halves:
+        half.finish()
 
     lane = lane_id((8, 128))
     row = row_id((8, 128))
@@ -752,22 +879,8 @@
             target[at, 128:] = (b * co + a * si).astype(BF)
         s.v01[at, :] = value[:, 512:].astype(BF)
 
+    up_gather.forward_near()
     by_rows(SEQ, 256, project)
-    slab_gather.relay()
-    c_gather.finish()
-
-    s.terms[...] = jnp.zeros((8, WIDTH), F32)
-    for i in range(GROUP):
-
-        def loss_rows(at, i=i):
-            here = pl.ds(pl.multiple_of(OWN * i + at.start, at.size), at.size)
-            grad = s.c_all[i, at, :].astype(F32) * loss_scale
-            s.dm[here, :] = (last_weight * grad).astype(BF)
-            hg_o[here, :] = (own_weight * grad).astype(BF)
-            s.terms[...] += sublane_sum(grad * hist[here, :].astype(F32))
-
-        by_rows(OWN, 32, loss_rows)
-    up_gather.forward()
 
     lane2 = lax.div(lax.rem(lane_id((1, 256)), 128), jnp.int32(32))
     head_mask = [jnp.where(lane2 == h, 1.0, 0.0).astype(BF) for h in range(3)]
@@ -775,8 +888,9 @@
     half_id = lax.div(lane_id((1, 128)), jnp.int32(64))
     half_mask = [jnp.where(half_id == h, 1.0, 0.0).astype(BF) for h in range(2)]
     root = HD**-0.5
-    o_gathers = []
-    for b in range(2):
+    o_gathers = [GroupGather(lambda i, b=b: s.o_l.at[i, b]) for b in range(2)]
+
+    def attend(b):
         rows = slice(QBLOCK * b, QBLOCK * (b + 1))
         keys = QBLOCK * (b + 1)
         query = s.qv[rows, :]
@@ -793,6 +907,13 @@
                 first = first + dot(probs.astype(BF), s.v01[:keys, :] * half_mask[h])
             else:
                 third = dot(probs.astype(BF), s.qv[:keys, :])
+            if b == 1 and h == 0:
+                up_gather.forward_two()
+                for half in downs:
+                    half.send_near(False)
+                    half.send_mirror()
+            if b == 1 and h == 1:
+                downs[0].forward_two()
         s.o_l[d, b, :QBLOCK, :] = first.astype(BF)
         lane = lane_id((QBLOCK, 128))
         third = jnp.where(
@@ -801,17 +922,21 @@
         lane = lane_id((OWN, 128))
         third = jnp.where(lane < 64, third[:OWN], pltpu.roll(third[OWN:], 64, 1))
         s.o_l[d, b, QBLOCK:, :] = third.astype(BF)
-        o_gathers.append(GroupGather(lambda i, b=b: s.o_l.at[i, b]))
         o_gathers[b].send()
-        if b == 0:
-            slab_gather.finish()
-            for k in range(GROUP):
-                for i in range(ROWS):
-                    tiles = [t.astype(F32) for t in tiles_of(s.wo_l[k, i])]
-                    at = CHUNK * (GROUP * i + k)
-                    for t, tile in enumerate(unfold(tiles, 6)):
-                        s.g_out[at : at + CHUNK, 128 * t : 128 * (t + 1)] = tile
-    down_gather.forward()
+
+    attend(1)
+    slab_gather.relay()
+    attend(0)
+    for half in downs:
+        half.forward_cross()
+    up_gather.forward_mirror()
+    slab_gather.finish()
+    for k in range(GROUP):
+        for i in range(ROWS):
+            tiles = [t.astype(F32) for t in tiles_of(s.wo_l[k, i])]
+            at = CHUNK * (GROUP * i + k)
+            for t, tile in enumerate(unfold(tiles, 6)):
+                s.g_out[at : at + CHUNK, 128 * t : 128 * (t + 1)] = tile
 
     def out_place(head):
         k, h = divmod(head, 3)
@@ -825,9 +950,26 @@
     s.w_own[96:128, :] = third_rows[:32, :]
     s.w_own[224:256, :] = third_rows[32:, :]
     s.w_own[256:, :] = rows_at(s.w_out.at[pl.ds(0, 512)], d, 128)[...]
-
-    for b in range(2):
-        o_gathers[b].relay()
+    o_gathers[1].relay()
+    c_gather.finish()
+
+    s.terms[...] = jnp.zeros((8, WIDTH), F32)
+    for i in range(GROUP):
+
+        def loss_rows(at, i=i):
+            here = pl.ds(pl.multiple_of(OWN * i + at.start, at.size), at.size)
+            grad = s.c_all[i, at, :].astype(F32) * loss_scale
+            s.dm[here, :] = (last_weight * grad).astype(BF)
+            hg_o[here, :] = (own_weight * grad).astype(BF)
+            s.terms[...] += sublane_sum(grad * hist[here, :].astype(F32))
+
+        by_rows(OWN, 32, loss_rows)
+
+    downs[1].forward_two()
+    for b in (1, 0):
+        if b == 0:
+            o_gathers[0].relay()
+            downs[0].forward_mirror()
         o_gathers[b].finish()
         rows = slice(QBLOCK * b, QBLOCK * (b + 1))
         thirds = []
@@ -862,15 +1004,21 @@
 
     by_rows(SEQ, 256, widen)
 
+    rate = 0.7978845608028654
+
     def gate(at):
         u = s.part[at, :]
-        rate = 0.7978845608028654
         bend = jnp.tanh(rate * (u + 0.044715 * u * u * u))
         s.act[at, :] = (0.5 * u * (1.0 + bend)).astype(BF)
+        s.slope[at, :] = bend
+
+    by_rows(SEQ, 32, gate)
+    downs[1].forward_mirror()
+
+    def gate_slope(at):
+        u, bend = s.part[at, :], s.slope[at, :]
         inner = rate * (1.0 + 3 * 0.044715 * u * u)
         s.slope[at, :] = 0.5 * (1.0 + bend) + 0.5 * u * (1.0 - bend * bend) * inner
-
-    by_rows(SEQ, 32, gate)
 
     def block_of(ref):
         def block(index, at):
@@ -881,10 +1029,12 @@
     for i in range(3):
         cols = slice(QBLOCK * i, QBLOCK * (i + 1))
         s.g_down[cols, :] = dot(s.act[:, cols], s.dm[...], 0, 0)
-    down_sum = RowSum("down", block_of(s.g_down), 16)
+    down_sum = RowSum("down", block_of(s.g_down), 16, True)
     down_sum.send()
-
-    down_gather.finish()
+    by_rows(SEQ, 32, gate_slope)
+    for half in downs:
+        half.forward_near()
+        half.finish()
 
     def narrow(at):
         value = dot(s.dm[at, :], s.w_down[...], 1, 1)
@@ -898,17 +1048,35 @@
     by_rows(SEQ, 256, second_back)
     mid_sum = GroupSum("mid", s.part)
     mid_sum.send()
-    down_sum.middle()
 
     for i in range(3):
         cols = slice(QBLOCK * i, QBLOCK * (i + 1))
         s.g_up[cols, :] = dot(s.h2[:, cols], s.du[...], 0, 0)
-    up_sum = RowSum("up", block_of(s.g_up), 16)
+    up_sum = RowSum("up", block_of(s.g_up), 16, True)
+    mid_sum.middle()
     up_sum.send()
-    mid_sum.middle()
+    down_sum.send_own()
+
+    def block_out(at):
+        value = dot(s.act[at, :], s.w_down[...])
+        s.part2[at, :] = value
+
+    s.terms2[...] = jnp.zeros((8, WIDTH), F32)
+    by_rows(SEQ, 256, block_out)
+    for i in range(GROUP):
+
+        def mix(at, i=i):
+            here = pl.ds(pl.multiple_of(OWN * i + at.start, at.size), at.size)
+            value = s.part2[here, :]
+            loss = s.c_all[i, at, :].astype(F32) * loss_scale
+            s.terms2[...] += sublane_sum(loss * value)
+            s.part2[here, :] = own_weight * hist[here, :].astype(F32) + last_weight * value
+
+        by_rows(OWN, 32, mix)
+    mix_sum = GroupSum("mix", s.part2)
+    mix_sum.send()
     mid_sum.wait()
 
-    s.terms2[...] = jnp.zeros((8, WIDTH), F32)
     s.t0[...] = jnp.zeros((8, WIDTH), F32)
 
     def second_norm_back(at):
@@ -928,26 +1096,11 @@
     dy_gather = GroupGather(lambda i: s.dyb.at[i])
     dy_gather.send()
 
-    def block_out(at):
-        value = dot(s.act[at, :], s.w_down[...])
-        s.part[at, :] = value
-
-    by_rows(SEQ, 256, block_out)
-    for i in range(GROUP):
-
-        def mix(at, i=i):
-            here = pl.ds(pl.multiple_of(OWN * i + at.start, at.size), at.size)
-            value = s.part[here, :]
-            loss = s.c_all[i, at, :].astype(F32) * loss_scale
-            s.terms2[...] += sublane_sum(loss * value)
-            s.part[here, :] = own_weight * hist[here, :].astype(F32) + last_weight * value
-
-        by_rows(OWN, 32, mix)
-    mix_sum = GroupSum("mix", s.part)
-    mix_sum.send()
-    up_sum.middle()
+    mix_sum.middle()
+    down_sum.send_mirror()
+    up_sum.send_own()
     dy_gather.relay()
-    mix_sum.middle()
+    down_sum.send_two()
     dy_gather.finish()
 
     by_group = s.dyb[...].reshape(SEQ, WIDTH)
@@ -967,7 +1120,7 @@
         tiles = tiles_of(s.g_out[pl.ds(start, CHUNK), :])
         return jnp.concatenate(fold(tiles), axis=1)
 
-    out_sum = RowSum("out", out_block, 16)
+    out_sum = RowSum("out", out_block, 16, False)
     out_sum.send()
     mix_sum.wait()
 
@@ -976,6 +1129,7 @@
         out_o[at, :] = (mix_sum.value(at) + last_weight * s.y[here, :]).astype(BF)
 
     by_rows(OWN, 32, write_out)
+    up_sum.send_mirror()
 
     for b in range(2):
         rows = slice(QBLOCK * b, QBLOCK * (b + 1))
@@ -1034,7 +1188,7 @@
     for i in range(3):
         cols = slice(QBLOCK * i, QBLOCK * (i + 1))
         s.g_qkv[cols, :] = dot(s.h1[:, cols], s.dqkv[...], 0, 0)
-    qkv_sum = RowSum("qkv", block_of(s.g_qkv), 16)
+    qkv_sum = RowSum("qkv", block_of(s.g_qkv), 16, True)
     qkv_sum.send()
 
     def first_back(at):
@@ -1043,22 +1197,61 @@
     by_rows(SEQ, 256, first_back)
     in_sum = GroupSum("in", s.part)
     in_sum.send()
-    out_sum.middle()
+    s.gain_sum[...] = jnp.zeros((8, WIDTH), F32)
+    s.shift_sum[...] = jnp.zeros((8, WIDTH), F32)
+
+    def first_norm_sums(at):
+        grad = s.part[at, :]
+        s.gain_sum[...] += sublane_sum(grad * s.normal[at, :])
+        s.shift_sum[...] += sublane_sum(grad)
+
+    by_rows(SEQ, 32, first_norm_sums)
     in_sum.middle()
-
-    def spread(total, landing):
-        copies = [
-            copy_to(total.at[pl.ds(pl.multiple_of(CHUNK * m, CHUNK), CHUNK)], landing.at[d], device)
-            for m, device in mates
-        ]
-        landing[d] = total[pl.ds(pl.multiple_of(CHUNK * d, CHUNK), CHUNK), :]
+    s.t0[0:1, :] = jnp.sum(s.gain_sum[...], axis=0, keepdims=True)
+    s.t0[1:2, :] = jnp.sum(s.shift_sum[...], axis=0, keepdims=True)
+    lane = lane_id((1, WIDTH))
+    own_term = jnp.sum(jnp.sum(s.terms[...], axis=0, keepdims=True), axis=1, keepdims=True)
+    last_term = jnp.sum(jnp.sum(s.terms2[...], axis=0, keepdims=True), axis=1, keepdims=True)
+    s.t0[4:5, :] = jnp.where(lane == d, own_term, jnp.where(lane == GROUP, last_term, 0.0))
+    small = copy_to(s.t0, s.t1, x_dev)
+    up_sum.send_two()
+    out_sum.send_mirror()
+    qkv_sum.send_own()
+    out_sum.send_near()
+    out_sum.send_two()
+
+    def spread(total, staged, landing):
+        copies = []
+        for m, device in mates:
+            rows = total[pl.ds(pl.multiple_of(CHUNK * m, CHUNK), CHUNK), :]
+            for t, tile in enumerate(fold(tiles_of(rows))):
+                staged[m, :, 128 * t : 128 * (t + 1)] = tile.astype(BF)
+            copies.append(copy_to(staged.at[m], landing.at[d], device))
+        rows = total[pl.ds(pl.multiple_of(CHUNK * d, CHUNK), CHUNK), :]
+        for t, tile in enumerate(fold(tiles_of(rows))):
+            landing[d, :, 128 * t : 128 * (t + 1)] = tile.astype(BF)
         return copies
 
+    def collect(copies, landing, count, back, target):
+        for copy in copies:
+            copy.wait_recv()
+        tiles = []
+        for k in range(GROUP):
+            tiles += unfold([t.astype(F32) for t in tiles_of(landing[k])], count)
+        for t, tile in enumerate(permute_chunks(tiles, back)):
+            target[:, 128 * t : 128 * (t + 1)] = tile
+
+    qkv_sum.send_mirror()
+    small.wait_recv()
+    s.tz[z] = s.t0[...] + s.t1[...]
+    small_z = [
+        copy_to(s.tz.at[z], s.tz.at[z], device) for device in (two_dev, mirror_dev, near_dev)
+    ]
+    qkv_sum.send_two()
     down_sum.finish()
     gd_o[...] = s.f_down[...]
     up_sum.finish()
-    up_spread = spread(s.f_up, s.a_up)
-    qkv_sum.middle()
+    up_spread = spread(s.f_up, s.b_up, s.a_up)
     in_sum.wait()
 
     def first_norm_back(at):
@@ -1066,34 +1259,16 @@
         normal, scale = standardize(x_in[at, :].astype(F32))
         back = norm_back(grad, s.norms[0:1, :], normal, scale)
         ig_o[at, :] = (s.dy[at, :] + back).astype(BF)
-        s.t0[0:1, :] += jnp.sum(grad * normal, axis=0, keepdims=True)
-        s.t0[1:2, :] += jnp.sum(grad, axis=0, keepdims=True)
 
     by_rows(OWN, 32, first_norm_back)
-
-    lane = lane_id((1, WIDTH))
-    own_term = jnp.sum(jnp.sum(s.terms[...], axis=0, keepdims=True), axis=1, keepdims=True)
-    last_term = jnp.sum(jnp.sum(s.terms2[...], axis=0, keepdims=True), axis=1, keepdims=True)
-    s.t0[4:5, :] = jnp.where(lane == d, own_term, jnp.where(lane == GROUP, last_term, 0.0))
-    small = copy_to(s.t0, s.t1, x_dev)
-    out_sum.finish()
-    for t, tile in enumerate(unfold(tiles_of(s.f_out[...]), 6)):
-        go_o[:, 128 * t : 128 * (t + 1)] = tile
-    small.wait_recv()
-    s.tz[z] = s.t0[...] + s.t1[...]
-    small_z = [copy_to(s.tz.at[z], s.tz.at[z], z_dev[k]) for k in (1, 2, 3)]
-    for copy in up_spread:
-        copy.wait_recv()
-    tiles = [t for k in range(GROUP) for t in tiles_of(s.a_up[k])]
-    for t, tile in enumerate(permute_chunks(tiles, UP_BACK)):
-        gu_o[:, 128 * t : 128 * (t + 1)] = tile
     for copy in small_z:
         copy.wait_recv()
     s.td[d] = (s.tz[0] + s.tz[1]) + (s.tz[2] + s.tz[3])
     small_d = [copy_to(s.td.at[d], s.td.at[d], device) for m, device in mates]
-
-    qkv_sum.finish()
-    qkv_spread = spread(s.f_qkv, s.a_qkv)
+    out_sum.finish()
+    for t, tile in enumerate(unfold(tiles_of(s.f_out[...]), 6)):
+        go_o[:, 128 * t : 128 * (t + 1)] = tile
+    collect(up_spread, s.a_up, 6, UP_BACK, gu_o)
     for copy in small_d:
         copy.wait_recv()
     value = (s.td[0] + s.td[1]) + (s.td[2] + s.td[3])
@@ -1106,13 +1281,41 @@
         preferred_element_type=F32,
         precision=lax.Precision.HIGHEST,
     )
-    for copy in qkv_spread:
-        copy.wait_recv()
-    tiles = [t for k in range(GROUP) for t in tiles_of(s.a_qkv[k])]
-    for t, tile in enumerate(permute_chunks(tiles, QKV_BACK)):
-        gq_o[:, 128 * t : 128 * (t + 1)] = tile
+    qkv_sum.finish()
+    qkv_spread = spread(s.f_qkv, s.b_qkv, s.a_qkv)
+    collect(qkv_spread, s.a_qkv, 5, QKV_BACK, gq_o)
     for copy in sent:
         copy.wait_send()
+
+    @pl.when(inside)
+    def _():
+        for copy in sent_inside:
+            copy.wait_send()
+
+    @pl.when(jnp.logical_not(inside))
+    def _():
+        for copy in sent_outside:
+            copy.wait_send()
+
+
+def finish_kernel(*refs):
+    count = N_OUT - 2
+    ins, refs = refs[:count], refs[count:]
+    (norm, depth), refs = refs[:2], refs[2:]
+    outs, (norm_o, depth_o), refs = refs[:count], refs[count : count + 2], refs[count + 2 :]
+    held, sems = refs[:-1], refs[-1]
+    first = [pltpu.make_async_copy(a, b, sems.at[i]) for i, (a, b) in enumerate(zip(ins, held))]
+    for copy in first:
+        copy.start()
+    norm_o[...] = norm[:4, :CHUNK]
+    depth_o[...] = depth[4:5, : GROUP + 1]
+    second = []
+    for i, copy in enumerate(first):
+        copy.wait()
+        second.append(pltpu.make_async_copy(held[i], outs[i], sems.at[count + i]))
+        second[i].start()
+    for copy in second:
+        copy.wait()
 
 
 def fused(
@@ -1130,26 +1333,28 @@
     cosine, sine = tables()
     vmem = pl.BlockSpec(memory_space=pltpu.VMEM)
     smem = pl.BlockSpec(memory_space=pltpu.SMEM)
+    anywhere = pl.BlockSpec(memory_space=pl.ANY)
     shape = jax.ShapeDtypeStruct
+    shapes = (
+        shape((OWN, WIDTH), BF),
+        shape((OWN, WIDTH), BF),
+        shape((SEQ, WIDTH), BF),
+        shape((CHUNK, 3 * WIDTH), F32),
+        shape((CHUNK, WIDTH), F32),
+        shape((CHUNK, 4 * WIDTH), F32),
+        shape((BLOCK, WIDTH), F32),
+        shape((8, 128), F32),
+        shape((8, 128), F32),
+    )
     outs = pl.pallas_call(
         fused_kernel,
-        out_shape=(
-            shape((OWN, WIDTH), BF),
-            shape((OWN, WIDTH), BF),
-            shape((SEQ, WIDTH), BF),
-            shape((CHUNK, 3 * WIDTH), F32),
-            shape((CHUNK, WIDTH), F32),
-            shape((CHUNK, 4 * WIDTH), F32),
-            shape((BLOCK, WIDTH), F32),
-            shape((8, 128), F32),
-            shape((8, 128), F32),
-        ),
+        out_shape=shapes,
         in_specs=[vmem] * 9 + [smem] + [vmem] * 2,
         out_specs=[vmem] * 9,
         scratch_shapes=[pltpu.VMEM(dims, kind) for dims, kind in SCRATCH.values()]
         + [pltpu.SemaphoreType.DMA((N_SEMS,))] * 2,
         compiler_params=pltpu.CompilerParams(
-            collective_id=0, has_side_effects=True, vmem_limit_bytes=62 * 2**20
+            collective_id=0, has_side_effects=True, vmem_limit_bytes=VMEM_MIB * 2**20
         ),
         cost_estimate=pl.CostEstimate(flops=12 * 10**9, bytes_accessed=4 * 10**6, transcendentals=10**6),
     )(
@@ -1166,18 +1371,17 @@
         jnp.asarray(cosine),
         jnp.asarray(sine),
     )
-    out, input_grad, history_grad, g_qkv, g_out, g_up, g_down, g_norm, g_depth = outs
-    return (
-        out,
-        input_grad,
-        history_grad.reshape(1, SEQ, WIDTH),
-        g_qkv,
-        g_out,
-        g_up,
-        g_down,
-        g_norm[:4, :CHUNK],
-        g_depth[4, : GROUP + 1],
-    )
+    held = pl.pallas_call(
+        finish_kernel,
+        out_shape=shapes[:7] + (shape((4, CHUNK), F32), shape((1, GROUP + 1), F32)),
+        in_specs=[anywhere] * 7 + [vmem] * 2,
+        out_specs=[anywhere] * 7 + [vmem] * 2,
+        scratch_shapes=[pltpu.VMEM(one.shape, one.dtype) for one in shapes[:7]]
+        + [pltpu.SemaphoreType.DMA((14,))],
+        compiler_params=pltpu.CompilerParams(vmem_limit_bytes=VMEM_MIB * 2**20),
+    )(*outs)
+    out, input_grad, history_grad, *grads, g_depth = held
+    return (out, input_grad, history_grad.reshape(1, SEQ, WIDTH), *grads, g_depth.reshape(GROUP + 1))
 
 
 def fits(mesh, block_input, history, up_weight):

time: 130 us -> 114 us (0.88)
  local copies, waits for them, and re-layouts: 10.2 us -> 0 us
  Pallas kernels: 119 us -> 113 us
    unnamed x17 -> x0, local copies, waits for them, and re-layouts: 7.71 us -> none
    pallas_call x1 -> x2, Pallas kernels: 119 us -> 113 us  [the longest x1 109 us: fused(): pl.pallas_call(fused_kernel, out_shape=shapes, in_specs=[vmem] * 9 + [sme...]
where the time goes in v2:
time: 114 us; the launch traced here: 113 us
  Pallas kernels  113 us (99%)
    pallas_call x1, Pallas kernels, fused(): pl.pallas_call(fused_kernel, out_shape=shapes, in_specs=[vmem] * 9 + [sme...  109 us
    pallas_call x1, Pallas kernels, fused(): pl.pallas_call(finish_kernel, out_shape=shapes[:7] + (shape((4, CHUNK), F...  3.9 us

profile of v2, /device:TPU:0, one launch (start us, length us, event | category | flops | bytes accessed | tf_op | source)
XLA Modules:
  0.0 113.4 jit_solution(6739295074709850719)
XLA Ops:
  0.6 108.7 %shard_map.187 = (bf16[128,768]{1,0:T(8,128)(2,1)}, bf16[128,768]{1,0:T(8,128)(2,1)}, bf16[512,768]{1,0:T(8,128)(2,1)}, f32[24,2304]{1,0:T(8,128)}, f32[24,768]{...) custom-call(bf16[128,768]{1,0:T(8,128)(2,1)} %refs_0_.1, ...), custom_call_target="tpu_custom_call" | custom-call | flops 12000000000 | bytes 4000000 | tf_op jit(solution)/shard_map/pallas_call | solution.py:1349
  109.3 3.9 %shard_map.188 = (bf16[128,768]{1,0:T(8,128)(2,1)}, bf16[128,768]{1,0:T(8,128)(2,1)}, bf16[512,768]{1,0:T(8,128)(2,1)}, f32[24,2304]{1,0:T(8,128)}, f32[24,768]{...) custom-call(bf16[128,768]{1,0:T(8,128)(2,1)} %get-tuple-element.27.refs_0_, ...), custom_call_target="tpu_custom_call" | custom-call | tf_op jit(solution)/shard_map/pallas_call | solution.py:1374

commit v3 on v2

--- a/solution.py
+++ b/solution.py
@@ -395,17 +395,31 @@
 
 
 SCRATCH = dict(
+    hist=((SEQ, WIDTH), BF),
+    cot=((OWN, WIDTH), BF),
+    wq=((CHUNK, 3 * WIDTH), BF),
+    wo=((CHUNK, WIDTH), BF),
+    wu=((CHUNK, 4 * WIDTH), BF),
+    cosine=((SEQ, 128), F32),
+    sine=((SEQ, 128), F32),
+    r_0=((OWN, WIDTH), BF),
+    r_1=((OWN, WIDTH), BF),
+    r_2=((SEQ, WIDTH), BF),
+    r_3=((CHUNK, 3 * WIDTH), F32),
+    r_4=((CHUNK, WIDTH), F32),
+    r_5=((CHUNK, 4 * WIDTH), F32),
+    r_6=((BLOCK, WIDTH), F32),
     x_all=((GROUP, OWN, WIDTH), BF),
     c_all=((GROUP, OWN, WIDTH), BF),
     qp_s=((GROUP, 16, 1024), BF),
-    qp_l=((GROUP, 16, 1024), BF),
+    q_all=((ROWS, GROUP, 16, 1024), BF),
     up_s=((GROUP, 16, 1152), BF),
     up_l=((GROUP, 16, 1152), BF),
     tmp=((BLOCK, WIDTH), F32),
     w_qkv=((WIDTH, PACK), BF),
     w_up=((WIDTH, WIDTH), BF),
     w_down=((WIDTH, WIDTH), BF),
-    wo_l=((GROUP, ROWS, 16, 1152), BF),
+    wo_l=((GROUP, 2, ROWS // 2, 16, 1152), BF),
     w_out=((WIDTH, WIDTH), BF),
     w_own=((384, WIDTH), BF),
     norms=((8, WIDTH), F32),
@@ -439,12 +453,18 @@
     terms=((8, WIDTH), F32),
     terms2=((8, WIDTH), F32),
     t0=((8, WIDTH), F32),
-    t1=((8, WIDTH), F32),
-    tz=((4, 8, WIDTH), F32),
     td=((4, 8, WIDTH), F32),
-    a_qkv=((GROUP, 16, 1024), BF),
+    ext=((ROWS, 16, 128), F32),
+    u0=((8, 128), F32),
+    u1=((8, 128), F32),
+    uz=((4, 8, 128), F32),
+    ud=((4, 8, 128), F32),
+    fin=((4, GROUP, 16, 1024), BF),
+    q_sum=((GROUP, 16, 1024), F32),
     a_up=((GROUP, 16, 1152), BF),
-    b_qkv=((GROUP, 16, 1024), BF),
+    f_down=((BLOCK, WIDTH), F32),
+    f_up=((BLOCK, WIDTH), F32),
+    f_out=((16, 1280), F32),
     b_up=((GROUP, 16, 1152), BF),
     gain_sum=((8, WIDTH), F32),
     shift_sum=((8, WIDTH), F32),
@@ -452,8 +472,7 @@
 for _name, _rows, _cols in (
     ("down", BLOCK, WIDTH),
     ("up", BLOCK, WIDTH),
-    ("out", 16, 1152),
-    ("qkv", BLOCK, PACK),
+    ("out", 16, 1280),
 ):
     SCRATCH["xs_" + _name] = ((4, _rows, _cols), BF)
     SCRATCH["xl_" + _name] = ((4, _rows, _cols), BF)
@@ -461,13 +480,18 @@
     SCRATCH["zl_" + _name] = ((3, _rows, _cols), BF)
     SCRATCH["ns_" + _name] = ((2, _rows, _cols), BF)
     SCRATCH["nl_" + _name] = ((2, _rows, _cols), BF)
-    SCRATCH["f_" + _name] = ((_rows, _cols), F32)
+for _h in range(2):
+    for _name in ("xs", "xl"):
+        SCRATCH[f"{_name}_qkv{_h}"] = ((4, BLOCK // 2, PACK), BF)
+    for _name in ("cs", "cl", "zs", "zl"):
+        SCRATCH[f"{_name}_qkv{_h}"] = ((BLOCK // 2, PACK), BF)
+    SCRATCH[f"ps_qkv{_h}"] = ((4, 2, 16, 1024), BF)
 for _name in ("mix", "mid", "in"):
     SCRATCH["s1_" + _name] = ((2, OWN, WIDTH), BF)
     SCRATCH["l1_" + _name] = ((2, OWN, WIDTH), BF)
     SCRATCH["s2_" + _name] = ((OWN, WIDTH), BF)
     SCRATCH["l2_" + _name] = ((OWN, WIDTH), BF)
-N_SEMS = 160
+N_SEMS = 224
 N_IN = 12
 N_OUT = 9
 VMEM_MIB = 60
@@ -478,12 +502,13 @@
 
 
 def fused_kernel(*refs):
-    (x_in, hist, cot, mask, wq, wo, wu, wd, nrm, dw, cosine, sine) = refs[:N_IN]
-    (out_o, ig_o, hg_o, gq_o, go_o, gu_o, gd_o, ng_o, dg_o) = refs[N_IN : N_IN + N_OUT]
+    (x_hbm, hist_hbm, cot_hbm, mask, wq_hbm, wo_hbm, wu_hbm, wd_hbm) = refs[:8]
+    (nrm, dw, cosine_hbm, sine_hbm) = refs[8:N_IN]
+    results, (ng_o, dg_o) = refs[N_IN : N_IN + N_OUT - 2], refs[N_IN + N_OUT - 2 : N_IN + N_OUT]
     s = Names()
     for name, ref in zip(SCRATCH, refs[N_IN + N_OUT :]):
         setattr(s, name, ref)
-    send_sems, recv_sems = refs[-2:]
+    send_sems, recv_sems, local_sems = refs[-3:]
 
     r, d = lax.axis_index("rows"), lax.axis_index("depth")
     z, x = lax.div(r, 2), lax.rem(r, 2)
@@ -493,13 +518,12 @@
     z_two, z_mirror, z_near = lax.rem(z + 2, 4), 3 - z, z + 1 - 2 * lax.rem(z, 2)
     two_dev, mirror_dev, near_dev = ((2 * zk + x, d) for zk in (z_two, z_mirror, z_near))
     inside = lax.rem(z + 1, 4) >= 2
+    outside = jnp.logical_not(inside)
     core_d, y_d, far_d = 2 * yy + other_c, 2 * other_y + c, 2 * other_y + other_c
     core_dev, y_dev, far_dev = (r, core_d), (r, y_d), (r, far_d)
     mates = ((core_d, core_dev), (y_d, y_dev), (far_d, far_dev))
     counter = [0]
     sent = []
-    sent_inside = []
-    sent_outside = []
 
     def prepare(src, dst, device, arrival=None):
         index = counter[0]
@@ -516,9 +540,19 @@
 
     def copy_to(src, dst, device):
         copy, _ = prepare(src, dst, device)
-        copy.start()
-        sent.append(copy)
+        start(copy)
         return copy
+
+    def start(copy, condition=None):
+        if condition is None:
+            copy.start()
+        else:
+            pl.when(condition)(copy.start)
+        sent.append((copy, condition))
+
+    def reserve(count):
+        counter[0] += count
+        return counter[0] - count
 
     def rows_at(ref, index, size):
         return ref.at[pl.ds(pl.multiple_of(index * size, size), size)]
@@ -530,10 +564,41 @@
 
         lax.fori_loop(0, count // step, one, 0)
 
+    hist, cot, wq, wo, wu, cosine, sine = s.hist, s.cot, s.wq, s.wo, s.wu, s.cosine, s.sine
+    loads = {}
+    for name, source, target in (
+        ("wq", wq_hbm, wq),
+        ("x", x_hbm, s.x_all.at[d]),
+        ("wo", wo_hbm, wo),
+        ("wu", wu_hbm, wu),
+        ("wd", wd_hbm, rows_at(s.w_down, r, BLOCK)),
+        ("cot", cot_hbm, cot),
+        ("cosine", cosine_hbm, cosine),
+        ("sine", sine_hbm, sine),
+        ("hist", hist_hbm, hist),
+    ):
+        loads[name] = pltpu.make_async_copy(source, target, local_sems.at[len(loads)])
+        loads[name].start()
+    out_o, ig_o, hg_o, gq_o, go_o, gu_o, gd_o = (
+        getattr(s, f"r_{i}") for i in range(N_OUT - 2)
+    )
+    stores = []
+
+    def store(i):
+        copy = pltpu.make_async_copy(
+            getattr(s, f"r_{i}"), results[i], local_sems.at[len(loads) + i]
+        )
+        copy.start()
+        stores.append(copy)
+
     barrier = pltpu.get_barrier_semaphore()
-    for device in (x_dev, two_dev, mirror_dev, near_dev, core_dev, y_dev, far_dev):
+    partners = [x_dev, core_dev, y_dev, far_dev]
+    partners += [
+        (2 * zk + x, m) for zk in (z_two, z_mirror, z_near) for m in (d, core_d, y_d, far_d)
+    ]
+    for device in partners:
         pl.semaphore_signal(barrier, inc=1, device_id=device, device_id_type=MESH)
-    pl.semaphore_wait(barrier, 7)
+    pl.semaphore_wait(barrier, len(partners))
 
     class Gather:
         def __init__(self, piece, cross=False):
@@ -541,48 +606,49 @@
             self.along_x = []
 
         def send_two(self):
-            mine = self.piece(r)
+            mine = self.piece(z, x)
             self.two = copy_to(mine, mine, two_dev)
 
         def send_mirror(self):
-            mine, passed = self.piece(r), self.piece(2 * z_two + x)
+            mine, passed = self.piece(z, x), self.piece(z_two, x)
             self.mirror, index = prepare(mine, mine, mirror_dev)
             self.passing, _ = prepare(passed, passed, near_dev, index)
-            sent_inside.extend([self.mirror, self.passing])
-            pl.when(inside)(self.mirror.start)
+            start(self.mirror, inside)
 
         def send_near(self, where=None):
             if where is not False:
-                mine = self.piece(r)
+                mine = self.piece(z, x)
                 self.near, _ = prepare(mine, mine, near_dev)
-                sent.append(self.near)
-            if where is None:
-                self.near.start()
-            else:
-                pl.when(jnp.logical_not(inside) if where else inside)(self.near.start)
-
-        def send_x(self, index=r):
-            piece = self.piece(index)
+            start(self.near, None if where is None else outside if where else inside)
+
+        def send_x(self, zk=z):
+            piece = self.piece(zk, x)
             self.along_x.append(copy_to(piece, piece, x_dev))
 
+        def arrive_near(self):
+            self.near.wait_recv()
+
         def forward_near(self):
-            self.near.wait_recv()
+            self.arrive_near()
             if not self.cross:
-                self.send_x(2 * z_near + x)
+                self.send_x(z_near)
 
         def forward_cross(self):
             self.along_x[0].wait_recv()
-            piece = self.piece(2 * z + other_x)
+            piece = self.piece(z, other_x)
             self.along_x[0] = copy_to(piece, piece, near_dev)
 
+        def pass_two(self):
+            self.two.wait_recv()
+            start(self.passing, inside)
+
         def forward_two(self):
-            self.two.wait_recv()
-            pl.when(inside)(self.passing.start)
-            self.send_x(2 * z_two + x)
+            self.pass_two()
+            self.send_x(z_two)
 
         def forward_mirror(self):
             self.mirror.wait_recv()
-            self.send_x(2 * z_mirror + x)
+            self.send_x(z_mirror)
 
         def finish(self):
             for copy in self.along_x:
@@ -607,10 +673,11 @@
             self.on.wait_recv()
 
     class RowSum:
-        def __init__(self, name, block, step, cross):
-            self.xs, self.xl, self.zs, self.zl, self.ns, self.nl, self.total = (
-                getattr(s, p + name) for p in ("xs_", "xl_", "zs_", "zl_", "ns_", "nl_", "f_")
+        def __init__(self, name, total, block, step, cross):
+            self.xs, self.xl, self.zs, self.zl, self.ns, self.nl = (
+                getattr(s, p + name) for p in ("xs_", "xl_", "zs_", "zl_", "ns_", "nl_")
             )
+            self.total = total
             self.block, self.step, self.cross = block, step, cross
             self.count = self.total.shape[0]
             self.along_x = {}
@@ -631,15 +698,15 @@
         def send(self):
             self.send_x("mirror", z_mirror)
             if self.cross:
-                self.stage(self.ns.at[0], 2 * z_near + other_x)
-                self.crossing = copy_to(self.ns.at[0], self.nl.at[0], near_dev)
+                self.send_crossing()
             self.send_x("two", z_two)
-            if self.cross:
-                self.stage(self.ns.at[1], 2 * z_near + x)
-                self.near = copy_to(self.ns.at[1], self.nl.at[1], near_dev)
-            else:
+            if not self.cross:
                 self.send_x("near", z_near)
                 self.send_x("own", z)
+
+        def send_crossing(self):
+            self.stage(self.ns.at[0], 2 * z_near + other_x)
+            self.crossing = copy_to(self.ns.at[0], self.nl.at[0], near_dev)
 
         def send_own(self):
             self.crossing.wait_recv()
@@ -650,10 +717,8 @@
             self.stage(self.zs.at[0], 2 * z_mirror + x, self.xl.at[z_mirror])
             self.mirror, _ = prepare(self.zs.at[0], self.zl.at[0], mirror_dev)
             self.passing, _ = prepare(self.zs.at[0], self.zl.at[2], near_dev)
-            sent_inside.append(self.mirror)
-            sent_outside.append(self.passing)
-            pl.when(inside)(self.mirror.start)
-            pl.when(jnp.logical_not(inside))(self.passing.start)
+            start(self.mirror, inside)
+            start(self.passing, outside)
 
         def send_two(self):
             self.along_x["two"].wait_recv()
@@ -663,15 +728,18 @@
                 self.passing.wait_recv()
                 self.stage(self.zs.at[1], 2 * z_two + x, self.xl.at[z_two], self.zl.at[2])
 
-            @pl.when(jnp.logical_not(inside))
+            @pl.when(outside)
             def _():
                 self.stage(self.zs.at[1], 2 * z_two + x, self.xl.at[z_two])
 
             self.two = copy_to(self.zs.at[1], self.zl.at[1], two_dev)
 
         def send_near(self):
-            self.along_x["near"].wait_recv()
-            self.stage(self.ns.at[1], 2 * z_near + x, self.xl.at[z_near])
+            extras = ()
+            if not self.cross:
+                self.along_x["near"].wait_recv()
+                extras = (self.xl.at[z_near],)
+            self.stage(self.ns.at[1], 2 * z_near + x, *extras)
             self.near = copy_to(self.ns.at[1], self.nl.at[1], near_dev)
 
         def finish(self):
@@ -698,39 +766,127 @@
 
                 by_rows(self.count, self.step, add_mirror)
 
+    class SpreadSum:
+        def __init__(self, half, arrivals):
+            self.xs, self.xl, self.cs, self.cl, self.zs, self.zl, self.ps = (
+                getattr(s, f"{p}_qkv{half}") for p in ("xs", "xl", "cs", "cl", "zs", "zl", "ps")
+            )
+            self.half, self.arrivals = half, arrivals
+            self.along_x = {}
+
+        def value(self, index, *extras):
+            rows = BLOCK // 2
+            start_row = pl.multiple_of((2 * index + self.half) * rows, rows)
+            value = s.g_qkv[pl.ds(start_row, rows), :]
+            for extra in extras:
+                value = value + extra.astype(F32)
+            return value
+
+        def send_x(self, name, zk, *extras):
+            self.xs[zk] = self.value(2 * zk + other_x, *extras).astype(BF)
+            self.along_x[name] = copy_to(self.xs.at[zk], self.xl.at[zk], x_dev)
+
+        def send_crossing(self):
+            self.cs[...] = self.value(2 * z_near + other_x).astype(BF)
+            self.crossing = copy_to(self.cs, self.cl, near_dev)
+
+        def send_own(self):
+            self.crossing.wait_recv()
+            self.send_x("own", z, self.cl[...])
+
+        def deliver(self, slot, zk, value, condition=None):
+            for j in range(2):
+                to = 2 * self.half + j
+                for t, tile in enumerate(fold(tiles_of(value[CHUNK * j : CHUNK * (j + 1)]))):
+                    self.ps[slot, j, :, 128 * t : 128 * (t + 1)] = tile.astype(BF)
+                copy, _ = prepare(
+                    self.ps.at[slot, j],
+                    s.fin.at[slot, d],
+                    (2 * zk + x, to),
+                    self.arrivals + GROUP * slot + d,
+                )
+                if slot == 3:
+                    start(copy, d != to)
+
+                    @pl.when(d == to)
+                    def _(j=j):
+                        s.fin[slot, d] = self.ps[slot, j]
+                else:
+                    start(copy, condition)
+
+        def send_mirror(self):
+            self.along_x["mirror"].wait_recv()
+            value = self.value(2 * z_mirror + x, self.xl[z_mirror])
+            self.deliver(2, z_mirror, value, inside)
+            self.zs[...] = value.astype(BF)
+            self.passing, _ = prepare(self.zs, self.zl, near_dev)
+            start(self.passing, outside)
+
+        def send_two(self):
+            self.along_x["two"].wait_recv()
+
+            @pl.when(outside)
+            def _():
+                self.zl[...] = jnp.zeros((BLOCK // 2, PACK), BF)
+
+            pl.when(inside)(self.passing.wait_recv)
+            self.deliver(0, z_two, self.value(2 * z_two + x, self.xl[z_two], self.zl[...]))
+
+        def send_near(self):
+            self.deliver(1, z_near, self.value(2 * z_near + x))
+
+        def keep_own(self):
+            self.along_x["own"].wait_recv()
+            self.deliver(3, z, self.value(r, self.xl[z]))
+
     class GroupSum:
-        def __init__(self, name, source):
+        def __init__(self, name, source, parts=1):
             self.s1, self.l1, self.s2, self.l2 = (
                 getattr(s, p + name) for p in ("s1_", "l1_", "s2_", "l2_")
             )
-            self.source = source
+            self.source, self.parts, self.size = source, parts, OWN // parts
+            self.first, self.second = {}, {}
 
         def block(self, index, at):
             return self.source[pl.ds(pl.multiple_of(index * OWN + at.start, at.size), at.size), :]
 
+        def part(self, i):
+            return pl.ds(self.size * i, self.size)
+
+        def over(self, i, body):
+            def shifted(at):
+                body(pl.ds(pl.multiple_of(self.size * i + at.start, at.size), at.size))
+
+            by_rows(self.size, 32, shifted)
+
         def send(self):
-            self.first = []
             for j, yj in enumerate((other_y, yy)):
+                for i in range(self.parts):
+
+                    def stage(at):
+                        self.s1[j, at, :] = self.block(2 * yj + other_c, at).astype(BF)
+
+                    self.over(i, stage)
+                    self.first[j, i] = copy_to(
+                        self.s1.at[j, self.part(i)], self.l1.at[j, self.part(i)], core_dev
+                    )
+
+        def middle(self):
+            for i in range(self.parts):
+                self.first[0, i].wait_recv()
 
                 def stage(at):
-                    self.s1[j, at, :] = self.block(2 * yj + other_c, at).astype(BF)
-
-                by_rows(OWN, 32, stage)
-                self.first.append(copy_to(self.s1.at[j], self.l1.at[j], core_dev))
-
-        def middle(self):
-            self.first[0].wait_recv()
-
-            def stage(at):
-                value = self.block(2 * other_y + c, at) + self.l1[0, at, :].astype(F32)
-                self.s2[at, :] = value.astype(BF)
-
-            by_rows(OWN, 32, stage)
-            self.second = copy_to(self.s2, self.l2, y_dev)
-
-        def wait(self):
-            self.first[1].wait_recv()
-            self.second.wait_recv()
+                    value = self.block(2 * other_y + c, at) + self.l1[0, at, :].astype(F32)
+                    self.s2[at, :] = value.astype(BF)
+
+                self.over(i, stage)
+                self.second[i] = copy_to(
+                    self.s2.at[self.part(i)], self.l2.at[self.part(i)], y_dev
+                )
+
+        def wait(self, i=0):
+            self.first[1, i].wait_recv()
+            self.second[i].wait_recv()
 
         def value(self, at):
             return (
@@ -739,13 +895,71 @@
                 + self.l2[at, :].astype(F32)
             )
 
-    out_gather = Gather(lambda i: s.wo_l.at[d, i])
-    for t, tile in enumerate(fold(tiles_of(wo[...].astype(F32)))):
-        s.wo_l[d, r, :, 128 * t : 128 * (t + 1)] = tile.astype(BF)
-    out_gather.send_two()
-    out_gather.send_mirror()
-    out_gather.send_near()
-    out_gather.send_x()
+    class PieceGather:
+        def __init__(self):
+            self.along_x = {}
+
+        def fan(self, zk, mates_only=False, condition=None):
+            copies = [None] if mates_only else []
+            for m in (core_d, y_d, far_d) if mates_only else (d, core_d, y_d, far_d):
+                copy, _ = prepare(s.qp_s.at[m], s.q_all.at[r, d], (2 * zk + x, m))
+                start(copy, condition)
+                copies.append(copy)
+            return copies
+
+        def slab(self, zk, xk, h):
+            return s.q_all.at[2 * zk + xk, pl.ds(pl.multiple_of(2 * (other_y if h else yy), 2), 2)]
+
+        def send(self):
+            self.own = self.fan(z, mates_only=True)
+            self.two = self.fan(z_two)
+            self.near = self.fan(z_near)
+            self.mirror = self.fan(z_mirror, condition=inside)
+            self.passing = []
+            for h in range(2):
+                slab = self.slab(z_two, x, h)
+                self.passing.append(prepare(slab, slab, near_dev)[0])
+
+        def send_x(self, name, zk, h):
+            slab = self.slab(zk, x, h)
+            self.along_x[name, h] = copy_to(slab, slab, x_dev)
+
+        def wait(self, copies, h):
+            for copy in copies[2 * h : 2 * h + 2]:
+                if copy is not None:
+                    copy.wait_recv()
+
+        def forward_own(self, h):
+            self.wait(self.own, h)
+            self.send_x("own", z, h)
+
+        def forward_near(self, h):
+            self.wait(self.near, h)
+            self.send_x("near", z_near, h)
+
+        def forward_two(self, h):
+            self.wait(self.two, h)
+            start(self.passing[h], inside)
+            self.send_x("two", z_two, h)
+
+        def forward_mirror(self, h):
+            pl.when(inside)(lambda: self.wait(self.mirror, h))
+            pl.when(outside)(self.passing[h].wait_recv)
+            self.send_x("mirror", z_mirror, h)
+
+        def finish(self, name):
+            for h in range(2):
+                self.along_x[name, h].wait_recv()
+
+    def assemble(landing, count, target, row):
+        for k in range(GROUP):
+            tiles = [t.astype(F32) for t in tiles_of(landing[k])]
+            for t, tile in enumerate(unfold(tiles, count)):
+                s.tmp[CHUNK * k : CHUNK * (k + 1), 128 * t : 128 * (t + 1)] = tile
+        rows_at(target, row, BLOCK)[...] = s.tmp[:, : 128 * count].astype(BF)
+
+    def assemble_qkv(row):
+        assemble(s.q_all.at[row], 5, s.w_qkv, row)
 
     lane = lane_id((CHUNK, 128))
     eye = row_id((CHUNK, CHUNK)) == lane_id((CHUNK, CHUNK))
@@ -759,15 +973,27 @@
     ones = jnp.sum(mask_row, axis=1, keepdims=True)
     extra = jnp.where((lane == 104) & (row_id((CHUNK, 128)) == 0), ones, extra)
 
+    loads["wq"].wait()
     wq_tiles = tiles_of(wq[...].astype(F32))
     for k in range(GROUP):
         tiles = permute_chunks(wq_tiles, qkv_picks(k))
         tiles[2] = tiles[2] + extra
         for t, tile in enumerate(fold(tiles)):
             s.qp_s[k, :, 128 * t : 128 * (t + 1)] = tile.astype(BF)
-    qp_copies = [copy_to(s.qp_s.at[m], s.qp_l.at[d], device) for m, device in mates]
-    s.qp_l[d] = s.qp_s[d]
-
+    qkv_gather = PieceGather()
+    qkv_gather.send()
+    s.q_all[r, d] = s.qp_s[d]
+
+    loads["wo"].wait()
+    out_gather = Gather(lambda zk, xk: s.wo_l.at[d, xk, zk])
+    for t, tile in enumerate(fold(tiles_of(wo[...].astype(F32)))):
+        s.wo_l[d, x, z, :, 128 * t : 128 * (t + 1)] = tile.astype(BF)
+    out_gather.send_two()
+    out_gather.send_mirror()
+    out_gather.send_near()
+    out_gather.send_x()
+
+    loads["wu"].wait()
     wu_tiles = tiles_of(wu[...].astype(F32))
     for k in range(GROUP):
         for t, tile in enumerate(fold(permute_chunks(wu_tiles, up_picks(k)))):
@@ -775,59 +1001,25 @@
     up_copies = [copy_to(s.up_s.at[m], s.up_l.at[d], device) for m, device in mates]
     s.up_l[d] = s.up_s[d]
 
-    rows_at(s.w_down, r, BLOCK)[...] = wd[...]
-    downs = [
-        Gather(lambda i, h=h: rows_at(s.w_down, 2 * i + h, BLOCK // 2), cross=True) for h in range(2)
-    ]
-    downs[0].send_two()
-    downs[0].send_near(True)
-    for half in downs:
-        half.send_x()
-
-    s.x_all[d] = x_in[...]
+    loads["x"].wait()
     x_gather = GroupGather(lambda i: s.x_all.at[i])
     x_gather.send()
 
+    loads["wd"].wait()
+    up_gather = Gather(lambda zk, xk: rows_at(s.w_up, 2 * zk + xk, BLOCK), cross=True)
+    downs = [
+        Gather(
+            lambda zk, xk, h=h: rows_at(s.w_down, 2 * (2 * zk + xk) + h, BLOCK // 2), cross=h == 0
+        )
+        for h in range(2)
+    ]
     diagonal = jnp.where(
         row_id((OWN, OWN)) == lane_id((OWN, OWN)), jnp.broadcast_to(mask_row, (OWN, OWN)), 0.0
     )
+    loads["cot"].wait()
     s.c_all[d] = dot(diagonal.astype(BF), cot[...]).astype(BF)
     c_gather = GroupGather(lambda i: s.c_all.at[i])
     c_gather.send()
-
-    def assemble(landing, count, target):
-        for k in range(GROUP):
-            tiles = [t.astype(F32) for t in tiles_of(landing[k])]
-            for t, tile in enumerate(unfold(tiles, count)):
-                s.tmp[CHUNK * k : CHUNK * (k + 1), 128 * t : 128 * (t + 1)] = tile
-        rows_at(target, r, BLOCK)[...] = s.tmp[:, : 128 * count].astype(BF)
-
-    for copy in qp_copies:
-        copy.wait_recv()
-    assemble(s.qp_l, 5, s.w_qkv)
-    halves = [Gather(lambda i, h=h: rows_at(s.w_qkv, 2 * i + h, BLOCK // 2)) for h in range(2)]
-    for half in halves:
-        half.send_two()
-    for half in halves:
-        half.send_near()
-        half.send_x()
-    for half in halves:
-        half.send_mirror()
-    out_gather.forward_two()
-    out_gather.forward_near()
-    for copy in up_copies:
-        copy.wait_recv()
-    assemble(s.up_l, 6, s.w_up)
-    up_gather = Gather(lambda i: rows_at(s.w_up, i, BLOCK))
-    up_gather.send_two()
-    up_gather.send_near(True)
-    up_gather.send_x()
-    x_gather.relay()
-    halves[0].forward_near()
-    halves[0].forward_two()
-    out_gather.forward_mirror()
-    halves[1].forward_near()
-    x_gather.finish()
 
     def normalize(i):
         def one(at):
@@ -836,23 +1028,47 @@
 
         by_rows(OWN, 64, one)
 
-    normalize(0)
-    halves[1].forward_two()
+    qkv_gather.forward_own(0)
+    qkv_gather.forward_near(0)
+    qkv_gather.forward_own(1)
+    assemble_qkv(r)
+    qkv_gather.forward_two(0)
+    qkv_gather.forward_near(1)
+    assemble_qkv(2 * z_near + x)
+    qkv_gather.forward_two(1)
+    out_gather.pass_two()
+    assemble_qkv(2 * z_two + x)
+    for copy in up_copies:
+        copy.wait_recv()
+    assemble(s.up_l, 6, s.w_up, r)
+    up_gather.send_two()
+    up_gather.send_near(True)
+    qkv_gather.forward_mirror(0)
+    x_gather.relay()
+    qkv_gather.forward_mirror(1)
     up_gather.send_near(False)
     up_gather.send_mirror()
-    downs[1].send_two()
-    downs[1].send_near(True)
-    normalize(1)
-    halves[0].forward_mirror()
-    normalize(2)
-    normalize(3)
-    out_gather.finish()
-    slab_gather = GroupGather(lambda i: s.wo_l.at[i])
-    slab_gather.send()
-    halves[1].forward_mirror()
+    for half in downs:
+        half.send_two()
+        half.send_near()
+    out_gather.send_x(z_two)
+    out_gather.forward_near()
+    out_gather.forward_mirror()
+    up_gather.send_x()
+    for half in downs:
+        half.send_x()
+    columns = [GroupGather(lambda i, xk=xk: s.wo_l.at[i, xk]) for xk in (x, other_x)]
+    columns[0].send()
+    assemble_qkv(2 * z_mirror + x)
+    x_gather.finish()
+    for i in range(GROUP):
+        normalize(i)
+    for name, zk in (("own", z), ("near", z_near), ("two", z_two)):
+        qkv_gather.finish(name)
+        assemble_qkv(2 * zk + other_x)
     c_gather.relay()
-    for half in halves:
-        half.finish()
+    qkv_gather.finish("mirror")
+    assemble_qkv(2 * z_mirror + other_x)
 
     lane = lane_id((8, 128))
     row = row_id((8, 128))
@@ -879,7 +1095,8 @@
             target[at, 128:] = (b * co + a * si).astype(BF)
         s.v01[at, :] = value[:, 512:].astype(BF)
 
-    up_gather.forward_near()
+    loads["cosine"].wait()
+    loads["sine"].wait()
     by_rows(SEQ, 256, project)
 
     lane2 = lax.div(lax.rem(lane_id((1, 256)), 128), jnp.int32(32))
@@ -910,10 +1127,10 @@
             if b == 1 and h == 0:
                 up_gather.forward_two()
                 for half in downs:
-                    half.send_near(False)
                     half.send_mirror()
             if b == 1 and h == 1:
-                downs[0].forward_two()
+                out_gather.finish()
+                columns[1].send()
         s.o_l[d, b, :QBLOCK, :] = first.astype(BF)
         lane = lane_id((QBLOCK, 128))
         third = jnp.where(
@@ -925,15 +1142,17 @@
         o_gathers[b].send()
 
     attend(1)
-    slab_gather.relay()
+    columns[0].relay()
     attend(0)
-    for half in downs:
-        half.forward_cross()
+    up_gather.forward_cross()
+    columns[1].relay()
+    downs[1].forward_near()
     up_gather.forward_mirror()
-    slab_gather.finish()
+    for column in columns:
+        column.finish()
     for k in range(GROUP):
         for i in range(ROWS):
-            tiles = [t.astype(F32) for t in tiles_of(s.wo_l[k, i])]
+            tiles = [t.astype(F32) for t in tiles_of(s.wo_l[k, i % 2, i // 2])]
             at = CHUNK * (GROUP * i + k)
             for t, tile in enumerate(unfold(tiles, 6)):
                 s.g_out[at : at + CHUNK, 128 * t : 128 * (t + 1)] = tile
@@ -950,9 +1169,12 @@
     s.w_own[96:128, :] = third_rows[:32, :]
     s.w_own[224:256, :] = third_rows[32:, :]
     s.w_own[256:, :] = rows_at(s.w_out.at[pl.ds(0, 512)], d, 128)[...]
+    downs[0].forward_two()
+    downs[0].forward_cross()
     o_gathers[1].relay()
     c_gather.finish()
 
+    loads["hist"].wait()
     s.terms[...] = jnp.zeros((8, WIDTH), F32)
     for i in range(GROUP):
 
@@ -965,6 +1187,7 @@
 
         by_rows(OWN, 32, loss_rows)
 
+    store(2)
     downs[1].forward_two()
     for b in (1, 0):
         if b == 0:
@@ -997,6 +1220,7 @@
 
             by_rows(OWN, 64, second_norm)
 
+    up_gather.arrive_near()
     up_gather.finish()
 
     def widen(at):
@@ -1020,20 +1244,21 @@
         inner = rate * (1.0 + 3 * 0.044715 * u * u)
         s.slope[at, :] = 0.5 * (1.0 + bend) + 0.5 * u * (1.0 - bend * bend) * inner
 
-    def block_of(ref):
+    def block_of(ref, shift=0):
         def block(index, at):
-            return ref[pl.ds(pl.multiple_of(index * BLOCK + at.start, at.size), at.size), :]
+            start = pl.multiple_of(index * BLOCK + shift + at.start, at.size)
+            return ref[pl.ds(start, at.size), :]
 
         return block
 
     for i in range(3):
         cols = slice(QBLOCK * i, QBLOCK * (i + 1))
         s.g_down[cols, :] = dot(s.act[:, cols], s.dm[...], 0, 0)
-    down_sum = RowSum("down", block_of(s.g_down), 16, True)
+    down_sum = RowSum("down", s.f_down, block_of(s.g_down), 16, True)
     down_sum.send()
     by_rows(SEQ, 32, gate_slope)
+    downs[0].arrive_near()
     for half in downs:
-        half.forward_near()
         half.finish()
 
     def narrow(at):
@@ -1046,16 +1271,16 @@
         s.part[at, :] = dot(s.du[at, :], s.w_up[...], 1, 1)
 
     by_rows(SEQ, 256, second_back)
-    mid_sum = GroupSum("mid", s.part)
+    mid_sum = GroupSum("mid", s.part, 4)
     mid_sum.send()
 
     for i in range(3):
         cols = slice(QBLOCK * i, QBLOCK * (i + 1))
         s.g_up[cols, :] = dot(s.h2[:, cols], s.du[...], 0, 0)
-    up_sum = RowSum("up", block_of(s.g_up), 16, True)
+    up_sum = RowSum("up", s.f_up, block_of(s.g_up), 16, True)
     mid_sum.middle()
+    down_sum.send_mirror()
     up_sum.send()
-    down_sum.send_own()
 
     def block_out(at):
         value = dot(s.act[at, :], s.w_down[...])
@@ -1075,8 +1300,6 @@
         by_rows(OWN, 32, mix)
     mix_sum = GroupSum("mix", s.part2)
     mix_sum.send()
-    mid_sum.wait()
-
     s.t0[...] = jnp.zeros((8, WIDTH), F32)
 
     def second_norm_back(at):
@@ -1092,45 +1315,33 @@
         s.t0[3:4, :] += jnp.sum(grad, axis=0, keepdims=True)
         s.terms2[...] += sublane_sum(loss * value)
 
-    by_rows(OWN, 32, second_norm_back)
-    dy_gather = GroupGather(lambda i: s.dyb.at[i])
-    dy_gather.send()
-
+    dy_gathers = []
+    for i in range(4):
+        mid_sum.wait(i)
+        mid_sum.over(i, second_norm_back)
+        dy_gathers.append(GroupGather(lambda j, i=i: s.dyb.at[j, mid_sum.part(i)]))
+        dy_gathers[i].send()
+
+    down_sum.send_two()
+    down_sum.send_own()
     mix_sum.middle()
-    down_sum.send_mirror()
+    lane = lane_id((8, 128))
+    own_term = jnp.sum(jnp.sum(s.terms[...], axis=0, keepdims=True), axis=1, keepdims=True)
+    last_term = jnp.sum(jnp.sum(s.terms2[...], axis=0, keepdims=True), axis=1, keepdims=True)
+    s.u0[...] = jnp.where(lane == d, own_term, jnp.where(lane == GROUP, last_term, 0.0))
+    depth_x = copy_to(s.u0, s.u1, x_dev)
+    for i, one in enumerate(dy_gathers):
+        one.relay()
+        if i == 0:
+            up_sum.send_mirror()
+    for one in dy_gathers:
+        one.finish()
     up_sum.send_own()
-    dy_gather.relay()
-    down_sum.send_two()
-    dy_gather.finish()
+    down_sum.send_near()
 
     by_group = s.dyb[...].reshape(SEQ, WIDTH)
 
     s.dob[...] = dot(by_group, s.w_own[...], 1, 1).astype(BF)
-    for p in range(3):
-        cols = slice(QBLOCK * p, QBLOCK * (p + 1))
-        value = dot(s.ob[:, cols], by_group, 0, 0)
-        for i in range(4):
-            place = QBLOCK * p + 64 * i
-            for head in range(HEADS):
-                if out_place(head) == place:
-                    s.g_out[64 * head : 64 * head + 64, :] = value[64 * i : 64 * i + 64]
-
-    def out_block(index, at):
-        start = pl.multiple_of((GROUP * index + d) * CHUNK, 8)
-        tiles = tiles_of(s.g_out[pl.ds(start, CHUNK), :])
-        return jnp.concatenate(fold(tiles), axis=1)
-
-    out_sum = RowSum("out", out_block, 16, False)
-    out_sum.send()
-    mix_sum.wait()
-
-    def write_out(at):
-        here = pl.ds(pl.multiple_of(OWN * d + at.start, at.size), at.size)
-        out_o[at, :] = (mix_sum.value(at) + last_weight * s.y[here, :]).astype(BF)
-
-    by_rows(OWN, 32, write_out)
-    up_sum.send_mirror()
-
     for b in range(2):
         rows = slice(QBLOCK * b, QBLOCK * (b + 1))
         keys = QBLOCK * (b + 1)
@@ -1172,6 +1383,9 @@
                 else:
                     s.dv[new, cols] += dv[QBLOCK:]
         s.dq[rows, :] = dq * root
+        if b == 0:
+            up_sum.send_two()
+            up_sum.send_near()
 
     def turn_back(at):
         co, si = cosine[at, :], sine[at, :]
@@ -1188,8 +1402,18 @@
     for i in range(3):
         cols = slice(QBLOCK * i, QBLOCK * (i + 1))
         s.g_qkv[cols, :] = dot(s.h1[:, cols], s.dqkv[...], 0, 0)
-    qkv_sum = RowSum("qkv", block_of(s.g_qkv), 16, True)
-    qkv_sum.send()
+    qkv_arrivals = reserve(16)
+    sums = [SpreadSum(h, qkv_arrivals) for h in range(2)]
+    for one in sums:
+        one.send_x("mirror", z_mirror)
+        one.send_crossing()
+    for one in sums:
+        one.send_x("two", z_two)
+    depth_x.wait_recv()
+    s.uz[z] = s.u0[...] + s.u1[...]
+    depth_z = [
+        copy_to(s.uz.at[z], s.uz.at[z], device) for device in (two_dev, mirror_dev, near_dev)
+    ]
 
     def first_back(at):
         s.part[at, :] = dot(s.dqkv[at, :], s.w_qkv[...], 1, 1)
@@ -1206,19 +1430,49 @@
         s.shift_sum[...] += sublane_sum(grad)
 
     by_rows(SEQ, 32, first_norm_sums)
-    in_sum.middle()
     s.t0[0:1, :] = jnp.sum(s.gain_sum[...], axis=0, keepdims=True)
     s.t0[1:2, :] = jnp.sum(s.shift_sum[...], axis=0, keepdims=True)
-    lane = lane_id((1, WIDTH))
-    own_term = jnp.sum(jnp.sum(s.terms[...], axis=0, keepdims=True), axis=1, keepdims=True)
-    last_term = jnp.sum(jnp.sum(s.terms2[...], axis=0, keepdims=True), axis=1, keepdims=True)
-    s.t0[4:5, :] = jnp.where(lane == d, own_term, jnp.where(lane == GROUP, last_term, 0.0))
-    small = copy_to(s.t0, s.t1, x_dev)
-    up_sum.send_two()
-    out_sum.send_mirror()
-    qkv_sum.send_own()
-    out_sum.send_near()
-    out_sum.send_two()
+    s.td[d] = s.t0[...]
+    norm_copies = [copy_to(s.td.at[d], s.td.at[d], device) for m, device in mates]
+    in_sum.middle()
+    for p in range(3):
+        cols = slice(QBLOCK * p, QBLOCK * (p + 1))
+        value = dot(s.ob[:, cols], s.dyb[...].reshape(SEQ, WIDTH), 0, 0)
+        for i in range(4):
+            place = QBLOCK * p + 64 * i
+            for head in range(HEADS):
+                if out_place(head) == place:
+                    s.g_out[64 * head : 64 * head + 64, :] = value[64 * i : 64 * i + 64]
+
+    for one in sums:
+        one.send_mirror()
+    for copy in norm_copies:
+        copy.wait_recv()
+    value = (s.td[0] + s.td[1]) + (s.td[2] + s.td[3])
+    value = pltpu.roll(value, lax.rem(WIDTH - CHUNK * d, WIDTH), 1)
+    for i in range(ROWS):
+        shift = (WIDTH - BLOCK * i) % WIDTH
+        shifted = pltpu.roll(value, shift, 1) if shift else value
+        s.ext[i] = jnp.concatenate([shifted[:, :128], jnp.zeros((8, 128), F32)], axis=0)
+
+    def out_block(index, at):
+        start_row = pl.multiple_of((GROUP * index + d) * CHUNK, 8)
+        tiles = tiles_of(s.g_out[pl.ds(start_row, CHUNK), :])
+        return jnp.concatenate(fold(tiles) + [s.ext[index]], axis=1)
+
+    out_sum = RowSum("out", s.f_out, out_block, 16, False)
+    out_sum.send()
+    down_sum.finish()
+    gd_o[...] = s.f_down[...]
+    store(6)
+    mix_sum.wait()
+
+    def write_out(at):
+        here = pl.ds(pl.multiple_of(OWN * d + at.start, at.size), at.size)
+        out_o[at, :] = (mix_sum.value(at) + last_weight * s.y[here, :]).astype(BF)
+
+    by_rows(OWN, 32, write_out)
+    store(0)
 
     def spread(total, staged, landing):
         copies = []
@@ -1241,61 +1495,81 @@
         for t, tile in enumerate(permute_chunks(tiles, back)):
             target[:, 128 * t : 128 * (t + 1)] = tile
 
-    qkv_sum.send_mirror()
-    small.wait_recv()
-    s.tz[z] = s.t0[...] + s.t1[...]
-    small_z = [
-        copy_to(s.tz.at[z], s.tz.at[z], device) for device in (two_dev, mirror_dev, near_dev)
-    ]
-    qkv_sum.send_two()
-    down_sum.finish()
-    gd_o[...] = s.f_down[...]
     up_sum.finish()
     up_spread = spread(s.f_up, s.b_up, s.a_up)
+    for one in sums:
+        one.send_two()
+    for one in sums:
+        one.send_near()
+    for one in sums:
+        one.send_own()
     in_sum.wait()
 
     def first_norm_back(at):
         grad = in_sum.value(at)
-        normal, scale = standardize(x_in[at, :].astype(F32))
+        normal, scale = standardize(s.x_all[d, at, :].astype(F32))
         back = norm_back(grad, s.norms[0:1, :], normal, scale)
         ig_o[at, :] = (s.dy[at, :] + back).astype(BF)
 
     by_rows(OWN, 32, first_norm_back)
-    for copy in small_z:
+    store(1)
+    out_sum.send_mirror()
+    for copy in depth_z:
         copy.wait_recv()
-    s.td[d] = (s.tz[0] + s.tz[1]) + (s.tz[2] + s.tz[3])
-    small_d = [copy_to(s.td.at[d], s.td.at[d], device) for m, device in mates]
-    out_sum.finish()
-    for t, tile in enumerate(unfold(tiles_of(s.f_out[...]), 6)):
-        go_o[:, 128 * t : 128 * (t + 1)] = tile
+    s.ud[d] = (s.uz[0] + s.uz[1]) + (s.uz[2] + s.uz[3])
+    depth_d = [copy_to(s.ud.at[d], s.ud.at[d], device) for m, device in mates]
+    out_sum.send_near()
+    for one in sums:
+        one.keep_own()
     collect(up_spread, s.a_up, 6, UP_BACK, gu_o)
-    for copy in small_d:
+    store(5)
+    out_sum.send_two()
+    for copy in depth_d:
         copy.wait_recv()
-    value = (s.td[0] + s.td[1]) + (s.td[2] + s.td[3])
-    dg_o[...] = value[:, :128]
-    choose = row_id((WIDTH, 128)) == lane_id((WIDTH, 128)) + CHUNK * (GROUP * r + d)
-    ng_o[...] = lax.dot_general(
-        value,
-        jnp.where(choose, 1.0, 0.0),
-        (((1,), (0,)), ((), ())),
-        preferred_element_type=F32,
-        precision=lax.Precision.HIGHEST,
-    )
-    qkv_sum.finish()
-    qkv_spread = spread(s.f_qkv, s.b_qkv, s.a_qkv)
-    collect(qkv_spread, s.a_qkv, 5, QKV_BACK, gq_o)
-    for copy in sent:
-        copy.wait_send()
+    dg_o[...] = (s.ud[0] + s.ud[1]) + (s.ud[2] + s.ud[3])
+
+    def arrived(slot, k):
+        return pltpu.make_async_remote_copy(
+            src_ref=s.fin.at[slot, k],
+            dst_ref=s.fin.at[slot, k],
+            send_sem=send_sems.at[0],
+            recv_sem=recv_sems.at[qkv_arrivals + GROUP * slot + k],
+            device_id=x_dev,
+            device_id_type=MESH,
+        )
+
+    for k in range(GROUP):
+        pl.when(d != k)(arrived(3, k).wait_recv)
+        arrived(1, k).wait_recv()
+        arrived(0, k).wait_recv()
+        s.q_sum[k] = (
+            s.fin[3, k].astype(F32) + s.fin[1, k].astype(F32) + s.fin[0, k].astype(F32)
+        )
 
     @pl.when(inside)
     def _():
-        for copy in sent_inside:
+        for k in range(GROUP):
+            arrived(2, k).wait_recv()
+            s.q_sum[k] += s.fin[2, k].astype(F32)
+
+    tiles = []
+    for k in range(GROUP):
+        tiles += unfold(tiles_of(s.q_sum[k]), 5)
+    for t, tile in enumerate(permute_chunks(tiles, QKV_BACK)):
+        gq_o[:, 128 * t : 128 * (t + 1)] = tile
+    store(3)
+    out_sum.finish()
+    for t, tile in enumerate(unfold(tiles_of(s.f_out[:, :1152]), 6)):
+        go_o[:, 128 * t : 128 * (t + 1)] = tile
+    ng_o[...] = s.f_out[:8, 1152:]
+    store(4)
+    for copy in stores:
+        copy.wait()
+    for copy, condition in sent:
+        if condition is None:
             copy.wait_send()
-
-    @pl.when(jnp.logical_not(inside))
-    def _():
-        for copy in sent_outside:
-            copy.wait_send()
+        else:
+            pl.when(condition)(copy.wait_send)
 
 
 def finish_kernel(*refs):
@@ -1308,7 +1582,7 @@
     for copy in first:
         copy.start()
     norm_o[...] = norm[:4, :CHUNK]
-    depth_o[...] = depth[4:5, : GROUP + 1]
+    depth_o[...] = depth[:1, : GROUP + 1]
     second = []
     for i, copy in enumerate(first):
         copy.wait()
@@ -1333,7 +1607,7 @@
     cosine, sine = tables()
     vmem = pl.BlockSpec(memory_space=pltpu.VMEM)
     smem = pl.BlockSpec(memory_space=pltpu.SMEM)
-    anywhere = pl.BlockSpec(memory_space=pl.ANY)
+    hbm = pl.BlockSpec(memory_space=pltpu.HBM)
     shape = jax.ShapeDtypeStruct
     shapes = (
         shape((OWN, WIDTH), BF),
@@ -1349,10 +1623,11 @@
     outs = pl.pallas_call(
         fused_kernel,
         out_shape=shapes,
-        in_specs=[vmem] * 9 + [smem] + [vmem] * 2,
-        out_specs=[vmem] * 9,
+        in_specs=[hbm] * 3 + [vmem] + [hbm] * 4 + [vmem, smem] + [hbm] * 2,
+        out_specs=[hbm] * 7 + [vmem] * 2,
         scratch_shapes=[pltpu.VMEM(dims, kind) for dims, kind in SCRATCH.values()]
-        + [pltpu.SemaphoreType.DMA((N_SEMS,))] * 2,
+        + [pltpu.SemaphoreType.DMA((N_SEMS,))] * 2
+        + [pltpu.SemaphoreType.DMA((16,))],
         compiler_params=pltpu.CompilerParams(
             collective_id=0, has_side_effects=True, vmem_limit_bytes=VMEM_MIB * 2**20
         ),
@@ -1374,8 +1649,8 @@
     held = pl.pallas_call(
         finish_kernel,
         out_shape=shapes[:7] + (shape((4, CHUNK), F32), shape((1, GROUP + 1), F32)),
-        in_specs=[anywhere] * 7 + [vmem] * 2,
-        out_specs=[anywhere] * 7 + [vmem] * 2,
+        in_specs=[hbm] * 7 + [vmem] * 2,
+        out_specs=[hbm] * 7 + [vmem] * 2,
         scratch_shapes=[pltpu.VMEM(one.shape, one.dtype) for one in shapes[:7]]
         + [pltpu.SemaphoreType.DMA((14,))],
         compiler_params=pltpu.CompilerParams(vmem_limit_bytes=VMEM_MIB * 2**20),

time: 114 us -> 103 us (0.904)
  Pallas kernels: 113 us -> 102 us
    pallas_call x1, Pallas kernels: 109 us -> 98 us  [fused(): pl.pallas_call(fused_kernel, out_shape=shapes, in_specs=[hbm] * 3 + [vmem...]
where the time goes in v3:
time: 103 us
  Pallas kernels  102 us (99%)
    pallas_call x1, Pallas kernels, fused(): pl.pallas_call(fused_kernel, out_shape=shapes, in_specs=[hbm] * 3 + [vmem...  98 us
    pallas_call x1, Pallas kernels, fused(): pl.pallas_call(finish_kernel, out_shape=shapes[:7] + (shape((4, CHUNK), F...  3.9 us

profile of v3, /device:TPU:0, one launch (start us, length us, event | category | flops | bytes accessed | tf_op | source)
XLA Modules:
  0.0 102.7 jit_solution(10270327197835535341)
XLA Ops:
  0.6 98.0 %shard_map.187 = (bf16[128,768]{1,0:T(8,128)(2,1)}, bf16[128,768]{1,0:T(8,128)(2,1)}, bf16[512,768]{1,0:T(8,128)(2,1)}, f32[24,2304]{1,0:T(8,128)}, f32[24,768]{...) custom-call(bf16[128,768]{1,0:T(8,128)(2,1)} %refs_0_.1, ...), custom_call_target="tpu_custom_call" | custom-call | flops 12000000000 | bytes 4000000 | tf_op jit(solution)/shard_map/pallas_call | solution.py:1623
  98.7 3.9 %shard_map.188 = (bf16[128,768]{1,0:T(8,128)(2,1)}, bf16[128,768]{1,0:T(8,128)(2,1)}, bf16[512,768]{1,0:T(8,128)(2,1)}, f32[24,2304]{1,0:T(8,128)}, f32[24,768]{...) custom-call(bf16[128,768]{1,0:T(8,128)(2,1)} %get-tuple-element.27.refs_0_, ...), custom_call_target="tpu_custom_call" | custom-call | tf_op jit(solution)/shard_map/pallas_call | solution.py:1649

commit v4 on v3

--- a/solution.py
+++ b/solution.py
@@ -412,7 +412,7 @@
     x_all=((GROUP, OWN, WIDTH), BF),
     c_all=((GROUP, OWN, WIDTH), BF),
     qp_s=((GROUP, 16, 1024), BF),
-    q_all=((ROWS, GROUP, 16, 1024), BF),
+    q_all=((ROWS * GROUP, 16, 1024), BF),
     up_s=((GROUP, 16, 1152), BF),
     up_l=((GROUP, 16, 1152), BF),
     tmp=((BLOCK, WIDTH), F32),
@@ -428,6 +428,8 @@
     qv=((SEQ, 256), BF),
     kk=((SEQ, 256), BF),
     v01=((SEQ, 128), BF),
+    v_all=((SEQ, 384), BF),
+    k_heads=((3, SEQ, 256), BF),
     probs=((3, SEQ, SEQ), F32),
     o_l=((GROUP, 2, 384, 128), BF),
     ob=((SEQ, WIDTH), BF),
@@ -445,7 +447,6 @@
     part2=((SEQ, WIDTH), F32),
     dy=((OWN, WIDTH), F32),
     dyb=((GROUP, OWN, WIDTH), BF),
-    dob=((SEQ, 384), BF),
     dq=((SEQ, 256), F32),
     dk=((SEQ, 256), F32),
     dv=((SEQ, 384), F32),
@@ -457,9 +458,9 @@
     ext=((ROWS, 16, 128), F32),
     u0=((8, 128), F32),
     u1=((8, 128), F32),
-    uz=((4, 8, 128), F32),
-    ud=((4, 8, 128), F32),
-    fin=((4, GROUP, 16, 1024), BF),
+    uzd=((8, 8, 128), F32),
+    fin=((16, 16, 1024), BF),
+    ps=((16, 16, 1024), BF),
     q_sum=((GROUP, 16, 1024), F32),
     a_up=((GROUP, 16, 1152), BF),
     f_down=((BLOCK, WIDTH), F32),
@@ -474,24 +475,21 @@
     ("up", BLOCK, WIDTH),
     ("out", 16, 1280),
 ):
-    SCRATCH["xs_" + _name] = ((4, _rows, _cols), BF)
+    SCRATCH["st_" + _name] = ((8, _rows, _cols), BF)
     SCRATCH["xl_" + _name] = ((4, _rows, _cols), BF)
-    SCRATCH["zs_" + _name] = ((2, _rows, _cols), BF)
     SCRATCH["zl_" + _name] = ((3, _rows, _cols), BF)
-    SCRATCH["ns_" + _name] = ((2, _rows, _cols), BF)
     SCRATCH["nl_" + _name] = ((2, _rows, _cols), BF)
 for _h in range(2):
-    for _name in ("xs", "xl"):
-        SCRATCH[f"{_name}_qkv{_h}"] = ((4, BLOCK // 2, PACK), BF)
-    for _name in ("cs", "cl", "zs", "zl"):
+    SCRATCH[f"st_qkv{_h}"] = ((6, BLOCK // 2, PACK), BF)
+    SCRATCH[f"xl_qkv{_h}"] = ((4, BLOCK // 2, PACK), BF)
+    for _name in ("cl", "zl"):
         SCRATCH[f"{_name}_qkv{_h}"] = ((BLOCK // 2, PACK), BF)
-    SCRATCH[f"ps_qkv{_h}"] = ((4, 2, 16, 1024), BF)
 for _name in ("mix", "mid", "in"):
-    SCRATCH["s1_" + _name] = ((2, OWN, WIDTH), BF)
+    SCRATCH["gs_" + _name] = ((3, OWN, WIDTH), BF)
     SCRATCH["l1_" + _name] = ((2, OWN, WIDTH), BF)
-    SCRATCH["s2_" + _name] = ((OWN, WIDTH), BF)
     SCRATCH["l2_" + _name] = ((OWN, WIDTH), BF)
-N_SEMS = 224
+N_SENDS = 36
+N_ARRIVALS = 116
 N_IN = 12
 N_OUT = 9
 VMEM_MIB = 60
@@ -522,37 +520,37 @@
     core_d, y_d, far_d = 2 * yy + other_c, 2 * other_y + c, 2 * other_y + other_c
     core_dev, y_dev, far_dev = (r, core_d), (r, y_d), (r, far_d)
     mates = ((core_d, core_dev), (y_d, y_dev), (far_d, far_dev))
-    counter = [0]
-    sent = []
-
-    def prepare(src, dst, device, arrival=None):
-        index = counter[0]
-        counter[0] += 1
-        copy = pltpu.make_async_remote_copy(
+    used = {"send": 0, "arrival": 0}
+    send_groups = []
+
+    def arrivals(count=1):
+        used["arrival"] += count
+        return used["arrival"] - count
+
+    def sends(view, condition=None):
+        used["send"] += 1
+        send_groups.append((used["send"] - 1, view, condition))
+        return used["send"] - 1
+
+    def prepare(src, dst, device, arrival, group):
+        return pltpu.make_async_remote_copy(
             src_ref=src,
             dst_ref=dst,
-            send_sem=send_sems.at[index],
-            recv_sem=recv_sems.at[index if arrival is None else arrival],
+            send_sem=send_sems.at[group],
+            recv_sem=recv_sems.at[arrival],
             device_id=device,
             device_id_type=MESH,
         )
-        return copy, index
-
-    def copy_to(src, dst, device):
-        copy, _ = prepare(src, dst, device)
-        start(copy)
-        return copy
-
-    def start(copy, condition=None):
+
+    def copy_to(src, dst, device, arrival, group, condition=None):
+        copy = prepare(src, dst, device, arrival, group)
         if condition is None:
             copy.start()
         else:
             pl.when(condition)(copy.start)
-        sent.append((copy, condition))
-
-    def reserve(count):
-        counter[0] += count
-        return counter[0] - count
+
+    def arrive(view, arrival):
+        prepare(view, view, x_dev, arrival, 0).wait_recv()
 
     def rows_at(ref, index, size):
         return ref.at[pl.ds(pl.multiple_of(index * size, size), size)]
@@ -601,32 +599,35 @@
     pl.semaphore_wait(barrier, len(partners))
 
     class Gather:
-        def __init__(self, piece, cross=False):
-            self.piece, self.cross = piece, cross
-            self.along_x = []
+        def __init__(self, piece, pieces, cross=False):
+            self.piece, self.pieces, self.cross = piece, pieces, cross
+            self.group, self.inner = sends(pieces(6)), sends(pieces(2), inside)
+            self.two, self.near, self.mirror, self.along_x = (arrivals() for _ in range(4))
+            self.own_x = arrivals() if cross else self.along_x
+
+        def copy(self, zk, xk, device, arrival, inner=False, condition=None):
+            piece = self.piece(zk, xk)
+            group = self.inner if inner else self.group
+            copy_to(piece, piece, device, arrival, group, condition)
 
         def send_two(self):
-            mine = self.piece(z, x)
-            self.two = copy_to(mine, mine, two_dev)
+            self.copy(z, x, two_dev, self.two)
 
         def send_mirror(self):
-            mine, passed = self.piece(z, x), self.piece(z_two, x)
-            self.mirror, index = prepare(mine, mine, mirror_dev)
-            self.passing, _ = prepare(passed, passed, near_dev, index)
-            start(self.mirror, inside)
+            self.copy(z, x, mirror_dev, self.mirror, True, inside)
 
         def send_near(self, where=None):
-            if where is not False:
-                mine = self.piece(z, x)
-                self.near, _ = prepare(mine, mine, near_dev)
-            start(self.near, None if where is None else outside if where else inside)
+            condition = None if where is None else outside if where else inside
+            self.copy(z, x, near_dev, self.near, condition=condition)
 
         def send_x(self, zk=z):
-            piece = self.piece(zk, x)
-            self.along_x.append(copy_to(piece, piece, x_dev))
+            self.copy(zk, x, x_dev, self.along_x)
+
+        def send_own_x(self):
+            self.copy(z, x, x_dev, self.own_x)
 
         def arrive_near(self):
-            self.near.wait_recv()
+            arrive(self.piece(z_near, x), self.near)
 
         def forward_near(self):
             self.arrive_near()
@@ -634,53 +635,61 @@
                 self.send_x(z_near)
 
         def forward_cross(self):
-            self.along_x[0].wait_recv()
-            piece = self.piece(z, other_x)
-            self.along_x[0] = copy_to(piece, piece, near_dev)
+            arrive(self.piece(z, other_x), self.own_x)
+            self.copy(z, other_x, near_dev, self.along_x)
 
         def pass_two(self):
-            self.two.wait_recv()
-            start(self.passing, inside)
+            arrive(self.piece(z_two, x), self.two)
+            self.copy(z_two, x, near_dev, self.mirror, True, inside)
 
         def forward_two(self):
             self.pass_two()
             self.send_x(z_two)
 
         def forward_mirror(self):
-            self.mirror.wait_recv()
+            arrive(self.piece(z_mirror, x), self.mirror)
             self.send_x(z_mirror)
 
         def finish(self):
-            for copy in self.along_x:
-                copy.wait_recv()
+            arrive(self.pieces(3 if self.cross else 4), self.along_x)
 
     class GroupGather:
-        def __init__(self, slab):
-            self.slab = slab
+        def __init__(self, slab, slabs, group=None):
+            self.slab, self.slabs = slab, slabs
+            self.group = sends(slabs(3)) if group is None else group
+            self.from_y, self.others = arrivals(), arrivals()
 
         def send(self):
             mine = self.slab(d)
-            self.to_core = copy_to(mine, mine, core_dev)
-            self.to_y = copy_to(mine, mine, y_dev)
+            copy_to(mine, mine, core_dev, self.others, self.group)
+            copy_to(mine, mine, y_dev, self.from_y, self.group)
 
         def relay(self):
-            self.to_y.wait_recv()
             slab = self.slab(y_d)
-            self.on = copy_to(slab, slab, core_dev)
+            arrive(slab, self.from_y)
+            copy_to(slab, slab, core_dev, self.others, self.group)
 
         def finish(self):
-            self.to_core.wait_recv()
-            self.on.wait_recv()
+            arrive(self.slabs(2), self.others)
 
     class RowSum:
         def __init__(self, name, total, block, step, cross):
-            self.xs, self.xl, self.zs, self.zl, self.ns, self.nl = (
-                getattr(s, p + name) for p in ("xs_", "xl_", "zs_", "zl_", "ns_", "nl_")
+            staged = getattr(s, "st_" + name)
+            self.xs, self.zs, self.ns = (
+                [staged.at[i + j] for j in range(n)] for i, n in ((0, 4), (4, 2), (6, 2))
             )
+            self.xs = staged.at[pl.ds(0, 4)]
+            self.xl, self.zl, self.nl = (getattr(s, p + name) for p in ("xl_", "zl_", "nl_"))
             self.total = total
             self.block, self.step, self.cross = block, step, cross
             self.count = self.total.shape[0]
-            self.along_x = {}
+            self.group = sends(staged.at[pl.ds(0, 7)])
+            self.along_x = {k: arrivals() for k in ("mirror", "two", "own")}
+            if not cross:
+                self.along_x["near"] = arrivals()
+            self.crossing, self.near, self.two, self.mirror, self.passing = (
+                arrivals() for _ in range(5)
+            )
 
         def stage(self, target, index, *extras):
             def one(at):
@@ -693,59 +702,62 @@
 
         def send_x(self, name, zk, *extras):
             self.stage(self.xs.at[zk], 2 * zk + other_x, *extras)
-            self.along_x[name] = copy_to(self.xs.at[zk], self.xl.at[zk], x_dev)
-
-        def send(self):
+            copy_to(self.xs.at[zk], self.xl.at[zk], x_dev, self.along_x[name], self.group)
+
+        def arrive_x(self, name, zk):
+            arrive(self.xl.at[zk], self.along_x[name])
+
+        def send(self, early_near=False):
             self.send_x("mirror", z_mirror)
             if self.cross:
                 self.send_crossing()
             self.send_x("two", z_two)
+            if self.cross and early_near:
+                self.send_near()
             if not self.cross:
                 self.send_x("near", z_near)
                 self.send_x("own", z)
 
         def send_crossing(self):
-            self.stage(self.ns.at[0], 2 * z_near + other_x)
-            self.crossing = copy_to(self.ns.at[0], self.nl.at[0], near_dev)
+            self.stage(self.ns[0], 2 * z_near + other_x)
+            copy_to(self.ns[0], self.nl.at[0], near_dev, self.crossing, self.group)
 
         def send_own(self):
-            self.crossing.wait_recv()
+            arrive(self.nl.at[0], self.crossing)
             self.send_x("own", z, self.nl.at[0])
 
         def send_mirror(self):
-            self.along_x["mirror"].wait_recv()
-            self.stage(self.zs.at[0], 2 * z_mirror + x, self.xl.at[z_mirror])
-            self.mirror, _ = prepare(self.zs.at[0], self.zl.at[0], mirror_dev)
-            self.passing, _ = prepare(self.zs.at[0], self.zl.at[2], near_dev)
-            start(self.mirror, inside)
-            start(self.passing, outside)
+            self.arrive_x("mirror", z_mirror)
+            self.stage(self.zs[0], 2 * z_mirror + x, self.xl.at[z_mirror])
+            copy_to(self.zs[0], self.zl.at[0], mirror_dev, self.mirror, self.group, inside)
+            copy_to(self.zs[0], self.zl.at[2], near_dev, self.passing, self.group, outside)
 
         def send_two(self):
-            self.along_x["two"].wait_recv()
+            self.arrive_x("two", z_two)
 
             @pl.when(inside)
             def _():
-                self.passing.wait_recv()
-                self.stage(self.zs.at[1], 2 * z_two + x, self.xl.at[z_two], self.zl.at[2])
+                arrive(self.zl.at[2], self.passing)
+                self.stage(self.zs[1], 2 * z_two + x, self.xl.at[z_two], self.zl.at[2])
 
             @pl.when(outside)
             def _():
-                self.stage(self.zs.at[1], 2 * z_two + x, self.xl.at[z_two])
-
-            self.two = copy_to(self.zs.at[1], self.zl.at[1], two_dev)
+                self.stage(self.zs[1], 2 * z_two + x, self.xl.at[z_two])
+
+            copy_to(self.zs[1], self.zl.at[1], two_dev, self.two, self.group)
 
         def send_near(self):
             extras = ()
             if not self.cross:
-                self.along_x["near"].wait_recv()
+                self.arrive_x("near", z_near)
                 extras = (self.xl.at[z_near],)
-            self.stage(self.ns.at[1], 2 * z_near + x, *extras)
-            self.near = copy_to(self.ns.at[1], self.nl.at[1], near_dev)
+            self.stage(self.ns[1], 2 * z_near + x, *extras)
+            copy_to(self.ns[1], self.nl.at[1], near_dev, self.near, self.group)
 
         def finish(self):
-            self.along_x["own"].wait_recv()
-            self.two.wait_recv()
-            self.near.wait_recv()
+            self.arrive_x("own", z)
+            arrive(self.zl.at[1], self.two)
+            arrive(self.nl.at[1], self.near)
 
             def add(at):
                 self.total[at, :] = (
@@ -759,7 +771,7 @@
 
             @pl.when(inside)
             def _():
-                self.mirror.wait_recv()
+                arrive(self.zl.at[0], self.mirror)
 
                 def add_mirror(at):
                     self.total[at, :] += self.zl[0, at, :].astype(F32)
@@ -767,12 +779,15 @@
                 by_rows(self.count, self.step, add_mirror)
 
     class SpreadSum:
-        def __init__(self, half, arrivals):
-            self.xs, self.xl, self.cs, self.cl, self.zs, self.zl, self.ps = (
-                getattr(s, f"{p}_qkv{half}") for p in ("xs", "xl", "cs", "cl", "zs", "zl", "ps")
-            )
-            self.half, self.arrivals = half, arrivals
-            self.along_x = {}
+        def __init__(self, half, shared):
+            staged = getattr(s, f"st_qkv{half}")
+            self.xs, self.cs, self.zs = staged.at[pl.ds(0, 4)], staged.at[4], staged.at[5]
+            self.xl, self.cl, self.zl = (getattr(s, f"{p}_qkv{half}") for p in ("xl", "cl", "zl"))
+            self.half = half
+            self.group = sends(staged.at[pl.ds(0, 4)])
+            self.inner, self.outer, self.last, self.final, self.final_mirror = shared
+            self.along_x = {k: arrivals() for k in ("mirror", "two", "own")}
+            self.crossing, self.passing = arrivals(), arrivals()
 
         def value(self, index, *extras):
             rows = BLOCK // 2
@@ -784,68 +799,72 @@
 
         def send_x(self, name, zk, *extras):
             self.xs[zk] = self.value(2 * zk + other_x, *extras).astype(BF)
-            self.along_x[name] = copy_to(self.xs.at[zk], self.xl.at[zk], x_dev)
+            copy_to(self.xs.at[zk], self.xl.at[zk], x_dev, self.along_x[name], self.group)
+
+        def arrive_x(self, name, zk):
+            arrive(self.xl.at[zk], self.along_x[name])
 
         def send_crossing(self):
             self.cs[...] = self.value(2 * z_near + other_x).astype(BF)
-            self.crossing = copy_to(self.cs, self.cl, near_dev)
+            copy_to(self.cs, self.cl, near_dev, self.crossing, self.group)
 
         def send_own(self):
-            self.crossing.wait_recv()
+            arrive(self.cl, self.crossing)
             self.send_x("own", z, self.cl[...])
 
-        def deliver(self, slot, zk, value, condition=None):
+        def deliver(self, slot, zk, value):
             for j in range(2):
                 to = 2 * self.half + j
+                at = 8 * self.half + 2 * slot + j
                 for t, tile in enumerate(fold(tiles_of(value[CHUNK * j : CHUNK * (j + 1)]))):
-                    self.ps[slot, j, :, 128 * t : 128 * (t + 1)] = tile.astype(BF)
-                copy, _ = prepare(
-                    self.ps.at[slot, j],
-                    s.fin.at[slot, d],
+                    s.ps[at, :, 128 * t : 128 * (t + 1)] = tile.astype(BF)
+                copy_to(
+                    s.ps.at[at],
+                    s.fin.at[GROUP * slot + d],
                     (2 * zk + x, to),
-                    self.arrivals + GROUP * slot + d,
+                    self.final_mirror if slot == 2 else self.final,
+                    self.inner if slot == 2 else self.last,
+                    inside if slot == 2 else d != to if slot == 3 else None,
                 )
                 if slot == 3:
-                    start(copy, d != to)
 
                     @pl.when(d == to)
-                    def _(j=j):
-                        s.fin[slot, d] = self.ps[slot, j]
-                else:
-                    start(copy, condition)
+                    def _(at=at):
+                        s.fin[GROUP * slot + d] = s.ps[at]
 
         def send_mirror(self):
-            self.along_x["mirror"].wait_recv()
+            self.arrive_x("mirror", z_mirror)
             value = self.value(2 * z_mirror + x, self.xl[z_mirror])
-            self.deliver(2, z_mirror, value, inside)
+            self.deliver(2, z_mirror, value)
             self.zs[...] = value.astype(BF)
-            self.passing, _ = prepare(self.zs, self.zl, near_dev)
-            start(self.passing, outside)
+            copy_to(self.zs, self.zl, near_dev, self.passing, self.outer, outside)
 
         def send_two(self):
-            self.along_x["two"].wait_recv()
+            self.arrive_x("two", z_two)
 
             @pl.when(outside)
             def _():
                 self.zl[...] = jnp.zeros((BLOCK // 2, PACK), BF)
 
-            pl.when(inside)(self.passing.wait_recv)
+            pl.when(inside)(lambda: arrive(self.zl, self.passing))
             self.deliver(0, z_two, self.value(2 * z_two + x, self.xl[z_two], self.zl[...]))
 
         def send_near(self):
             self.deliver(1, z_near, self.value(2 * z_near + x))
 
         def keep_own(self):
-            self.along_x["own"].wait_recv()
+            self.arrive_x("own", z)
             self.deliver(3, z, self.value(r, self.xl[z]))
 
     class GroupSum:
         def __init__(self, name, source, parts=1):
-            self.s1, self.l1, self.s2, self.l2 = (
-                getattr(s, p + name) for p in ("s1_", "l1_", "s2_", "l2_")
-            )
+            staged = getattr(s, "gs_" + name)
+            self.s1, self.s2 = staged.at[pl.ds(0, 2)], staged.at[2]
+            self.l1, self.l2 = (getattr(s, p + name) for p in ("l1_", "l2_"))
             self.source, self.parts, self.size = source, parts, OWN // parts
-            self.first, self.second = {}, {}
+            self.group = sends(staged)
+            self.first, self.second = arrivals(parts), arrivals(parts)
+            self.kept = arrivals()
 
         def block(self, index, at):
             return self.source[pl.ds(pl.multiple_of(index * OWN + at.start, at.size), at.size), :]
@@ -859,34 +878,41 @@
 
             by_rows(self.size, 32, shifted)
 
-        def send(self):
+        def send(self, i=0):
             for j, yj in enumerate((other_y, yy)):
-                for i in range(self.parts):
-
-                    def stage(at):
-                        self.s1[j, at, :] = self.block(2 * yj + other_c, at).astype(BF)
-
-                    self.over(i, stage)
-                    self.first[j, i] = copy_to(
-                        self.s1.at[j, self.part(i)], self.l1.at[j, self.part(i)], core_dev
-                    )
-
-        def middle(self):
-            for i in range(self.parts):
-                self.first[0, i].wait_recv()
 
                 def stage(at):
-                    value = self.block(2 * other_y + c, at) + self.l1[0, at, :].astype(F32)
-                    self.s2[at, :] = value.astype(BF)
+                    self.s1[j, at, :] = self.block(2 * yj + other_c, at).astype(BF)
 
                 self.over(i, stage)
-                self.second[i] = copy_to(
-                    self.s2.at[self.part(i)], self.l2.at[self.part(i)], y_dev
+                copy_to(
+                    self.s1.at[j, self.part(i)],
+                    self.l1.at[j, self.part(i)],
+                    core_dev,
+                    self.kept if j else self.first + i,
+                    self.group,
                 )
 
+        def middle(self, i=0):
+            arrive(self.l1.at[0, self.part(i)], self.first + i)
+
+            def stage(at):
+                value = self.block(2 * other_y + c, at) + self.l1[0, at, :].astype(F32)
+                self.s2[at, :] = value.astype(BF)
+
+            self.over(i, stage)
+            copy_to(
+                self.s2.at[self.part(i)],
+                self.l2.at[self.part(i)],
+                y_dev,
+                self.second + i,
+                self.group,
+            )
+
         def wait(self, i=0):
-            self.first[1, i].wait_recv()
-            self.second[i].wait_recv()
+            if i == 0:
+                arrive(self.l1.at[1], self.kept)
+            arrive(self.l2.at[self.part(i)], self.second + i)
 
         def value(self, at):
             return (
@@ -897,69 +923,73 @@
 
     class PieceGather:
         def __init__(self):
-            self.along_x = {}
-
-        def fan(self, zk, mates_only=False, condition=None):
-            copies = [None] if mates_only else []
-            for m in (core_d, y_d, far_d) if mates_only else (d, core_d, y_d, far_d):
-                copy, _ = prepare(s.qp_s.at[m], s.q_all.at[r, d], (2 * zk + x, m))
-                start(copy, condition)
-                copies.append(copy)
-            return copies
+            self.group = sends(s.q_all.at[pl.ds(0, 27)])
+            self.inner = sends(s.q_all.at[pl.ds(0, 8)], inside)
+            self.own, self.two, self.near, self.mirror = (arrivals(2) for _ in range(4))
+            self.along_x = {k: arrivals() for k in ("own", "near", "two", "mirror")}
+
+        def fan(self, zk, arrival, group, condition=None):
+            for i, m in enumerate((d, core_d, y_d, far_d)):
+                if i == 0 and zk is z:
+                    continue
+                copy_to(
+                    s.qp_s.at[m],
+                    s.q_all.at[GROUP * r + d],
+                    (2 * zk + x, m),
+                    arrival + i // 2,
+                    group,
+                    condition,
+                )
 
         def slab(self, zk, xk, h):
-            return s.q_all.at[2 * zk + xk, pl.ds(pl.multiple_of(2 * (other_y if h else yy), 2), 2)]
+            first = GROUP * (2 * zk + xk) + 2 * (other_y if h else yy)
+            return s.q_all.at[pl.ds(pl.multiple_of(first, 2), 2)]
 
         def send(self):
-            self.own = self.fan(z, mates_only=True)
-            self.two = self.fan(z_two)
-            self.near = self.fan(z_near)
-            self.mirror = self.fan(z_mirror, condition=inside)
-            self.passing = []
-            for h in range(2):
-                slab = self.slab(z_two, x, h)
-                self.passing.append(prepare(slab, slab, near_dev)[0])
+            self.fan(z, self.own, self.group)
+            self.fan(z_two, self.two, self.group)
+            self.fan(z_near, self.near, self.group)
+            self.fan(z_mirror, self.mirror, self.inner, inside)
 
         def send_x(self, name, zk, h):
             slab = self.slab(zk, x, h)
-            self.along_x[name, h] = copy_to(slab, slab, x_dev)
-
-        def wait(self, copies, h):
-            for copy in copies[2 * h : 2 * h + 2]:
-                if copy is not None:
-                    copy.wait_recv()
+            copy_to(slab, slab, x_dev, self.along_x[name], self.group)
 
         def forward_own(self, h):
-            self.wait(self.own, h)
+            if h:
+                arrive(self.slab(z, x, h), self.own + h)
+            else:
+                arrive(s.q_all.at[GROUP * r + core_d], self.own)
             self.send_x("own", z, h)
 
         def forward_near(self, h):
-            self.wait(self.near, h)
+            arrive(self.slab(z_near, x, h), self.near + h)
             self.send_x("near", z_near, h)
 
         def forward_two(self, h):
-            self.wait(self.two, h)
-            start(self.passing[h], inside)
+            slab = self.slab(z_two, x, h)
+            arrive(slab, self.two + h)
+            copy_to(slab, slab, near_dev, self.mirror + h, self.inner, inside)
             self.send_x("two", z_two, h)
 
         def forward_mirror(self, h):
-            pl.when(inside)(lambda: self.wait(self.mirror, h))
-            pl.when(outside)(self.passing[h].wait_recv)
+            arrive(self.slab(z_mirror, x, h), self.mirror + h)
             self.send_x("mirror", z_mirror, h)
 
-        def finish(self, name):
-            for h in range(2):
-                self.along_x[name, h].wait_recv()
+        def finish(self, name, zk):
+            first = pl.multiple_of(GROUP * (2 * zk + other_x), GROUP)
+            arrive(s.q_all.at[pl.ds(first, GROUP)], self.along_x[name])
 
     def assemble(landing, count, target, row):
         for k in range(GROUP):
-            tiles = [t.astype(F32) for t in tiles_of(landing[k])]
+            landed = landing[k][...] if isinstance(landing, list) else landing[k]
+            tiles = [t.astype(F32) for t in tiles_of(landed)]
             for t, tile in enumerate(unfold(tiles, count)):
                 s.tmp[CHUNK * k : CHUNK * (k + 1), 128 * t : 128 * (t + 1)] = tile
         rows_at(target, row, BLOCK)[...] = s.tmp[:, : 128 * count].astype(BF)
 
     def assemble_qkv(row):
-        assemble(s.q_all.at[row], 5, s.w_qkv, row)
+        assemble([s.q_all.at[GROUP * row + k] for k in range(GROUP)], 5, s.w_qkv, row)
 
     lane = lane_id((CHUNK, 128))
     eye = row_id((CHUNK, CHUNK)) == lane_id((CHUNK, CHUNK))
@@ -982,34 +1012,45 @@
             s.qp_s[k, :, 128 * t : 128 * (t + 1)] = tile.astype(BF)
     qkv_gather = PieceGather()
     qkv_gather.send()
-    s.q_all[r, d] = s.qp_s[d]
+    s.q_all[GROUP * r + d] = s.qp_s[d]
 
     loads["wo"].wait()
-    out_gather = Gather(lambda zk, xk: s.wo_l.at[d, xk, zk])
+    out_gather = Gather(
+        lambda zk, xk: s.wo_l.at[d, xk, zk],
+        lambda n: s.wo_l.at[0, 0, pl.ds(0, n)] if n <= 4 else s.wo_l.at[0, :, pl.ds(0, n // 2)],
+    )
     for t, tile in enumerate(fold(tiles_of(wo[...].astype(F32)))):
         s.wo_l[d, x, z, :, 128 * t : 128 * (t + 1)] = tile.astype(BF)
     out_gather.send_two()
     out_gather.send_mirror()
     out_gather.send_near()
-    out_gather.send_x()
+    out_gather.send_own_x()
 
     loads["wu"].wait()
     wu_tiles = tiles_of(wu[...].astype(F32))
     for k in range(GROUP):
         for t, tile in enumerate(fold(permute_chunks(wu_tiles, up_picks(k)))):
             s.up_s[k, :, 128 * t : 128 * (t + 1)] = tile.astype(BF)
-    up_copies = [copy_to(s.up_s.at[m], s.up_l.at[d], device) for m, device in mates]
+    up_arrival, up_group = arrivals(), sends(s.up_s.at[pl.ds(0, 3)])
+    for m, device in mates:
+        copy_to(s.up_s.at[m], s.up_l.at[d], device, up_arrival, up_group)
     s.up_l[d] = s.up_s[d]
 
     loads["x"].wait()
-    x_gather = GroupGather(lambda i: s.x_all.at[i])
+    x_gather = GroupGather(lambda i: s.x_all.at[i], lambda n: s.x_all.at[pl.ds(0, n)])
     x_gather.send()
 
     loads["wd"].wait()
-    up_gather = Gather(lambda zk, xk: rows_at(s.w_up, 2 * zk + xk, BLOCK), cross=True)
+    up_gather = Gather(
+        lambda zk, xk: rows_at(s.w_up, 2 * zk + xk, BLOCK),
+        lambda n: s.w_up.at[pl.ds(0, n * BLOCK)],
+        cross=True,
+    )
     downs = [
         Gather(
-            lambda zk, xk, h=h: rows_at(s.w_down, 2 * (2 * zk + xk) + h, BLOCK // 2), cross=h == 0
+            lambda zk, xk, h=h: rows_at(s.w_down, 2 * (2 * zk + xk) + h, BLOCK // 2),
+            lambda n: s.w_down.at[pl.ds(0, n * BLOCK // 2)],
+            cross=h == 0,
         )
         for h in range(2)
     ]
@@ -1018,7 +1059,7 @@
     )
     loads["cot"].wait()
     s.c_all[d] = dot(diagonal.astype(BF), cot[...]).astype(BF)
-    c_gather = GroupGather(lambda i: s.c_all.at[i])
+    c_gather = GroupGather(lambda i: s.c_all.at[i], lambda n: s.c_all.at[pl.ds(0, n)])
     c_gather.send()
 
     def normalize(i):
@@ -1028,9 +1069,11 @@
 
         by_rows(OWN, 64, one)
 
+    for half in downs:
+        half.send_own_x()
     qkv_gather.forward_own(0)
+    qkv_gather.forward_own(1)
     qkv_gather.forward_near(0)
-    qkv_gather.forward_own(1)
     assemble_qkv(r)
     qkv_gather.forward_two(0)
     qkv_gather.forward_near(1)
@@ -1038,8 +1081,7 @@
     qkv_gather.forward_two(1)
     out_gather.pass_two()
     assemble_qkv(2 * z_two + x)
-    for copy in up_copies:
-        copy.wait_recv()
+    arrive(s.up_l.at[pl.ds(0, 3)], up_arrival)
     assemble(s.up_l, 6, s.w_up, r)
     up_gather.send_two()
     up_gather.send_near(True)
@@ -1054,20 +1096,21 @@
     out_gather.send_x(z_two)
     out_gather.forward_near()
     out_gather.forward_mirror()
-    up_gather.send_x()
-    for half in downs:
-        half.send_x()
-    columns = [GroupGather(lambda i, xk=xk: s.wo_l.at[i, xk]) for xk in (x, other_x)]
+    up_gather.send_own_x()
+    columns = [
+        GroupGather(lambda i, xk=xk: s.wo_l.at[i, xk], lambda n: s.wo_l.at[pl.ds(0, n), 0])
+        for xk in (x, other_x)
+    ]
     columns[0].send()
     assemble_qkv(2 * z_mirror + x)
     x_gather.finish()
     for i in range(GROUP):
         normalize(i)
     for name, zk in (("own", z), ("near", z_near), ("two", z_two)):
-        qkv_gather.finish(name)
+        qkv_gather.finish(name, zk)
         assemble_qkv(2 * zk + other_x)
     c_gather.relay()
-    qkv_gather.finish("mirror")
+    qkv_gather.finish("mirror", z_mirror)
     assemble_qkv(2 * z_mirror + other_x)
 
     lane = lane_id((8, 128))
@@ -1105,7 +1148,10 @@
     half_id = lax.div(lane_id((1, 128)), jnp.int32(64))
     half_mask = [jnp.where(half_id == h, 1.0, 0.0).astype(BF) for h in range(2)]
     root = HD**-0.5
-    o_gathers = [GroupGather(lambda i, b=b: s.o_l.at[i, b]) for b in range(2)]
+    o_gathers = [
+        GroupGather(lambda i, b=b: s.o_l.at[i, b], lambda n: s.o_l.at[pl.ds(0, n), 0])
+        for b in range(2)
+    ]
 
     def attend(b):
         rows = slice(QBLOCK * b, QBLOCK * (b + 1))
@@ -1144,6 +1190,11 @@
     attend(1)
     columns[0].relay()
     attend(0)
+    for h in range(3):
+        s.probs[h, :QBLOCK, QBLOCK:] = jnp.zeros((QBLOCK, QBLOCK), F32)
+        s.k_heads[h] = s.kk[...] * head_mask[h]
+    s.v_all[:, :256] = s.qv[...]
+    s.v_all[:, 256:] = s.v01[...]
     up_gather.forward_cross()
     columns[1].relay()
     downs[1].forward_near()
@@ -1220,6 +1271,7 @@
 
             by_rows(OWN, 64, second_norm)
 
+    downs[1].forward_mirror()
     up_gather.arrive_near()
     up_gather.finish()
 
@@ -1237,7 +1289,6 @@
         s.slope[at, :] = bend
 
     by_rows(SEQ, 32, gate)
-    downs[1].forward_mirror()
 
     def gate_slope(at):
         u, bend = s.part[at, :], s.slope[at, :]
@@ -1255,51 +1306,42 @@
         cols = slice(QBLOCK * i, QBLOCK * (i + 1))
         s.g_down[cols, :] = dot(s.act[:, cols], s.dm[...], 0, 0)
     down_sum = RowSum("down", s.f_down, block_of(s.g_down), 16, True)
-    down_sum.send()
+    down_sum.send(early_near=True)
     by_rows(SEQ, 32, gate_slope)
     downs[0].arrive_near()
     for half in downs:
         half.finish()
 
-    def narrow(at):
-        value = dot(s.dm[at, :], s.w_down[...], 1, 1)
-        s.du[at, :] = (value * s.slope[at, :]).astype(BF)
-
-    by_rows(SEQ, 256, narrow)
-
-    def second_back(at):
-        s.part[at, :] = dot(s.du[at, :], s.w_up[...], 1, 1)
-
-    by_rows(SEQ, 256, second_back)
     mid_sum = GroupSum("mid", s.part, 4)
-    mid_sum.send()
-
-    for i in range(3):
+
+    def quarter(ref, i):
+        return jnp.concatenate(
+            [ref[OWN * j + 32 * i : OWN * j + 32 * (i + 1), :] for j in range(GROUP)], axis=0
+        )
+
+    def put_quarter(ref, i, value):
+        for j in range(GROUP):
+            ref[OWN * j + 32 * i : OWN * j + 32 * (i + 1), :] = value[32 * j : 32 * (j + 1)]
+
+    for i in range(4):
+        value = dot(quarter(s.dm, i), s.w_down[...], 1, 1)
+        value = (value * quarter(s.slope, i)).astype(BF)
+        put_quarter(s.du, i, value)
+        put_quarter(s.part, i, dot(value, s.w_up[...], 1, 1))
+        mid_sum.send(i)
+        if i >= 1:
+            mid_sum.middle(i - 1)
+
+    down_sum.send_mirror()
+    mid_sum.middle(3)
+    down_sum.send_own()
+
+    def up_part(i):
         cols = slice(QBLOCK * i, QBLOCK * (i + 1))
         s.g_up[cols, :] = dot(s.h2[:, cols], s.du[...], 0, 0)
-    up_sum = RowSum("up", s.f_up, block_of(s.g_up), 16, True)
-    mid_sum.middle()
-    down_sum.send_mirror()
-    up_sum.send()
-
-    def block_out(at):
-        value = dot(s.act[at, :], s.w_down[...])
-        s.part2[at, :] = value
-
+
+    up_part(0)
     s.terms2[...] = jnp.zeros((8, WIDTH), F32)
-    by_rows(SEQ, 256, block_out)
-    for i in range(GROUP):
-
-        def mix(at, i=i):
-            here = pl.ds(pl.multiple_of(OWN * i + at.start, at.size), at.size)
-            value = s.part2[here, :]
-            loss = s.c_all[i, at, :].astype(F32) * loss_scale
-            s.terms2[...] += sublane_sum(loss * value)
-            s.part2[here, :] = own_weight * hist[here, :].astype(F32) + last_weight * value
-
-        by_rows(OWN, 32, mix)
-    mix_sum = GroupSum("mix", s.part2)
-    mix_sum.send()
     s.t0[...] = jnp.zeros((8, WIDTH), F32)
 
     def second_norm_back(at):
@@ -1315,77 +1357,88 @@
         s.t0[3:4, :] += jnp.sum(grad, axis=0, keepdims=True)
         s.terms2[...] += sublane_sum(loss * value)
 
+    up_sum = RowSum("up", s.f_up, block_of(s.g_up), 16, True)
     dy_gathers = []
+    dy_group = sends(s.dyb.at[pl.ds(0, 3)])
     for i in range(4):
         mid_sum.wait(i)
         mid_sum.over(i, second_norm_back)
-        dy_gathers.append(GroupGather(lambda j, i=i: s.dyb.at[j, mid_sum.part(i)]))
+        dy_gathers.append(
+            GroupGather(
+                lambda j, i=i: s.dyb.at[j, mid_sum.part(i)],
+                lambda n: s.dyb.at[pl.ds(0, n), mid_sum.part(0)],
+                dy_group,
+            )
+        )
         dy_gathers[i].send()
-
-    down_sum.send_two()
-    down_sum.send_own()
-    mix_sum.middle()
+        if i < 2:
+            up_part(i + 1)
+        if i == 2:
+            up_sum.send(early_near=True)
+
+    def block_out(at):
+        value = dot(s.act[at, :], s.w_down[...])
+        s.part2[at, :] = value
+
+    by_rows(SEQ, 256, block_out)
+    def mix_quarter(i):
+        def mix(at):
+            here = pl.ds(pl.multiple_of(OWN * i + at.start, at.size), at.size)
+            value = s.part2[here, :]
+            loss = s.c_all[i, at, :].astype(F32) * loss_scale
+            s.terms2[...] += sublane_sum(loss * value)
+            s.part2[here, :] = own_weight * hist[here, :].astype(F32) + last_weight * value
+
+        by_rows(OWN, 32, mix)
+
+    dy_gathers[0].relay()
+    mix_quarter(0)
+    mix_quarter(1)
+    dy_gathers[1].relay()
+    mix_quarter(2)
+    mix_quarter(3)
+    mix_sum = GroupSum("mix", s.part2)
+    mix_sum.send()
     lane = lane_id((8, 128))
     own_term = jnp.sum(jnp.sum(s.terms[...], axis=0, keepdims=True), axis=1, keepdims=True)
     last_term = jnp.sum(jnp.sum(s.terms2[...], axis=0, keepdims=True), axis=1, keepdims=True)
     s.u0[...] = jnp.where(lane == d, own_term, jnp.where(lane == GROUP, last_term, 0.0))
-    depth_x = copy_to(s.u0, s.u1, x_dev)
-    for i, one in enumerate(dy_gathers):
-        one.relay()
+    depth_x, depth_z, depth_d = (arrivals() for _ in range(3))
+    depth_group = sends(s.uzd.at[pl.ds(0, 7)])
+    copy_to(s.u0, s.u1, x_dev, depth_x, depth_group)
+    down_sum.send_two()
+
+    lane = lane_id((1, 384))
+    head_lanes = [jnp.where(lax.div(lane, jnp.int32(64)) == 4 + h, 1.0, 0.0) for h in range(2)]
+    head_lanes = [m.astype(BF) for m in head_lanes + [jnp.where(lane < 256, 1.0, 0.0)]]
+    for i in range(4):
+        dy_gathers[i].finish()
+        rows = s.dyb[:, 32 * i : 32 * (i + 1), :].reshape(OWN, WIDTH)
+        grad = dot(rows, s.w_own[...], 1, 1).astype(BF)
+        grad = jnp.concatenate([grad * m for m in head_lanes], axis=0)
+        probs = jnp.concatenate([quarter(s.probs.at[h], i) for h in range(3)], axis=0)
+        dp = dot(grad, s.v_all[...], 1, 1)
+        delta = jnp.sum(dp * probs, axis=1, keepdims=True)
+        ds = (probs * (dp - delta)).astype(BF)
+        query = quarter(s.qv, i)
+        query = jnp.concatenate([query * m for m in head_mask], axis=0)
+        dk = dot(ds, query, 0, 0) * root
+        dv = dot(probs.astype(BF), grad, 0, 0)
         if i == 0:
+            s.dk[...] = dk
+            s.dv[...] = dv
+        else:
+            s.dk[...] += dk
+            s.dv[...] += dv
+        dq = sum(dot(ds[OWN * h : OWN * (h + 1)], s.k_heads[h]) for h in range(3))
+        put_quarter(s.dq, i, dq * root)
+        if i < 2:
+            dy_gathers[i + 2].relay()
+        if i == 1:
+            mix_sum.middle()
+        if i == 2:
             up_sum.send_mirror()
-    for one in dy_gathers:
-        one.finish()
-    up_sum.send_own()
-    down_sum.send_near()
-
-    by_group = s.dyb[...].reshape(SEQ, WIDTH)
-
-    s.dob[...] = dot(by_group, s.w_own[...], 1, 1).astype(BF)
-    for b in range(2):
-        rows = slice(QBLOCK * b, QBLOCK * (b + 1))
-        keys = QBLOCK * (b + 1)
-        query = s.qv[rows, :]
-        dq = jnp.zeros((QBLOCK, 256), F32)
-        for h in range(3):
-            probs = s.probs[h, rows, :keys]
-            if h < 2:
-                grad = s.dob[rows, 256:] * half_mask[h]
-                dp = dot(grad, s.v01[:keys, :], 1, 1)
-            else:
-                grad = s.dob[rows, :256]
-                dp = dot(grad, s.qv[:keys, :], 1, 1)
-            delta = jnp.sum(dp * probs, axis=1, keepdims=True)
-            ds = (probs * (dp - delta)).astype(BF)
-            dq = dq + dot(ds, s.kk[:keys, :] * head_mask[h])
-            dk = dot(ds, query * head_mask[h], 0, 0) * root
-            dv = dot(probs.astype(BF), grad, 0, 0)
-            cols = slice(256, 384) if h < 2 else slice(0, 256)
-            if b == 0:
-                old, new = slice(0, QBLOCK), None
-            else:
-                old, new = slice(0, QBLOCK), slice(QBLOCK, SEQ)
-            if h == 0 and b == 0:
-                s.dk[old, :] = dk[:QBLOCK]
-            else:
-                s.dk[old, :] += dk[:QBLOCK]
-            if b == 0 and h != 1:
-                s.dv[old, cols] = dv[:QBLOCK]
-            else:
-                s.dv[old, cols] += dv[:QBLOCK]
-            if new is not None:
-                if h == 0:
-                    s.dk[new, :] = dk[QBLOCK:]
-                else:
-                    s.dk[new, :] += dk[QBLOCK:]
-                if h != 1:
-                    s.dv[new, cols] = dv[QBLOCK:]
-                else:
-                    s.dv[new, cols] += dv[QBLOCK:]
-        s.dq[rows, :] = dq * root
-        if b == 0:
-            up_sum.send_two()
-            up_sum.send_near()
+            up_sum.send_own()
 
     def turn_back(at):
         co, si = cosine[at, :], sine[at, :]
@@ -1402,18 +1455,23 @@
     for i in range(3):
         cols = slice(QBLOCK * i, QBLOCK * (i + 1))
         s.g_qkv[cols, :] = dot(s.h1[:, cols], s.dqkv[...], 0, 0)
-    qkv_arrivals = reserve(16)
-    sums = [SpreadSum(h, qkv_arrivals) for h in range(2)]
+    shared = (
+        sends(s.fin.at[pl.ds(0, 4)], inside),
+        sends(s.st_qkv0.at[pl.ds(0, 2)], outside),
+        sends(s.fin.at[pl.ds(0, 11)]),
+        arrivals(),
+        arrivals(),
+    )
+    sums = [SpreadSum(h, shared) for h in range(2)]
     for one in sums:
         one.send_x("mirror", z_mirror)
         one.send_crossing()
     for one in sums:
         one.send_x("two", z_two)
-    depth_x.wait_recv()
-    s.uz[z] = s.u0[...] + s.u1[...]
-    depth_z = [
-        copy_to(s.uz.at[z], s.uz.at[z], device) for device in (two_dev, mirror_dev, near_dev)
-    ]
+    arrive(s.u1, depth_x)
+    s.uzd[z] = s.u0[...] + s.u1[...]
+    for device in (two_dev, mirror_dev, near_dev):
+        copy_to(s.uzd.at[z], s.uzd.at[z], device, depth_z, depth_group)
 
     def first_back(at):
         s.part[at, :] = dot(s.dqkv[at, :], s.w_qkv[...], 1, 1)
@@ -1433,7 +1491,9 @@
     s.t0[0:1, :] = jnp.sum(s.gain_sum[...], axis=0, keepdims=True)
     s.t0[1:2, :] = jnp.sum(s.shift_sum[...], axis=0, keepdims=True)
     s.td[d] = s.t0[...]
-    norm_copies = [copy_to(s.td.at[d], s.td.at[d], device) for m, device in mates]
+    norm_arrival, norm_group = arrivals(), sends(s.td.at[pl.ds(0, 3)])
+    for m, device in mates:
+        copy_to(s.td.at[d], s.td.at[d], device, norm_arrival, norm_group)
     in_sum.middle()
     for p in range(3):
         cols = slice(QBLOCK * p, QBLOCK * (p + 1))
@@ -1444,10 +1504,10 @@
                 if out_place(head) == place:
                     s.g_out[64 * head : 64 * head + 64, :] = value[64 * i : 64 * i + 64]
 
+    up_sum.send_two()
     for one in sums:
         one.send_mirror()
-    for copy in norm_copies:
-        copy.wait_recv()
+    arrive(s.td.at[pl.ds(0, 3)], norm_arrival)
     value = (s.td[0] + s.td[1]) + (s.td[2] + s.td[3])
     value = pltpu.roll(value, lax.rem(WIDTH - CHUNK * d, WIDTH), 1)
     for i in range(ROWS):
@@ -1462,48 +1522,43 @@
 
     out_sum = RowSum("out", s.f_out, out_block, 16, False)
     out_sum.send()
+    for one in sums:
+        one.send_own()
+
     down_sum.finish()
     gd_o[...] = s.f_down[...]
     store(6)
-    mix_sum.wait()
-
-    def write_out(at):
-        here = pl.ds(pl.multiple_of(OWN * d + at.start, at.size), at.size)
-        out_o[at, :] = (mix_sum.value(at) + last_weight * s.y[here, :]).astype(BF)
-
-    by_rows(OWN, 32, write_out)
-    store(0)
-
     def spread(total, staged, landing):
-        copies = []
+        arrival, group = arrivals(), sends(staged.at[pl.ds(0, 3)])
         for m, device in mates:
             rows = total[pl.ds(pl.multiple_of(CHUNK * m, CHUNK), CHUNK), :]
             for t, tile in enumerate(fold(tiles_of(rows))):
                 staged[m, :, 128 * t : 128 * (t + 1)] = tile.astype(BF)
-            copies.append(copy_to(staged.at[m], landing.at[d], device))
+            copy_to(staged.at[m], landing.at[d], device, arrival, group)
         rows = total[pl.ds(pl.multiple_of(CHUNK * d, CHUNK), CHUNK), :]
         for t, tile in enumerate(fold(tiles_of(rows))):
             landing[d, :, 128 * t : 128 * (t + 1)] = tile.astype(BF)
-        return copies
-
-    def collect(copies, landing, count, back, target):
-        for copy in copies:
-            copy.wait_recv()
+        return arrival
+
+    def collect(arrival, landing, count, back, target):
+        arrive(landing.at[pl.ds(0, 3)], arrival)
         tiles = []
         for k in range(GROUP):
             tiles += unfold([t.astype(F32) for t in tiles_of(landing[k])], count)
         for t, tile in enumerate(permute_chunks(tiles, back)):
             target[:, 128 * t : 128 * (t + 1)] = tile
 
-    up_sum.finish()
-    up_spread = spread(s.f_up, s.b_up, s.a_up)
-    for one in sums:
-        one.send_two()
-    for one in sums:
-        one.send_near()
-    for one in sums:
-        one.send_own()
+    mix_sum.wait()
+
+    def write_out(at):
+        here = pl.ds(pl.multiple_of(OWN * d + at.start, at.size), at.size)
+        out_o[at, :] = (mix_sum.value(at) + last_weight * s.y[here, :]).astype(BF)
+
+    by_rows(OWN, 32, write_out)
+    store(0)
+
     in_sum.wait()
+    out_sum.send_mirror()
 
     def first_norm_back(at):
         grad = in_sum.value(at)
@@ -1513,44 +1568,36 @@
 
     by_rows(OWN, 32, first_norm_back)
     store(1)
-    out_sum.send_mirror()
-    for copy in depth_z:
-        copy.wait_recv()
-    s.ud[d] = (s.uz[0] + s.uz[1]) + (s.uz[2] + s.uz[3])
-    depth_d = [copy_to(s.ud.at[d], s.ud.at[d], device) for m, device in mates]
+    for one in sums:
+        one.send_two()
+    for one in sums:
+        one.send_near()
+    arrive(s.uzd.at[pl.ds(0, 3)], depth_z)
+    s.uzd[4 + d] = (s.uzd[0] + s.uzd[1]) + (s.uzd[2] + s.uzd[3])
+    for m, device in mates:
+        copy_to(s.uzd.at[4 + d], s.uzd.at[4 + d], device, depth_d, depth_group)
     out_sum.send_near()
     for one in sums:
         one.keep_own()
+    up_sum.finish()
+    up_spread = spread(s.f_up, s.b_up, s.a_up)
+    out_sum.send_two()
     collect(up_spread, s.a_up, 6, UP_BACK, gu_o)
     store(5)
-    out_sum.send_two()
-    for copy in depth_d:
-        copy.wait_recv()
-    dg_o[...] = (s.ud[0] + s.ud[1]) + (s.ud[2] + s.ud[3])
-
-    def arrived(slot, k):
-        return pltpu.make_async_remote_copy(
-            src_ref=s.fin.at[slot, k],
-            dst_ref=s.fin.at[slot, k],
-            send_sem=send_sems.at[0],
-            recv_sem=recv_sems.at[qkv_arrivals + GROUP * slot + k],
-            device_id=x_dev,
-            device_id_type=MESH,
-        )
-
+    arrive(s.uzd.at[pl.ds(0, 3)], depth_d)
+    dg_o[...] = (s.uzd[4] + s.uzd[5]) + (s.uzd[6] + s.uzd[7])
+
+    arrive(s.fin.at[pl.ds(0, 11)], shared[3])
     for k in range(GROUP):
-        pl.when(d != k)(arrived(3, k).wait_recv)
-        arrived(1, k).wait_recv()
-        arrived(0, k).wait_recv()
         s.q_sum[k] = (
-            s.fin[3, k].astype(F32) + s.fin[1, k].astype(F32) + s.fin[0, k].astype(F32)
+            s.fin[12 + k].astype(F32) + s.fin[4 + k].astype(F32) + s.fin[k].astype(F32)
         )
 
     @pl.when(inside)
     def _():
+        arrive(s.fin.at[pl.ds(0, 4)], shared[4])
         for k in range(GROUP):
-            arrived(2, k).wait_recv()
-            s.q_sum[k] += s.fin[2, k].astype(F32)
+            s.q_sum[k] += s.fin[8 + k].astype(F32)
 
     tiles = []
     for k in range(GROUP):
@@ -1565,11 +1612,13 @@
     store(4)
     for copy in stores:
         copy.wait()
-    for copy, condition in sent:
+    for group, view, condition in send_groups:
+        wait = prepare(view, view, x_dev, 0, group).wait_send
         if condition is None:
-            copy.wait_send()
+            wait()
         else:
-            pl.when(condition)(copy.wait_send)
+            pl.when(condition)(wait)
+    assert used["send"] <= N_SENDS and used["arrival"] <= N_ARRIVALS, used
 
 
 def finish_kernel(*refs):
@@ -1626,8 +1675,7 @@
         in_specs=[hbm] * 3 + [vmem] + [hbm] * 4 + [vmem, smem] + [hbm] * 2,
         out_specs=[hbm] * 7 + [vmem] * 2,
         scratch_shapes=[pltpu.VMEM(dims, kind) for dims, kind in SCRATCH.values()]
-        + [pltpu.SemaphoreType.DMA((N_SEMS,))] * 2
-        + [pltpu.SemaphoreType.DMA((16,))],
+        + [pltpu.SemaphoreType.DMA((n,)) for n in (N_SENDS, N_ARRIVALS, 16)],
         compiler_params=pltpu.CompilerParams(
             collective_id=0, has_side_effects=True, vmem_limit_bytes=VMEM_MIB * 2**20
         ),

time: 103 us -> 97 us (0.942)
  Pallas kernels: 102 us -> 96 us
    pallas_call x1, Pallas kernels: 98 us -> 92.1 us  [fused(): pl.pallas_call(fused_kernel, out_shape=shapes, in_specs=[hbm] * 3 + [vmem...]
where the time goes in v4:
time: 97 us; the launch traced here: 96.8 us
  Pallas kernels  96 us (99%)
    pallas_call x1, Pallas kernels, fused(): pl.pallas_call(fused_kernel, out_shape=shapes, in_specs=[hbm] * 3 + [vmem...  92.1 us
    pallas_call x1, Pallas kernels, fused(): pl.pallas_call(finish_kernel, out_shape=shapes[:7] + (shape((4, CHUNK), F...  3.9 us

profile of v4, /device:TPU:0, one launch (start us, length us, event | category | flops | bytes accessed | tf_op | source)
XLA Modules:
  0.0 96.8 jit_solution(16244408441737345441)
XLA Ops:
  0.6 92.1 %shard_map.187 = (bf16[128,768]{1,0:T(8,128)(2,1)}, bf16[128,768]{1,0:T(8,128)(2,1)}, bf16[512,768]{1,0:T(8,128)(2,1)}, f32[24,2304]{1,0:T(8,128)}, f32[24,768]{...) custom-call(bf16[128,768]{1,0:T(8,128)(2,1)} %refs_0_.1, ...), custom_call_target="tpu_custom_call" | custom-call | flops 12000000000 | bytes 4000000 | tf_op jit(solution)/shard_map/pallas_call | solution.py:1672
  92.7 3.9 %shard_map.188 = (bf16[128,768]{1,0:T(8,128)(2,1)}, bf16[128,768]{1,0:T(8,128)(2,1)}, bf16[512,768]{1,0:T(8,128)(2,1)}, f32[24,2304]{1,0:T(8,128)}, f32[24,768]{...) custom-call(bf16[128,768]{1,0:T(8,128)(2,1)} %get-tuple-element.27.refs_0_, ...), custom_call_target="tpu_custom_call" | custom-call | tf_op jit(solution)/shard_map/pallas_call | solution.py:1697

commit v5 on v4

--- a/solution.py
+++ b/solution.py
@@ -402,13 +402,6 @@
     wu=((CHUNK, 4 * WIDTH), BF),
     cosine=((SEQ, 128), F32),
     sine=((SEQ, 128), F32),
-    r_0=((OWN, WIDTH), BF),
-    r_1=((OWN, WIDTH), BF),
-    r_2=((SEQ, WIDTH), BF),
-    r_3=((CHUNK, 3 * WIDTH), F32),
-    r_4=((CHUNK, WIDTH), F32),
-    r_5=((CHUNK, 4 * WIDTH), F32),
-    r_6=((BLOCK, WIDTH), F32),
     x_all=((GROUP, OWN, WIDTH), BF),
     c_all=((GROUP, OWN, WIDTH), BF),
     qp_s=((GROUP, 16, 1024), BF),
@@ -562,6 +555,14 @@
 
         lax.fori_loop(0, count // step, one, 0)
 
+    barrier = pltpu.get_barrier_semaphore()
+    partners = [x_dev, core_dev, y_dev, far_dev]
+    partners += [
+        (2 * zk + x, m) for zk in (z_two, z_mirror, z_near) for m in (d, core_d, y_d, far_d)
+    ]
+    for device in partners:
+        pl.semaphore_signal(barrier, inc=1, device_id=device, device_id_type=MESH)
+
     hist, cot, wq, wo, wu, cosine, sine = s.hist, s.cot, s.wq, s.wo, s.wu, s.cosine, s.sine
     loads = {}
     for name, source, target in (
@@ -577,26 +578,8 @@
     ):
         loads[name] = pltpu.make_async_copy(source, target, local_sems.at[len(loads)])
         loads[name].start()
-    out_o, ig_o, hg_o, gq_o, go_o, gu_o, gd_o = (
-        getattr(s, f"r_{i}") for i in range(N_OUT - 2)
-    )
-    stores = []
-
-    def store(i):
-        copy = pltpu.make_async_copy(
-            getattr(s, f"r_{i}"), results[i], local_sems.at[len(loads) + i]
-        )
-        copy.start()
-        stores.append(copy)
-
-    barrier = pltpu.get_barrier_semaphore()
-    partners = [x_dev, core_dev, y_dev, far_dev]
-    partners += [
-        (2 * zk + x, m) for zk in (z_two, z_mirror, z_near) for m in (d, core_d, y_d, far_d)
-    ]
-    for device in partners:
-        pl.semaphore_signal(barrier, inc=1, device_id=device, device_id_type=MESH)
-    pl.semaphore_wait(barrier, len(partners))
+    out_o, ig_o, hg_o, gq_o, go_o, gu_o, gd_o = results
+
 
     class Gather:
         def __init__(self, piece, pieces, cross=False):
@@ -732,19 +715,20 @@
             copy_to(self.zs[0], self.zl.at[0], mirror_dev, self.mirror, self.group, inside)
             copy_to(self.zs[0], self.zl.at[2], near_dev, self.passing, self.group, outside)
 
-        def send_two(self):
-            self.arrive_x("two", z_two)
-
+        def send_two_outside(self):
+            @pl.when(outside)
+            def _():
+                self.arrive_x("two", z_two)
+                self.stage(self.zs[1], 2 * z_two + x, self.xl.at[z_two])
+                copy_to(self.zs[1], self.zl.at[1], two_dev, self.two, self.group)
+
+        def send_two_inside(self):
             @pl.when(inside)
             def _():
+                self.arrive_x("two", z_two)
                 arrive(self.zl.at[2], self.passing)
                 self.stage(self.zs[1], 2 * z_two + x, self.xl.at[z_two], self.zl.at[2])
-
-            @pl.when(outside)
-            def _():
-                self.stage(self.zs[1], 2 * z_two + x, self.xl.at[z_two])
-
-            copy_to(self.zs[1], self.zl.at[1], two_dev, self.two, self.group)
+                copy_to(self.zs[1], self.zl.at[1], two_dev, self.two, self.group)
 
         def send_near(self):
             extras = ()
@@ -786,7 +770,7 @@
             self.half = half
             self.group = sends(staged.at[pl.ds(0, 4)])
             self.inner, self.outer, self.last, self.final, self.final_mirror = shared
-            self.along_x = {k: arrivals() for k in ("mirror", "two", "own")}
+            self.along_x = {k: arrivals() for k in ("mirror", "two", "near", "own")}
             self.crossing, self.passing = arrivals(), arrivals()
 
         def value(self, index, *extras):
@@ -805,12 +789,20 @@
             arrive(self.xl.at[zk], self.along_x[name])
 
         def send_crossing(self):
-            self.cs[...] = self.value(2 * z_near + other_x).astype(BF)
-            copy_to(self.cs, self.cl, near_dev, self.crossing, self.group)
-
-        def send_own(self):
-            arrive(self.cl, self.crossing)
-            self.send_x("own", z, self.cl[...])
+            @pl.when(inside)
+            def _():
+                self.cs[...] = self.value(2 * z_near + other_x).astype(BF)
+                copy_to(self.cs, self.cl, near_dev, self.crossing, self.group)
+
+        def send_third(self):
+            pl.when(inside)(lambda: self.send_x("own", z))
+            pl.when(outside)(lambda: self.send_x("near", z_near))
+
+        def send_own_outside(self):
+            @pl.when(outside)
+            def _():
+                arrive(self.cl, self.crossing)
+                self.send_x("own", z, self.cl[...])
 
         def deliver(self, slot, zk, value):
             for j in range(2):
@@ -850,7 +842,12 @@
             self.deliver(0, z_two, self.value(2 * z_two + x, self.xl[z_two], self.zl[...]))
 
         def send_near(self):
-            self.deliver(1, z_near, self.value(2 * z_near + x))
+            pl.when(inside)(lambda: self.deliver(1, z_near, self.value(2 * z_near + x)))
+
+            @pl.when(outside)
+            def _():
+                self.arrive_x("near", z_near)
+                self.deliver(1, z_near, self.value(2 * z_near + x, self.xl[z_near]))
 
         def keep_own(self):
             self.arrive_x("own", z)
@@ -1010,37 +1007,40 @@
         tiles[2] = tiles[2] + extra
         for t, tile in enumerate(fold(tiles)):
             s.qp_s[k, :, 128 * t : 128 * (t + 1)] = tile.astype(BF)
-    qkv_gather = PieceGather()
-    qkv_gather.send()
     s.q_all[GROUP * r + d] = s.qp_s[d]
-
     loads["wo"].wait()
-    out_gather = Gather(
-        lambda zk, xk: s.wo_l.at[d, xk, zk],
-        lambda n: s.wo_l.at[0, 0, pl.ds(0, n)] if n <= 4 else s.wo_l.at[0, :, pl.ds(0, n // 2)],
-    )
     for t, tile in enumerate(fold(tiles_of(wo[...].astype(F32)))):
         s.wo_l[d, x, z, :, 128 * t : 128 * (t + 1)] = tile.astype(BF)
-    out_gather.send_two()
-    out_gather.send_mirror()
-    out_gather.send_near()
-    out_gather.send_own_x()
-
     loads["wu"].wait()
     wu_tiles = tiles_of(wu[...].astype(F32))
     for k in range(GROUP):
         for t, tile in enumerate(fold(permute_chunks(wu_tiles, up_picks(k)))):
             s.up_s[k, :, 128 * t : 128 * (t + 1)] = tile.astype(BF)
+    s.up_l[d] = s.up_s[d]
+    diagonal = jnp.where(
+        row_id((OWN, OWN)) == lane_id((OWN, OWN)), jnp.broadcast_to(mask_row, (OWN, OWN)), 0.0
+    )
+    loads["cot"].wait()
+    s.c_all[d] = dot(diagonal.astype(BF), cot[...]).astype(BF)
+    loads["x"].wait()
+    loads["wd"].wait()
+    pl.semaphore_wait(barrier, len(partners))
+
+    qkv_gather = PieceGather()
+    qkv_gather.send()
+    out_gather = Gather(
+        lambda zk, xk: s.wo_l.at[d, xk, zk],
+        lambda n: s.wo_l.at[0, 0, pl.ds(0, n)] if n <= 4 else s.wo_l.at[0, :, pl.ds(0, n // 2)],
+    )
+    out_gather.send_two()
+    out_gather.send_mirror()
+    out_gather.send_near()
+    out_gather.send_own_x()
     up_arrival, up_group = arrivals(), sends(s.up_s.at[pl.ds(0, 3)])
     for m, device in mates:
         copy_to(s.up_s.at[m], s.up_l.at[d], device, up_arrival, up_group)
-    s.up_l[d] = s.up_s[d]
-
-    loads["x"].wait()
     x_gather = GroupGather(lambda i: s.x_all.at[i], lambda n: s.x_all.at[pl.ds(0, n)])
     x_gather.send()
-
-    loads["wd"].wait()
     up_gather = Gather(
         lambda zk, xk: rows_at(s.w_up, 2 * zk + xk, BLOCK),
         lambda n: s.w_up.at[pl.ds(0, n * BLOCK)],
@@ -1054,11 +1054,6 @@
         )
         for h in range(2)
     ]
-    diagonal = jnp.where(
-        row_id((OWN, OWN)) == lane_id((OWN, OWN)), jnp.broadcast_to(mask_row, (OWN, OWN)), 0.0
-    )
-    loads["cot"].wait()
-    s.c_all[d] = dot(diagonal.astype(BF), cot[...]).astype(BF)
     c_gather = GroupGather(lambda i: s.c_all.at[i], lambda n: s.c_all.at[pl.ds(0, n)])
     c_gather.send()
 
@@ -1238,7 +1233,6 @@
 
         by_rows(OWN, 32, loss_rows)
 
-    store(2)
     downs[1].forward_two()
     for b in (1, 0):
         if b == 0:
@@ -1374,7 +1368,7 @@
         if i < 2:
             up_part(i + 1)
         if i == 2:
-            up_sum.send(early_near=True)
+            up_sum.send()
 
     def block_out(at):
         value = dot(s.act[at, :], s.w_down[...])
@@ -1391,6 +1385,7 @@
 
         by_rows(OWN, 32, mix)
 
+    down_sum.send_two_outside()
     dy_gathers[0].relay()
     mix_quarter(0)
     mix_quarter(1)
@@ -1406,7 +1401,7 @@
     depth_x, depth_z, depth_d = (arrivals() for _ in range(3))
     depth_group = sends(s.uzd.at[pl.ds(0, 7)])
     copy_to(s.u0, s.u1, x_dev, depth_x, depth_group)
-    down_sum.send_two()
+    down_sum.send_two_inside()
 
     lane = lane_id((1, 384))
     head_lanes = [jnp.where(lax.div(lane, jnp.int32(64)) == 4 + h, 1.0, 0.0) for h in range(2)]
@@ -1435,10 +1430,11 @@
         if i < 2:
             dy_gathers[i + 2].relay()
         if i == 1:
+            up_sum.send_mirror()
             mix_sum.middle()
         if i == 2:
-            up_sum.send_mirror()
             up_sum.send_own()
+            up_sum.send_near()
 
     def turn_back(at):
         co, si = cosine[at, :], sine[at, :]
@@ -1452,6 +1448,7 @@
         s.dqkv[at, 512:] = s.dv[at, 256:].astype(BF)
 
     by_rows(SEQ, 64, turn_back)
+    up_sum.send_two_outside()
     for i in range(3):
         cols = slice(QBLOCK * i, QBLOCK * (i + 1))
         s.g_qkv[cols, :] = dot(s.h1[:, cols], s.dqkv[...], 0, 0)
@@ -1468,6 +1465,8 @@
         one.send_crossing()
     for one in sums:
         one.send_x("two", z_two)
+    for one in sums:
+        one.send_third()
     arrive(s.u1, depth_x)
     s.uzd[z] = s.u0[...] + s.u1[...]
     for device in (two_dev, mirror_dev, near_dev):
@@ -1479,6 +1478,7 @@
     by_rows(SEQ, 256, first_back)
     in_sum = GroupSum("in", s.part)
     in_sum.send()
+    up_sum.send_two_inside()
     s.gain_sum[...] = jnp.zeros((8, WIDTH), F32)
     s.shift_sum[...] = jnp.zeros((8, WIDTH), F32)
 
@@ -1504,7 +1504,6 @@
                 if out_place(head) == place:
                     s.g_out[64 * head : 64 * head + 64, :] = value[64 * i : 64 * i + 64]
 
-    up_sum.send_two()
     for one in sums:
         one.send_mirror()
     arrive(s.td.at[pl.ds(0, 3)], norm_arrival)
@@ -1521,13 +1520,15 @@
         return jnp.concatenate(fold(tiles) + [s.ext[index]], axis=1)
 
     out_sum = RowSum("out", s.f_out, out_block, 16, False)
-    out_sum.send()
+    out_sum.send_x("mirror", z_mirror)
+    out_sum.send_x("two", z_two)
     for one in sums:
-        one.send_own()
+        one.send_own_outside()
+    out_sum.send_x("near", z_near)
+    out_sum.send_x("own", z)
 
     down_sum.finish()
     gd_o[...] = s.f_down[...]
-    store(6)
     def spread(total, staged, landing):
         arrival, group = arrivals(), sends(staged.at[pl.ds(0, 3)])
         for m, device in mates:
@@ -1555,10 +1556,11 @@
         out_o[at, :] = (mix_sum.value(at) + last_weight * s.y[here, :]).astype(BF)
 
     by_rows(OWN, 32, write_out)
-    store(0)
-
+
+    for one in sums:
+        one.send_two()
+    out_sum.send_mirror()
     in_sum.wait()
-    out_sum.send_mirror()
 
     def first_norm_back(at):
         grad = in_sum.value(at)
@@ -1567,23 +1569,19 @@
         ig_o[at, :] = (s.dy[at, :] + back).astype(BF)
 
     by_rows(OWN, 32, first_norm_back)
-    store(1)
-    for one in sums:
-        one.send_two()
     for one in sums:
         one.send_near()
+    up_sum.finish()
+    up_spread = spread(s.f_up, s.b_up, s.a_up)
     arrive(s.uzd.at[pl.ds(0, 3)], depth_z)
     s.uzd[4 + d] = (s.uzd[0] + s.uzd[1]) + (s.uzd[2] + s.uzd[3])
     for m, device in mates:
         copy_to(s.uzd.at[4 + d], s.uzd.at[4 + d], device, depth_d, depth_group)
-    out_sum.send_near()
     for one in sums:
         one.keep_own()
-    up_sum.finish()
-    up_spread = spread(s.f_up, s.b_up, s.a_up)
-    out_sum.send_two()
-    collect(up_spread, s.a_up, 6, UP_BACK, gu_o)
-    store(5)
+    out_sum.send_two_outside()
+    out_sum.send_two_inside()
+    out_sum.send_near()
     arrive(s.uzd.at[pl.ds(0, 3)], depth_d)
     dg_o[...] = (s.uzd[4] + s.uzd[5]) + (s.uzd[6] + s.uzd[7])
 
@@ -1604,14 +1602,11 @@
         tiles += unfold(tiles_of(s.q_sum[k]), 5)
     for t, tile in enumerate(permute_chunks(tiles, QKV_BACK)):
         gq_o[:, 128 * t : 128 * (t + 1)] = tile
-    store(3)
+    collect(up_spread, s.a_up, 6, UP_BACK, gu_o)
     out_sum.finish()
     for t, tile in enumerate(unfold(tiles_of(s.f_out[:, :1152]), 6)):
         go_o[:, 128 * t : 128 * (t + 1)] = tile
     ng_o[...] = s.f_out[:8, 1152:]
-    store(4)
-    for copy in stores:
-        copy.wait()
     for group, view, condition in send_groups:
         wait = prepare(view, view, x_dev, 0, group).wait_send
         if condition is None:
@@ -1625,19 +1620,13 @@
     count = N_OUT - 2
     ins, refs = refs[:count], refs[count:]
     (norm, depth), refs = refs[:2], refs[2:]
-    outs, (norm_o, depth_o), refs = refs[:count], refs[count : count + 2], refs[count + 2 :]
-    held, sems = refs[:-1], refs[-1]
-    first = [pltpu.make_async_copy(a, b, sems.at[i]) for i, (a, b) in enumerate(zip(ins, held))]
-    for copy in first:
+    outs, (norm_o, depth_o), sems = refs[:count], refs[count : count + 2], refs[-1]
+    copies = [pltpu.make_async_copy(a, b, sems.at[i]) for i, (a, b) in enumerate(zip(ins, outs))]
+    for copy in copies:
         copy.start()
     norm_o[...] = norm[:4, :CHUNK]
     depth_o[...] = depth[:1, : GROUP + 1]
-    second = []
-    for i, copy in enumerate(first):
-        copy.wait()
-        second.append(pltpu.make_async_copy(held[i], outs[i], sems.at[count + i]))
-        second[i].start()
-    for copy in second:
+    for copy in copies:
         copy.wait()
 
 
@@ -1671,11 +1660,11 @@
     )
     outs = pl.pallas_call(
         fused_kernel,
-        out_shape=shapes,
+        out_shape=tuple(pltpu.VMEM(one.shape, one.dtype) for one in shapes),
         in_specs=[hbm] * 3 + [vmem] + [hbm] * 4 + [vmem, smem] + [hbm] * 2,
-        out_specs=[hbm] * 7 + [vmem] * 2,
+        out_specs=[vmem] * 9,
         scratch_shapes=[pltpu.VMEM(dims, kind) for dims, kind in SCRATCH.values()]
-        + [pltpu.SemaphoreType.DMA((n,)) for n in (N_SENDS, N_ARRIVALS, 16)],
+        + [pltpu.SemaphoreType.DMA((n,)) for n in (N_SENDS, N_ARRIVALS, 9)],
         compiler_params=pltpu.CompilerParams(
             collective_id=0, has_side_effects=True, vmem_limit_bytes=VMEM_MIB * 2**20
         ),
@@ -1697,11 +1686,10 @@
     held = pl.pallas_call(
         finish_kernel,
         out_shape=shapes[:7] + (shape((4, CHUNK), F32), shape((1, GROUP + 1), F32)),
-        in_specs=[hbm] * 7 + [vmem] * 2,
+        in_specs=[vmem] * 9,
         out_specs=[hbm] * 7 + [vmem] * 2,
-        scratch_shapes=[pltpu.VMEM(one.shape, one.dtype) for one in shapes[:7]]
-        + [pltpu.SemaphoreType.DMA((14,))],
-        compiler_params=pltpu.CompilerParams(vmem_limit_bytes=VMEM_MIB * 2**20),
+        scratch_shapes=[pltpu.SemaphoreType.DMA((7,))],
+        compiler_params=pltpu.CompilerParams(vmem_limit_bytes=4 * 2**20),
     )(*outs)
     out, input_grad, history_grad, *grads, g_depth = held
     return (out, input_grad, history_grad.reshape(1, SEQ, WIDTH), *grads, g_depth.reshape(GROUP + 1))

time: 97 us -> 90.8 us (0.936)
  Pallas kernels: 96 us -> 89.8 us
    pallas_call x1, Pallas kernels: 92.1 us -> 87.9 us  [fused(): pl.pallas_call(fused_kernel, out_shape=tuple((pltpu.VMEM(one.shape, one.d...]
    pallas_call x1, Pallas kernels: 3.9 us -> 1.94 us  [fused(): pl.pallas_call(finish_kernel, out_shape=shapes[:7] + (shape((4, CHUNK), F...]
where the time goes in v5:
time: 90.8 us; the launch traced here: 90.6 us
  Pallas kernels  89.8 us (99%)
    pallas_call x1, Pallas kernels, fused(): pl.pallas_call(fused_kernel, out_shape=tuple((pltpu.VMEM(one.shape, one.d...  87.9 us
    pallas_call x1, Pallas kernels, fused(): pl.pallas_call(finish_kernel, out_shape=shapes[:7] + (shape((4, CHUNK), F...  1.94 us

profile of v5, /device:TPU:0, one launch (start us, length us, event | category | flops | bytes accessed | tf_op | source)
XLA Modules:
  0.0 90.6 jit_solution(6815431378712877880)
XLA Ops:
  0.6 87.9 %shard_map.187 = (bf16[128,768]{1,0:T(8,128)(2,1)S(1)}, bf16[128,768]{1,0:T(8,128)(2,1)S(1)}, bf16[512,768]{1,0:T(8,128)(2,1)S(1)}, f32[24,2304]{1,0:T(8,128)S(1...) custom-call(bf16[128,768]{1,0:T(8,128)(2,1)} %refs_0_.1, ...), custom_call_target="tpu_custom_call" | custom-call | flops 12000000000 | bytes 4000000 | tf_op jit(solution)/shard_map/pallas_call | solution.py:1661
  88.5 1.9 %shard_map.188 = (bf16[128,768]{1,0:T(8,128)(2,1)}, bf16[128,768]{1,0:T(8,128)(2,1)}, bf16[512,768]{1,0:T(8,128)(2,1)}, f32[24,2304]{1,0:T(8,128)}, f32[24,768]{...) custom-call(bf16[128,768]{1,0:T(8,128)(2,1)S(1)} %get-tuple-element.27.refs_0_, ...), custom_call_target="tpu_custom_call" | custom-call | tf_op jit(solution)/shard_map/pallas_call | solution.py:1686

commit v6 on v5

--- a/solution.py
+++ b/solution.py
@@ -334,6 +334,39 @@
     return [jnp.concatenate([tiles[i], low[i]], axis=0) for i in range(count)]
 
 
+def fold_qkv(tiles):
+    t0, t1, t2, t3, t4 = tiles
+    lane, lane8, lane16 = (lane_id((n, 128)) for n in (CHUNK, 8, 16))
+    turned = pltpu.roll(t3, 96, 1)
+    keys = jnp.where(lane < 96, t2, turned)
+    extra = jnp.where(
+        lane8 < 80,
+        pltpu.roll(t2[:8], 96, 1),
+        jnp.where(lane8 < 96, pltpu.roll(t2[8:16], 112, 1), t2[16:]),
+    )
+    right = jnp.concatenate([pltpu.roll(turned[16:], 64, 1), extra], axis=0)
+    shared = jnp.where(lane16 < 64, turned[:16], right)
+    return [t0[:16], t1[:16], t4[:16], keys[:16], shared] + [
+        jnp.concatenate([a[16:], b[16:]], axis=0) for a, b in ((t0, t1), (t4, keys))
+    ]
+
+
+def unfold_qkv(tiles):
+    u0, u1, u4, u3, shared, low01, low43 = tiles
+    lane = lane_id((CHUNK, 128))
+    t0 = jnp.concatenate([u0, low01[:8]], axis=0)
+    t1 = jnp.concatenate([u1, low01[8:]], axis=0)
+    t4 = jnp.concatenate([u4, low43[:8]], axis=0)
+    keys = jnp.concatenate([u3, low43[8:]], axis=0)
+    turned = jnp.concatenate([shared, pltpu.roll(shared[:8], 64, 1)], axis=0)
+    t3 = jnp.where(lane < 32, pltpu.roll(keys, 32, 1), pltpu.roll(turned, 32, 1))
+    t3 = jnp.where(lane < 96, t3, 0.0)
+    extra = shared[8:]
+    extra = jnp.concatenate([pltpu.roll(extra, 32, 1), pltpu.roll(extra, 16, 1), extra], axis=0)
+    t2 = jnp.where(lane < 96, keys, jnp.where(lane < 112, extra, 0.0))
+    return [t0, t1, t2, t3, t4]
+
+
 def qkv_chunk(block, head, half):
     return 24 * block + 2 * head + half
 
@@ -404,8 +437,8 @@
     sine=((SEQ, 128), F32),
     x_all=((GROUP, OWN, WIDTH), BF),
     c_all=((GROUP, OWN, WIDTH), BF),
-    qp_s=((GROUP, 16, 1024), BF),
-    q_all=((ROWS * GROUP, 16, 1024), BF),
+    qp_s=((GROUP, 16, 896), BF),
+    q_all=((ROWS * GROUP, 16, 896), BF),
     up_s=((GROUP, 16, 1152), BF),
     up_l=((GROUP, 16, 1152), BF),
     tmp=((BLOCK, WIDTH), F32),
@@ -422,7 +455,6 @@
     kk=((SEQ, 256), BF),
     v01=((SEQ, 128), BF),
     v_all=((SEQ, 384), BF),
-    k_heads=((3, SEQ, 256), BF),
     probs=((3, SEQ, SEQ), F32),
     o_l=((GROUP, 2, 384, 128), BF),
     ob=((SEQ, WIDTH), BF),
@@ -452,9 +484,9 @@
     u0=((8, 128), F32),
     u1=((8, 128), F32),
     uzd=((8, 8, 128), F32),
-    fin=((16, 16, 1024), BF),
-    ps=((16, 16, 1024), BF),
-    q_sum=((GROUP, 16, 1024), F32),
+    fin=((16, 16, 896), BF),
+    ps=((16, 16, 896), BF),
+    q_sum=((GROUP, 16, 896), F32),
     a_up=((GROUP, 16, 1152), BF),
     f_down=((BLOCK, WIDTH), F32),
     f_up=((BLOCK, WIDTH), F32),
@@ -808,7 +840,7 @@
             for j in range(2):
                 to = 2 * self.half + j
                 at = 8 * self.half + 2 * slot + j
-                for t, tile in enumerate(fold(tiles_of(value[CHUNK * j : CHUNK * (j + 1)]))):
+                for t, tile in enumerate(fold_qkv(tiles_of(value[CHUNK * j : CHUNK * (j + 1)]))):
                     s.ps[at, :, 128 * t : 128 * (t + 1)] = tile.astype(BF)
                 copy_to(
                     s.ps.at[at],
@@ -981,7 +1013,7 @@
         for k in range(GROUP):
             landed = landing[k][...] if isinstance(landing, list) else landing[k]
             tiles = [t.astype(F32) for t in tiles_of(landed)]
-            for t, tile in enumerate(unfold(tiles, count)):
+            for t, tile in enumerate(unfold_qkv(tiles) if count == 5 else unfold(tiles, count)):
                 s.tmp[CHUNK * k : CHUNK * (k + 1), 128 * t : 128 * (t + 1)] = tile
         rows_at(target, row, BLOCK)[...] = s.tmp[:, : 128 * count].astype(BF)
 
@@ -1005,7 +1037,7 @@
     for k in range(GROUP):
         tiles = permute_chunks(wq_tiles, qkv_picks(k))
         tiles[2] = tiles[2] + extra
-        for t, tile in enumerate(fold(tiles)):
+        for t, tile in enumerate(fold_qkv(tiles)):
             s.qp_s[k, :, 128 * t : 128 * (t + 1)] = tile.astype(BF)
     s.q_all[GROUP * r + d] = s.qp_s[d]
     loads["wo"].wait()
@@ -1187,7 +1219,6 @@
     attend(0)
     for h in range(3):
         s.probs[h, :QBLOCK, QBLOCK:] = jnp.zeros((QBLOCK, QBLOCK), F32)
-        s.k_heads[h] = s.kk[...] * head_mask[h]
     s.v_all[:, :256] = s.qv[...]
     s.v_all[:, 256:] = s.v01[...]
     up_gather.forward_cross()
@@ -1308,24 +1339,24 @@
 
     mid_sum = GroupSum("mid", s.part, 4)
 
-    def quarter(ref, i):
+    def quarter(ref, i, size=32):
         return jnp.concatenate(
-            [ref[OWN * j + 32 * i : OWN * j + 32 * (i + 1), :] for j in range(GROUP)], axis=0
+            [ref[OWN * j + 32 * i : OWN * j + 32 * i + size, :] for j in range(GROUP)], axis=0
         )
 
-    def put_quarter(ref, i, value):
+    def put_quarter(ref, i, value, size=32):
         for j in range(GROUP):
-            ref[OWN * j + 32 * i : OWN * j + 32 * (i + 1), :] = value[32 * j : 32 * (j + 1)]
-
-    for i in range(4):
-        value = dot(quarter(s.dm, i), s.w_down[...], 1, 1)
-        value = (value * quarter(s.slope, i)).astype(BF)
-        put_quarter(s.du, i, value)
-        put_quarter(s.part, i, dot(value, s.w_up[...], 1, 1))
+            ref[OWN * j + 32 * i : OWN * j + 32 * i + size, :] = value[size * j : size * (j + 1)]
+
+    for i in (0, 2):
+        value = dot(quarter(s.dm, i, 64), s.w_down[...], 1, 1)
+        value = (value * quarter(s.slope, i, 64)).astype(BF)
+        put_quarter(s.du, i, value, 64)
+        put_quarter(s.part, i, dot(value, s.w_up[...], 1, 1), 64)
         mid_sum.send(i)
-        if i >= 1:
-            mid_sum.middle(i - 1)
-
+        mid_sum.send(i + 1)
+    for i in range(3):
+        mid_sum.middle(i)
     down_sum.send_mirror()
     mid_sum.middle(3)
     down_sum.send_own()
@@ -1405,6 +1436,7 @@
 
     lane = lane_id((1, 384))
     head_lanes = [jnp.where(lax.div(lane, jnp.int32(64)) == 4 + h, 1.0, 0.0) for h in range(2)]
+    head_scale = [jnp.where(lane2 == h, root, 0.0) for h in range(3)]
     head_lanes = [m.astype(BF) for m in head_lanes + [jnp.where(lane < 256, 1.0, 0.0)]]
     for i in range(4):
         dy_gathers[i].finish()
@@ -1425,15 +1457,16 @@
         else:
             s.dk[...] += dk
             s.dv[...] += dv
-        dq = sum(dot(ds[OWN * h : OWN * (h + 1)], s.k_heads[h]) for h in range(3))
-        put_quarter(s.dq, i, dq * root)
+        dq = dot(ds, s.kk[...])
+        dq = sum(dq[OWN * h : OWN * (h + 1)] * head_scale[h] for h in range(3))
+        put_quarter(s.dq, i, dq)
         if i < 2:
             dy_gathers[i + 2].relay()
         if i == 1:
             up_sum.send_mirror()
+            up_sum.send_own()
             mix_sum.middle()
         if i == 2:
-            up_sum.send_own()
             up_sum.send_near()
 
     def turn_back(at):
@@ -1599,7 +1632,7 @@
 
     tiles = []
     for k in range(GROUP):
-        tiles += unfold(tiles_of(s.q_sum[k]), 5)
+        tiles += unfold_qkv(tiles_of(s.q_sum[k]))
     for t, tile in enumerate(permute_chunks(tiles, QKV_BACK)):
         gq_o[:, 128 * t : 128 * (t + 1)] = tile
     collect(up_spread, s.a_up, 6, UP_BACK, gu_o)

time: 90.8 us -> 89.2 us (0.982)
  Pallas kernels: 89.8 us -> 88.2 us
    pallas_call x1, Pallas kernels: 87.9 us -> 86.2 us  [fused(): pl.pallas_call(fused_kernel, out_shape=tuple((pltpu.VMEM(one.shape, one.d...]
where the time goes in v6:
time: 89.2 us; the launch traced here: 89 us
  Pallas kernels  88.2 us (99%)
    pallas_call x1, Pallas kernels, fused(): pl.pallas_call(fused_kernel, out_shape=tuple((pltpu.VMEM(one.shape, one.d...  86.2 us
    pallas_call x1, Pallas kernels, fused(): pl.pallas_call(finish_kernel, out_shape=shapes[:7] + (shape((4, CHUNK), F...  1.94 us

profile of v6, /device:TPU:0, one launch (start us, length us, event | category | flops | bytes accessed | tf_op | source)
XLA Modules:
  0.0 89.0 jit_solution(16607208173769353833)
XLA Ops:
  0.6 86.2 %shard_map.187 = (bf16[128,768]{1,0:T(8,128)(2,1)S(1)}, bf16[128,768]{1,0:T(8,128)(2,1)S(1)}, bf16[512,768]{1,0:T(8,128)(2,1)S(1)}, f32[24,2304]{1,0:T(8,128)S(1...) custom-call(bf16[128,768]{1,0:T(8,128)(2,1)} %refs_0_.1, ...), custom_call_target="tpu_custom_call" | custom-call | flops 12000000000 | bytes 4000000 | tf_op jit(solution)/shard_map/pallas_call | solution.py:1694
  86.9 1.9 %shard_map.188 = (bf16[128,768]{1,0:T(8,128)(2,1)}, bf16[128,768]{1,0:T(8,128)(2,1)}, bf16[512,768]{1,0:T(8,128)(2,1)}, f32[24,2304]{1,0:T(8,128)}, f32[24,768]{...) custom-call(bf16[128,768]{1,0:T(8,128)(2,1)S(1)} %get-tuple-element.27.refs_0_, ...), custom_call_target="tpu_custom_call" | custom-call | tf_op jit(solution)/shard_map/pallas_call | solution.py:1719

commit v7 on v6

--- a/solution.py
+++ b/solution.py
@@ -447,14 +447,14 @@
     w_down=((WIDTH, WIDTH), BF),
     wo_l=((GROUP, 2, ROWS // 2, 16, 1152), BF),
     w_out=((WIDTH, WIDTH), BF),
-    w_own=((384, WIDTH), BF),
+    w_own=((256, WIDTH), BF),
     norms=((8, WIDTH), F32),
     normal=((SEQ, WIDTH), F32),
     h1=((SEQ, WIDTH), BF),
     qv=((SEQ, 256), BF),
     kk=((SEQ, 256), BF),
     v01=((SEQ, 128), BF),
-    v_all=((SEQ, 384), BF),
+    v_all=((SEQ, 256), BF),
     probs=((3, SEQ, SEQ), F32),
     o_l=((GROUP, 2, 384, 128), BF),
     ob=((SEQ, WIDTH), BF),
@@ -474,7 +474,7 @@
     dyb=((GROUP, OWN, WIDTH), BF),
     dq=((SEQ, 256), F32),
     dk=((SEQ, 256), F32),
-    dv=((SEQ, 384), F32),
+    dv=((SEQ, 256), F32),
     dqkv=((SEQ, PACK), BF),
     terms=((8, WIDTH), F32),
     terms2=((8, WIDTH), F32),
@@ -513,8 +513,8 @@
     SCRATCH["gs_" + _name] = ((3, OWN, WIDTH), BF)
     SCRATCH["l1_" + _name] = ((2, OWN, WIDTH), BF)
     SCRATCH["l2_" + _name] = ((OWN, WIDTH), BF)
-N_SENDS = 36
-N_ARRIVALS = 116
+N_SENDS = 32
+N_ARRIVALS = 110
 N_IN = 12
 N_OUT = 9
 VMEM_MIB = 60
@@ -1040,39 +1040,11 @@
         for t, tile in enumerate(fold_qkv(tiles)):
             s.qp_s[k, :, 128 * t : 128 * (t + 1)] = tile.astype(BF)
     s.q_all[GROUP * r + d] = s.qp_s[d]
-    loads["wo"].wait()
-    for t, tile in enumerate(fold(tiles_of(wo[...].astype(F32)))):
-        s.wo_l[d, x, z, :, 128 * t : 128 * (t + 1)] = tile.astype(BF)
-    loads["wu"].wait()
-    wu_tiles = tiles_of(wu[...].astype(F32))
-    for k in range(GROUP):
-        for t, tile in enumerate(fold(permute_chunks(wu_tiles, up_picks(k)))):
-            s.up_s[k, :, 128 * t : 128 * (t + 1)] = tile.astype(BF)
-    s.up_l[d] = s.up_s[d]
-    diagonal = jnp.where(
-        row_id((OWN, OWN)) == lane_id((OWN, OWN)), jnp.broadcast_to(mask_row, (OWN, OWN)), 0.0
-    )
-    loads["cot"].wait()
-    s.c_all[d] = dot(diagonal.astype(BF), cot[...]).astype(BF)
-    loads["x"].wait()
-    loads["wd"].wait()
     pl.semaphore_wait(barrier, len(partners))
 
     qkv_gather = PieceGather()
     qkv_gather.send()
-    out_gather = Gather(
-        lambda zk, xk: s.wo_l.at[d, xk, zk],
-        lambda n: s.wo_l.at[0, 0, pl.ds(0, n)] if n <= 4 else s.wo_l.at[0, :, pl.ds(0, n // 2)],
-    )
-    out_gather.send_two()
-    out_gather.send_mirror()
-    out_gather.send_near()
-    out_gather.send_own_x()
-    up_arrival, up_group = arrivals(), sends(s.up_s.at[pl.ds(0, 3)])
-    for m, device in mates:
-        copy_to(s.up_s.at[m], s.up_l.at[d], device, up_arrival, up_group)
-    x_gather = GroupGather(lambda i: s.x_all.at[i], lambda n: s.x_all.at[pl.ds(0, n)])
-    x_gather.send()
+    loads["wd"].wait()
     up_gather = Gather(
         lambda zk, xk: rows_at(s.w_up, 2 * zk + xk, BLOCK),
         lambda n: s.w_up.at[pl.ds(0, n * BLOCK)],
@@ -1086,6 +1058,36 @@
         )
         for h in range(2)
     ]
+    loads["wo"].wait()
+    for t, tile in enumerate(fold(tiles_of(wo[...].astype(F32)))):
+        s.wo_l[d, x, z, :, 128 * t : 128 * (t + 1)] = tile.astype(BF)
+    out_gather = Gather(
+        lambda zk, xk: s.wo_l.at[d, xk, zk],
+        lambda n: s.wo_l.at[0, 0, pl.ds(0, n)] if n <= 4 else s.wo_l.at[0, :, pl.ds(0, n // 2)],
+    )
+    out_gather.send_two()
+    out_gather.send_mirror()
+    out_gather.send_near()
+    out_gather.send_own_x()
+    for half in downs:
+        half.send_own_x()
+    loads["wu"].wait()
+    wu_tiles = tiles_of(wu[...].astype(F32))
+    for k in range(GROUP):
+        for t, tile in enumerate(fold(permute_chunks(wu_tiles, up_picks(k)))):
+            s.up_s[k, :, 128 * t : 128 * (t + 1)] = tile.astype(BF)
+    s.up_l[d] = s.up_s[d]
+    up_arrival, up_group = arrivals(), sends(s.up_s.at[pl.ds(0, 3)])
+    for m, device in mates:
+        copy_to(s.up_s.at[m], s.up_l.at[d], device, up_arrival, up_group)
+    loads["x"].wait()
+    x_gather = GroupGather(lambda i: s.x_all.at[i], lambda n: s.x_all.at[pl.ds(0, n)])
+    x_gather.send()
+    diagonal = jnp.where(
+        row_id((OWN, OWN)) == lane_id((OWN, OWN)), jnp.broadcast_to(mask_row, (OWN, OWN)), 0.0
+    )
+    loads["cot"].wait()
+    s.c_all[d] = dot(diagonal.astype(BF), cot[...]).astype(BF)
     c_gather = GroupGather(lambda i: s.c_all.at[i], lambda n: s.c_all.at[pl.ds(0, n)])
     c_gather.send()
 
@@ -1096,8 +1098,6 @@
 
         by_rows(OWN, 64, one)
 
-    for half in downs:
-        half.send_own_x()
     qkv_gather.forward_own(0)
     qkv_gather.forward_own(1)
     qkv_gather.forward_near(0)
@@ -1119,7 +1119,8 @@
     up_gather.send_mirror()
     for half in downs:
         half.send_two()
-        half.send_near()
+    downs[1].send_near()
+    downs[0].send_near(True)
     out_gather.send_x(z_two)
     out_gather.forward_near()
     out_gather.forward_mirror()
@@ -1199,6 +1200,7 @@
                 third = dot(probs.astype(BF), s.qv[:keys, :])
             if b == 1 and h == 0:
                 up_gather.forward_two()
+                downs[0].send_near(False)
                 for half in downs:
                     half.send_mirror()
             if b == 1 and h == 1:
@@ -1219,8 +1221,16 @@
     attend(0)
     for h in range(3):
         s.probs[h, :QBLOCK, QBLOCK:] = jnp.zeros((QBLOCK, QBLOCK), F32)
-    s.v_all[:, :256] = s.qv[...]
-    s.v_all[:, 256:] = s.v01[...]
+    s.v_all[:, :128] = s.v01[...]
+
+    def third_values(at):
+        lane = lane_id((64, 128))
+        low = pltpu.roll(s.qv[at, :128].astype(F32), 32, 1)
+        high = pltpu.roll(s.qv[at, 128:].astype(F32), 64, 1)
+        both = jnp.where(lane < 32, low, jnp.where(lane < 64, high, 0.0))
+        s.v_all[at, 128:] = both.astype(BF)
+
+    by_rows(SEQ, 64, third_values)
     up_gather.forward_cross()
     columns[1].relay()
     downs[1].forward_near()
@@ -1241,13 +1251,10 @@
     for head in range(HEADS):
         at = out_place(head)
         s.w_out[at : at + 64, :] = s.g_out[64 * head : 64 * head + 64, :].astype(BF)
-    s.w_own[...] = jnp.zeros((384, WIDTH), BF)
-    third_rows = rows_at(s.w_out.at[pl.ds(512, 256)], d, 64)
-    s.w_own[96:128, :] = third_rows[:32, :]
-    s.w_own[224:256, :] = third_rows[32:, :]
-    s.w_own[256:, :] = rows_at(s.w_out.at[pl.ds(0, 512)], d, 128)[...]
+    s.w_own[:128, :] = rows_at(s.w_out.at[pl.ds(0, 512)], d, 128)[...]
+    s.w_own[128:192, :] = rows_at(s.w_out.at[pl.ds(512, 256)], d, 64)[...]
+    s.w_own[192:, :] = jnp.zeros((64, WIDTH), BF)
     downs[0].forward_two()
-    downs[0].forward_cross()
     o_gathers[1].relay()
     c_gather.finish()
 
@@ -1265,6 +1272,7 @@
         by_rows(OWN, 32, loss_rows)
 
     downs[1].forward_two()
+    downs[0].forward_cross()
     for b in (1, 0):
         if b == 0:
             o_gathers[0].relay()
@@ -1434,10 +1442,9 @@
     copy_to(s.u0, s.u1, x_dev, depth_x, depth_group)
     down_sum.send_two_inside()
 
-    lane = lane_id((1, 384))
-    head_lanes = [jnp.where(lax.div(lane, jnp.int32(64)) == 4 + h, 1.0, 0.0) for h in range(2)]
     head_scale = [jnp.where(lane2 == h, root, 0.0) for h in range(3)]
-    head_lanes = [m.astype(BF) for m in head_lanes + [jnp.where(lane < 256, 1.0, 0.0)]]
+    lane = lax.div(lane_id((1, 256)), jnp.int32(64))
+    head_lanes = [jnp.where(lane == h, 1.0, 0.0).astype(BF) for h in range(3)]
     for i in range(4):
         dy_gathers[i].finish()
         rows = s.dyb[:, 32 * i : 32 * (i + 1), :].reshape(OWN, WIDTH)
@@ -1466,19 +1473,20 @@
             up_sum.send_mirror()
             up_sum.send_own()
             mix_sum.middle()
-        if i == 2:
-            up_sum.send_near()
 
     def turn_back(at):
         co, si = cosine[at, :], sine[at, :]
+        lane = lane_id((64, 128))
         for left, source in ((0, s.dq), (256, s.dk)):
             a, b = source[at, :128], source[at, 128:]
             first, second = a * co + b * si, b * co - a * si
             if left == 0:
-                first, second = first + s.dv[at, :128], second + s.dv[at, 128:256]
+                third = s.dv[at, 128:]
+                first = jnp.where(lane < 96, first, pltpu.roll(third, 96, 1))
+                second = jnp.where(lane < 96, second, pltpu.roll(third, 64, 1))
             s.dqkv[at, left : left + 128] = first.astype(BF)
             s.dqkv[at, left + 128 : left + 256] = second.astype(BF)
-        s.dqkv[at, 512:] = s.dv[at, 256:].astype(BF)
+        s.dqkv[at, 512:] = s.dv[at, :128].astype(BF)
 
     by_rows(SEQ, 64, turn_back)
     up_sum.send_two_outside()
@@ -1539,6 +1547,7 @@
 
     for one in sums:
         one.send_mirror()
+    up_sum.send_near()
     arrive(s.td.at[pl.ds(0, 3)], norm_arrival)
     value = (s.td[0] + s.td[1]) + (s.td[2] + s.td[3])
     value = pltpu.roll(value, lax.rem(WIDTH - CHUNK * d, WIDTH), 1)
@@ -1618,6 +1627,8 @@
     arrive(s.uzd.at[pl.ds(0, 3)], depth_d)
     dg_o[...] = (s.uzd[4] + s.uzd[5]) + (s.uzd[6] + s.uzd[7])
 
+    collect(up_spread, s.a_up, 6, UP_BACK, gu_o)
+
     arrive(s.fin.at[pl.ds(0, 11)], shared[3])
     for k in range(GROUP):
         s.q_sum[k] = (
@@ -1635,7 +1646,6 @@
         tiles += unfold_qkv(tiles_of(s.q_sum[k]))
     for t, tile in enumerate(permute_chunks(tiles, QKV_BACK)):
         gq_o[:, 128 * t : 128 * (t + 1)] = tile
-    collect(up_spread, s.a_up, 6, UP_BACK, gu_o)
     out_sum.finish()
     for t, tile in enumerate(unfold(tiles_of(s.f_out[:, :1152]), 6)):
         go_o[:, 128 * t : 128 * (t + 1)] = tile

time: 89.2 us -> 88.8 us (level)
  no operation moved by 1% of the time
where the time goes in v7:
time: 88.8 us; the launch traced here: 88.6 us
  Pallas kernels  87.8 us (99%)
    pallas_call x1, Pallas kernels, fused(): pl.pallas_call(fused_kernel, out_shape=tuple((pltpu.VMEM(one.shape, one.d...  85.9 us
    pallas_call x1, Pallas kernels, fused(): pl.pallas_call(finish_kernel, out_shape=shapes[:7] + (shape((4, CHUNK), F...  1.94 us

profile of v7, /device:TPU:0, one launch (start us, length us, event | category | flops | bytes accessed | tf_op | source)
XLA Modules:
  0.0 88.6 jit_solution(15174106551851783313)
XLA Ops:
  0.6 85.9 %shard_map.187 = (bf16[128,768]{1,0:T(8,128)(2,1)S(1)}, bf16[128,768]{1,0:T(8,128)(2,1)S(1)}, bf16[512,768]{1,0:T(8,128)(2,1)S(1)}, f32[24,2304]{1,0:T(8,128)S(1...) custom-call(bf16[128,768]{1,0:T(8,128)(2,1)} %refs_0_.1, ...), custom_call_target="tpu_custom_call" | custom-call | flops 12000000000 | bytes 4000000 | tf_op jit(solution)/shard_map/pallas_call | solution.py:1704
  86.5 1.9 %shard_map.188 = (bf16[128,768]{1,0:T(8,128)(2,1)}, bf16[128,768]{1,0:T(8,128)(2,1)}, bf16[512,768]{1,0:T(8,128)(2,1)}, f32[24,2304]{1,0:T(8,128)}, f32[24,768]{...) custom-call(bf16[128,768]{1,0:T(8,128)(2,1)S(1)} %get-tuple-element.27.refs_0_, ...), custom_call_target="tpu_custom_call" | custom-call | tf_op jit(solution)/shard_map/pallas_call | solution.py:1729

commit v8 on v7

--- a/solution.py
+++ b/solution.py
@@ -505,10 +505,10 @@
     SCRATCH["zl_" + _name] = ((3, _rows, _cols), BF)
     SCRATCH["nl_" + _name] = ((2, _rows, _cols), BF)
 for _h in range(2):
-    SCRATCH[f"st_qkv{_h}"] = ((6, BLOCK // 2, PACK), BF)
-    SCRATCH[f"xl_qkv{_h}"] = ((4, BLOCK // 2, PACK), BF)
+    SCRATCH[f"st_qkv{_h}"] = ((6, 2, 16, 896), BF)
+    SCRATCH[f"xl_qkv{_h}"] = ((4, 2, 16, 896), BF)
     for _name in ("cl", "zl"):
-        SCRATCH[f"{_name}_qkv{_h}"] = ((BLOCK // 2, PACK), BF)
+        SCRATCH[f"{_name}_qkv{_h}"] = ((2, 16, 896), BF)
 for _name in ("mix", "mid", "in"):
     SCRATCH["gs_" + _name] = ((3, OWN, WIDTH), BF)
     SCRATCH["l1_" + _name] = ((2, OWN, WIDTH), BF)
@@ -809,12 +809,18 @@
             rows = BLOCK // 2
             start_row = pl.multiple_of((2 * index + self.half) * rows, rows)
             value = s.g_qkv[pl.ds(start_row, rows), :]
+            pieces = [fold_qkv(tiles_of(value[CHUNK * j : CHUNK * (j + 1)])) for j in range(2)]
+            pieces = [jnp.concatenate(tiles, axis=1) for tiles in pieces]
             for extra in extras:
-                value = value + extra.astype(F32)
-            return value
+                pieces = [piece + extra[j].astype(F32) for j, piece in enumerate(pieces)]
+            return pieces
+
+        def put(self, target, pieces):
+            for j, piece in enumerate(pieces):
+                target[j] = piece.astype(BF)
 
         def send_x(self, name, zk, *extras):
-            self.xs[zk] = self.value(2 * zk + other_x, *extras).astype(BF)
+            self.put(self.xs.at[zk], self.value(2 * zk + other_x, *extras))
             copy_to(self.xs.at[zk], self.xl.at[zk], x_dev, self.along_x[name], self.group)
 
         def arrive_x(self, name, zk):
@@ -823,7 +829,7 @@
         def send_crossing(self):
             @pl.when(inside)
             def _():
-                self.cs[...] = self.value(2 * z_near + other_x).astype(BF)
+                self.put(self.cs, self.value(2 * z_near + other_x))
                 copy_to(self.cs, self.cl, near_dev, self.crossing, self.group)
 
         def send_third(self):
@@ -840,8 +846,7 @@
             for j in range(2):
                 to = 2 * self.half + j
                 at = 8 * self.half + 2 * slot + j
-                for t, tile in enumerate(fold_qkv(tiles_of(value[CHUNK * j : CHUNK * (j + 1)]))):
-                    s.ps[at, :, 128 * t : 128 * (t + 1)] = tile.astype(BF)
+                s.ps[at] = value[j].astype(BF)
                 copy_to(
                     s.ps.at[at],
                     s.fin.at[GROUP * slot + d],
@@ -860,7 +865,7 @@
             self.arrive_x("mirror", z_mirror)
             value = self.value(2 * z_mirror + x, self.xl[z_mirror])
             self.deliver(2, z_mirror, value)
-            self.zs[...] = value.astype(BF)
+            self.put(self.zs, value)
             copy_to(self.zs, self.zl, near_dev, self.passing, self.outer, outside)
 
         def send_two(self):
@@ -868,7 +873,7 @@
 
             @pl.when(outside)
             def _():
-                self.zl[...] = jnp.zeros((BLOCK // 2, PACK), BF)
+                self.zl[...] = jnp.zeros((2, 16, 896), BF)
 
             pl.when(inside)(lambda: arrive(self.zl, self.passing))
             self.deliver(0, z_two, self.value(2 * z_two + x, self.xl[z_two], self.zl[...]))
@@ -1613,14 +1618,14 @@
     by_rows(OWN, 32, first_norm_back)
     for one in sums:
         one.send_near()
-    up_sum.finish()
-    up_spread = spread(s.f_up, s.b_up, s.a_up)
     arrive(s.uzd.at[pl.ds(0, 3)], depth_z)
     s.uzd[4 + d] = (s.uzd[0] + s.uzd[1]) + (s.uzd[2] + s.uzd[3])
     for m, device in mates:
         copy_to(s.uzd.at[4 + d], s.uzd.at[4 + d], device, depth_d, depth_group)
     for one in sums:
         one.keep_own()
+    up_sum.finish()
+    up_spread = spread(s.f_up, s.b_up, s.a_up)
     out_sum.send_two_outside()
     out_sum.send_two_inside()
     out_sum.send_near()

time: 88.8 us -> 89.1 us (level)
  no operation moved by 1% of the time
where the time goes in v8:
time: 89.1 us; the launch traced here: 88.9 us
  Pallas kernels  88.1 us (99%)
    pallas_call x1, Pallas kernels, fused(): pl.pallas_call(fused_kernel, out_shape=tuple((pltpu.VMEM(one.shape, one.d...  86.2 us
    pallas_call x1, Pallas kernels, fused(): pl.pallas_call(finish_kernel, out_shape=shapes[:7] + (shape((4, CHUNK), F...  1.94 us

profile of v8, /device:TPU:0, one launch (start us, length us, event | category | flops | bytes accessed | tf_op | source)
XLA Modules:
  0.0 88.9 jit_solution(4168140422201475539)
XLA Ops:
  0.6 86.2 %shard_map.187 = (bf16[128,768]{1,0:T(8,128)(2,1)S(1)}, bf16[128,768]{1,0:T(8,128)(2,1)S(1)}, bf16[512,768]{1,0:T(8,128)(2,1)S(1)}, f32[24,2304]{1,0:T(8,128)S(1...) custom-call(bf16[128,768]{1,0:T(8,128)(2,1)} %refs_0_.1, ...), custom_call_target="tpu_custom_call" | custom-call | flops 12000000000 | bytes 4000000 | tf_op jit(solution)/shard_map/pallas_call | solution.py:1709
  86.8 1.9 %shard_map.188 = (bf16[128,768]{1,0:T(8,128)(2,1)}, bf16[128,768]{1,0:T(8,128)(2,1)}, bf16[512,768]{1,0:T(8,128)(2,1)}, f32[24,2304]{1,0:T(8,128)}, f32[24,768]{...) custom-call(bf16[128,768]{1,0:T(8,128)(2,1)S(1)} %get-tuple-element.27.refs_0_, ...), custom_call_target="tpu_custom_call" | custom-call | tf_op jit(solution)/shard_map/pallas_call | solution.py:1734
